TPU v7x, 128 devices: a whole 4x4x4 slice. The times are simulated.
128 devices in a mesh: seq: 32 (over z, y, x_lo), tp: 4 (over x_hi, core).
Axes of the slice: x: 4 (x_hi: 2, x_lo: 2; x = x_hi * 2 + x_lo), y: 4, z: 4, core: 2. Of those that a mesh axis runs over, the one named last changes fastest.
Arguments:
- img: bfloat16 [4096, 2432], P('seq', 'tp'), may hold values from -0.119628906 to 0.119628906
- txt: bfloat16 [512, 2432], P('seq', 'tp'), may hold values from -0.119628906 to 0.119628906
- ctl: bfloat16 [4096, 2432], P('seq', 'tp'), may hold values from -6 to 6
- dy_img: bfloat16 [4096, 2432], P('seq', 'tp'), may hold values from -6 to 6
- text_output_cotangent: bfloat16 [512, 2432], P('seq', 'tp'), may hold values from -6 to 6
- live_text_length: int32 [1], replicated, may hold values from 128 to 512
- modulation: float32 [3, 3, 2432], replicated, may hold values from -3 to 3
- query_key_gains: float32 [3, 2, 64], replicated, may hold values from 0.1 to 1.9
- w_qkv_img: bfloat16 [2432, 3, 1536], P(None, None, 'tp'), may hold values from -0.125 to 0.125
- image_output_weight: bfloat16 [1536, 2432], P('tp'), may hold values from -0.15625 to 0.15625
- w_qkv_txt: bfloat16 [2432, 3, 1536], P(None, None, 'tp'), may hold values from -0.125 to 0.125
- text_output_weight: bfloat16 [1536, 2432], P('tp'), may hold values from -0.15625 to 0.15625
- w_qkv_ctl: bfloat16 [2432, 3, 1536], P(None, None, 'tp'), may hold values from -0.125 to 0.125
- w_out_ctl: bfloat16 [1536, 2432], P('tp'), may hold values from -0.15625 to 0.15625
Outputs:
- y_img: bfloat16 [4096, 2432], P('seq', 'tp')
- y_txt: bfloat16 [512, 2432], P('seq', 'tp')
- d_img: bfloat16 [4096, 2432], P('seq', 'tp')
- text_input_gradient: bfloat16 [512, 2432], P('seq', 'tp')
- control_input_gradient: bfloat16 [4096, 2432], P('seq', 'tp')
- grad_qkv_ctl: float32 [2432, 3, 1536], P('seq', None, 'tp')
- grad_out_ctl: float32 [1536, 2432], P('tp', 'seq')
Inputs may be any that keep to these rules, and one draw needn't show every extreme that they name: `live_text_length`: the number of live text tokens of the sample; text slots from this number on are padding and never attended to.
All inputs are finite; a program needn't handle non-finite values.
Results may differ from a plain program's by a relative error of at most 0.033.
Values may be sent and summed in bfloat16 or wider, within the bound.
No kernel may reach another device: no remote copies, remote signals or barrier semaphores. Data moves between devices by JAX's collectives and lax.ppermute only.
A program may use at most 256 MiB of HBM per device.

v0:
```python
import jax
import jax.numpy as jnp
from jax import lax
from jax.sharding import PartitionSpec as P

HEAD_SIZE = 64


EPS = 1e-06
CONTRACT_ROWS = (((0,), (0,)), ((), ()))
CONTRACT_COLS = (((1,), (1,)), ((), ()))


def rounded(value_rows):
    return lax.optimization_barrier(value_rows.astype(jnp.bfloat16)).astype(jnp.float32)


def norm_rows(rows_in, modulation_params):
    values = rows_in.astype(jnp.float32)
    centered_input = values - jnp.mean(values, axis=-1, keepdims=True)
    inverse_deviation = lax.rsqrt(
        jnp.mean(centered_input * centered_input, axis=-1, keepdims=True) + EPS
    )
    standardized_input = centered_input * inverse_deviation
    normalized_input = (
        standardized_input * (1.0 + modulation_params[1]) + modulation_params[0]
    ).astype(jnp.bfloat16)
    return (normalized_input, standardized_input, inverse_deviation)


def head_norm(values, gain):
    return values * lax.rsqrt(jnp.mean(values * values, axis=-1, keepdims=True) + EPS) * gain


def project(normalized_input, w_qkv, gains):
    row_count = normalized_input.shape[0]
    heads_on_shard = w_qkv.shape[2] // HEAD_SIZE
    proj = jnp.dot(
        normalized_input, w_qkv.reshape(w_qkv.shape[0], -1), preferred_element_type=jnp.float32
    )
    proj = proj.reshape(row_count, 3, heads_on_shard, HEAD_SIZE)
    query = head_norm(proj[:, 0], gains[0]).astype(jnp.bfloat16)
    key_portion = head_norm(proj[:, 1], gains[1]).astype(jnp.bfloat16)
    value_rows = proj[:, 2].astype(jnp.bfloat16)
    return (proj, query, key_portion, value_rows)


def projection_gradient(proj, gains, dquery, dkey, dvalue):
    ignored, back_query = jax.vjp(lambda values: head_norm(values, gains[0]), proj[:, 0])
    ignored, back_key = jax.vjp(lambda values: head_norm(values, gains[1]), proj[:, 1])
    stacked = jnp.stack([back_query(dquery)[0], back_key(dkey)[0], dvalue], 1)
    return stacked.astype(jnp.bfloat16).reshape(proj.shape[0], -1)


def attend_rows(query, key_portion, value_rows, valid_mask, score_scaling):
    score = (
        jnp.einsum("qhd,khd->hqk", query, key_portion, preferred_element_type=jnp.float32)
        * score_scaling
    )
    score = jnp.where(valid_mask[None, None, :], score, -jnp.inf)
    top = jnp.max(score, axis=-1, keepdims=True)
    lse = top + jnp.log(jnp.sum(jnp.exp(score - top), axis=-1, keepdims=True))
    probability = jnp.exp(score - lse)
    weights = probability.astype(jnp.bfloat16)
    attended = jnp.einsum(
        "hqk,khd->qhd", weights, value_rows, preferred_element_type=jnp.float32
    ).astype(jnp.bfloat16)
    return (attended, lse, probability, weights)


def query_gradient_list(attended, dout, probability, value_rows, key_portion, score_scaling):
    row_delta = jnp.sum(dout.astype(jnp.float32) * attended.astype(jnp.float32), axis=-1)
    prob_grad = jnp.einsum("qhd,khd->hqk", dout, value_rows, preferred_element_type=jnp.float32)
    dscore = (probability * (prob_grad - row_delta.T[:, :, None]) * score_scaling).astype(
        jnp.bfloat16
    )
    dquery = jnp.einsum("hqk,khd->qhd", dscore, key_portion, preferred_element_type=jnp.float32)
    return (row_delta, dscore, dquery)


def owning_gradients(
    queries, douts, lse, row_delta, key_portion, value_rows, valid_mask, score_scaling
):

    def one_head(items):
        query_head, dout_head, lse_head, delta_head, key_head, value_head = items
        score = (
            jnp.einsum("nqd,kd->nqk", query_head, key_head, preferred_element_type=jnp.float32)
            * score_scaling
        )
        score = jnp.where(valid_mask[None, None, :], score, -jnp.inf)
        probability = jnp.exp(score - lse_head[..., None])
        weights = probability.astype(jnp.bfloat16)
        prob_grad = jnp.einsum(
            "nqd,kd->nqk", dout_head, value_head, preferred_element_type=jnp.float32
        )
        dscore = (probability * (prob_grad - delta_head[..., None]) * score_scaling).astype(
            jnp.bfloat16
        )
        key_terms = rounded(
            jnp.einsum("nqk,nqd->nkd", dscore, query_head, preferred_element_type=jnp.float32)
        )
        value_terms = rounded(
            jnp.einsum("nqk,nqd->nkd", weights, dout_head, preferred_element_type=jnp.float32)
        )
        return (jnp.sum(key_terms, 0), jnp.sum(value_terms, 0))

    dkey, dvalue = lax.map(
        one_head,
        (
            jnp.moveaxis(queries, 2, 0),
            jnp.moveaxis(douts, 2, 0),
            jnp.moveaxis(lse, 2, 0),
            jnp.moveaxis(row_delta, 2, 0),
            jnp.moveaxis(key_portion, 1, 0),
            jnp.moveaxis(value_rows, 1, 0),
        ),
    )
    return (jnp.moveaxis(dkey, 0, 1), jnp.moveaxis(dvalue, 0, 1))


def output_backward(grads, w_out):
    result = lax.dot_general(grads, w_out, CONTRACT_COLS, preferred_element_type=jnp.float32)
    return result.astype(jnp.bfloat16).reshape(grads.shape[0], -1, HEAD_SIZE)


def qkv_back(grads, w_qkv):
    return lax.dot_general(
        grads, w_qkv.reshape(w_qkv.shape[0], -1), CONTRACT_COLS, preferred_element_type=jnp.float32
    )


def take_cols(array, first_col, col_count):
    return lax.dynamic_slice_in_dim(array, first_col, col_count, 1)


def per_device(
    img,
    txt,
    ctl,
    dy_img,
    text_output_cotangent,
    live_text_length,
    modulation,
    query_key_gains,
    w_qkv_img,
    image_output_weight,
    w_qkv_txt,
    text_output_weight,
    w_qkv_ctl,
    w_out_ctl,
):
    sequence_count = lax.axis_size("seq")
    seq_pos = lax.axis_index("seq")
    tp_pos = lax.axis_index("tp")
    image_rows = img.shape[0]
    text_rows = txt.shape[0]
    main_rows = image_rows + text_rows
    every_row = main_rows + image_rows
    share_cols = img.shape[1]
    model_width = modulation.shape[2]
    head_feature_width = image_output_weight.shape[0]
    heads_on_shard = head_feature_width // HEAD_SIZE
    score_scaling = HEAD_SIZE ** (-0.5)
    first_col = tp_pos * share_cols
    full_img, full_txt, full_ctl, full_dyi, full_dyt = (
        lax.all_gather(img, "tp", axis=1, tiled=True),
        lax.all_gather(txt, "tp", axis=1, tiled=True),
        lax.all_gather(ctl, "tp", axis=1, tiled=True),
        lax.all_gather(dy_img, "tp", axis=1, tiled=True),
        lax.all_gather(text_output_cotangent, "tp", axis=1, tiled=True),
    )
    n_img, image_normalized, rs_img = norm_rows(full_img, modulation[0])
    n_txt, text_normalized, rs_txt = norm_rows(full_txt, modulation[1])
    n_ctl, control_normalized, rs_ctl = norm_rows(full_ctl, modulation[2])
    image_projected, image_query, image_key, image_value = project(
        n_img, w_qkv_img, query_key_gains[0]
    )
    text_projected, text_query, text_key, text_value = project(n_txt, w_qkv_txt, query_key_gains[1])
    control_projected, control_query, k_ctl, v_ctl = project(n_ctl, w_qkv_ctl, query_key_gains[2])
    main_query = jnp.concatenate([image_query, text_query], 0)
    own_keys = jnp.concatenate([image_key, text_key], 0)
    own_vals = jnp.concatenate([image_value, text_value], 0)
    local_keys = jnp.concatenate([own_keys, k_ctl], 0).reshape(every_row, head_feature_width)
    local_vals = jnp.concatenate([own_vals, v_ctl], 0).reshape(every_row, head_feature_width)
    kv_local = jnp.concatenate([local_keys, local_vals], 1)
    kv_all = lax.all_gather(kv_local, "seq", axis=0, tiled=True)
    key_value_reshaped = kv_all.reshape(sequence_count, every_row, 2, heads_on_shard, HEAD_SIZE)
    main_keys = key_value_reshaped[:, :main_rows, 0].reshape(
        sequence_count * main_rows, heads_on_shard, HEAD_SIZE
    )
    main_values = key_value_reshaped[:, :main_rows, 1].reshape(
        sequence_count * main_rows, heads_on_shard, HEAD_SIZE
    )
    control_keys = key_value_reshaped[:, main_rows:, 0].reshape(
        sequence_count * image_rows, heads_on_shard, HEAD_SIZE
    )
    control_values = key_value_reshaped[:, main_rows:, 1].reshape(
        sequence_count * image_rows, heads_on_shard, HEAD_SIZE
    )
    slot_row_index = lax.broadcasted_iota(jnp.int32, (sequence_count, main_rows), 1)
    slot_shard = lax.broadcasted_iota(jnp.int32, (sequence_count, main_rows), 0)
    main_valid_mask = (
        (slot_row_index < image_rows)
        | (slot_shard * text_rows + slot_row_index - image_rows < live_text_length[0])
    ).reshape(-1)
    valid_ctl = jnp.full((sequence_count * image_rows,), True)
    main_output, main_logsumexp, main_probabilities, main_weights = attend_rows(
        main_query, main_keys, main_values, main_valid_mask, score_scaling
    )
    o_cblk, control_logsumexp, prob_ctl, wt_ctl = attend_rows(
        control_query, control_keys, control_values, valid_ctl, score_scaling
    )
    image_output = main_output[:image_rows].reshape(image_rows, head_feature_width)
    text_output = main_output[image_rows:].reshape(text_rows, head_feature_width)
    o_ctl = o_cblk.reshape(image_rows, head_feature_width)
    gate_img = modulation[0, 2]
    gate_txt = modulation[1, 2]
    gate_ctl = modulation[2, 2]
    mix_img = gate_img * jnp.dot(
        image_output, image_output_weight, preferred_element_type=jnp.float32
    ) + gate_ctl * jnp.dot(o_ctl, w_out_ctl, preferred_element_type=jnp.float32)
    mix_txt = gate_txt * jnp.dot(
        text_output, text_output_weight, preferred_element_type=jnp.float32
    )
    out_terms = jnp.concatenate([mix_img, mix_txt], 0)
    out_summed = take_cols(
        lax.psum(out_terms.astype(jnp.bfloat16), "tp").astype(jnp.float32), first_col, share_cols
    )
    y_img = (img.astype(jnp.float32) + out_summed[:image_rows]).astype(jnp.bfloat16)
    y_txt = (txt.astype(jnp.float32) + out_summed[image_rows:]).astype(jnp.bfloat16)
    image_modulation = (gate_img * full_dyi.astype(jnp.float32)).astype(jnp.bfloat16)
    text_modulation = (gate_txt * full_dyt.astype(jnp.float32)).astype(jnp.bfloat16)
    e_ctl = (gate_ctl * full_dyi.astype(jnp.float32)).astype(jnp.bfloat16)
    main_output_gradient = jnp.concatenate(
        [
            output_backward(image_modulation, image_output_weight),
            output_backward(text_modulation, text_output_weight),
        ],
        0,
    )
    control_output_gradient = output_backward(e_ctl, w_out_ctl)
    out_term = rounded(
        lax.dot_general(o_ctl, e_ctl, CONTRACT_ROWS, preferred_element_type=jnp.float32)
    )
    main_row_delta, main_score_gradient, main_query_gradient = query_gradient_list(
        main_output, main_output_gradient, main_probabilities, main_values, main_keys, score_scaling
    )
    control_row_delta, ds_ctl, control_query_gradient = query_gradient_list(
        o_cblk, control_output_gradient, prob_ctl, control_values, control_keys, score_scaling
    )
    query_row_values = jnp.concatenate([main_query, control_query], 0).reshape(
        every_row, head_feature_width
    )
    gradient_rows = jnp.concatenate([main_output_gradient, control_output_gradient], 0).reshape(
        every_row, head_feature_width
    )
    logsumexp_rows = jnp.concatenate([main_logsumexp[:, :, 0].T, control_logsumexp[:, :, 0].T], 0)
    delta_row_values = jnp.concatenate([main_row_delta, control_row_delta], 0)
    query_all = lax.all_gather(
        jnp.concatenate([query_row_values, gradient_rows], 1), "seq", axis=0, tiled=True
    )
    lse_all, delta_all = (
        lax.all_gather(logsumexp_rows, "seq", axis=0, tiled=True),
        lax.all_gather(delta_row_values, "seq", axis=0, tiled=True),
    )
    query_reshaped = query_all.reshape(sequence_count, every_row, 2, heads_on_shard, HEAD_SIZE)
    logsumexp_reshaped = lse_all.reshape(sequence_count, every_row, heads_on_shard)
    delta_reshaped = delta_all.reshape(sequence_count, every_row, heads_on_shard)
    owned_row = lax.broadcasted_iota(jnp.int32, (main_rows,), 0)
    own_valid = (owned_row < image_rows) | (
        seq_pos * text_rows + owned_row - image_rows < live_text_length[0]
    )
    main_key_gradient, main_value_gradient = owning_gradients(
        query_reshaped[:, :main_rows, 0],
        query_reshaped[:, :main_rows, 1],
        logsumexp_reshaped[:, :main_rows],
        delta_reshaped[:, :main_rows],
        own_keys,
        own_vals,
        own_valid,
        score_scaling,
    )
    control_key_gradient, control_value_gradient = owning_gradients(
        query_reshaped[:, main_rows:, 0],
        query_reshaped[:, main_rows:, 1],
        logsumexp_reshaped[:, main_rows:],
        delta_reshaped[:, main_rows:],
        k_ctl,
        v_ctl,
        jnp.full((image_rows,), True),
        score_scaling,
    )
    key_grads = jnp.concatenate(
        [
            jnp.concatenate([main_key_gradient, control_key_gradient], 0).reshape(
                every_row, head_feature_width
            ),
            jnp.concatenate([main_value_gradient, control_value_gradient], 0).reshape(
                every_row, head_feature_width
            ),
        ],
        1,
    )
    gradient_reshaped = key_grads.reshape(every_row, 2, heads_on_shard, HEAD_SIZE)
    image_projection_gradient = projection_gradient(
        image_projected,
        query_key_gains[0],
        main_query_gradient[:image_rows],
        gradient_reshaped[:image_rows, 0],
        gradient_reshaped[:image_rows, 1],
    )
    text_projection_gradient = projection_gradient(
        text_projected,
        query_key_gains[1],
        main_query_gradient[image_rows:],
        gradient_reshaped[image_rows:main_rows, 0],
        gradient_reshaped[image_rows:main_rows, 1],
    )
    dp_ctl = projection_gradient(
        control_projected,
        query_key_gains[2],
        control_query_gradient,
        gradient_reshaped[main_rows:, 0],
        gradient_reshaped[main_rows:, 1],
    )
    qkv_term = rounded(
        lax.dot_general(n_ctl, dp_ctl, CONTRACT_ROWS, preferred_element_type=jnp.float32)
    ).reshape(model_width, 3, head_feature_width)
    grad_qkv, grad_out = (
        lax.psum_scatter(
            qkv_term.astype(jnp.bfloat16), "seq", scatter_dimension=0, tiled=True
        ).astype(jnp.float32),
        lax.psum_scatter(
            out_term.astype(jnp.bfloat16), "seq", scatter_dimension=1, tiled=True
        ).astype(jnp.float32),
    )
    dn_terms = jnp.concatenate(
        [
            qkv_back(image_projection_gradient, w_qkv_img),
            qkv_back(text_projection_gradient, w_qkv_txt),
            qkv_back(dp_ctl, w_qkv_ctl),
        ],
        0,
    )
    factor = jnp.concatenate(
        [
            jnp.broadcast_to(1.0 + modulation[0, 1], (image_rows, model_width)),
            jnp.broadcast_to(1.0 + modulation[1, 1], (text_rows, model_width)),
            jnp.broadcast_to(1.0 + modulation[2, 1], (image_rows, model_width)),
        ],
        0,
    )
    standardized_all = jnp.concatenate([image_normalized, text_normalized, control_normalized], 0)
    inverse_deviation_all = jnp.concatenate([rs_img, rs_txt, rs_ctl], 0)
    dn_full = lax.psum(dn_terms.astype(jnp.bfloat16), "tp").astype(jnp.float32)
    scaled_input = dn_full * factor
    centered_input = scaled_input - jnp.mean(scaled_input, axis=-1, keepdims=True)
    backward_result = take_cols(
        (
            centered_input
            - standardized_all * jnp.mean(scaled_input * standardized_all, axis=-1, keepdims=True)
        )
        * inverse_deviation_all,
        first_col,
        share_cols,
    )
    d_img = (dy_img.astype(jnp.float32) + backward_result[:image_rows]).astype(jnp.bfloat16)
    text_input_gradient = (
        text_output_cotangent.astype(jnp.float32) + backward_result[image_rows:main_rows]
    ).astype(jnp.bfloat16)
    control_input_gradient = backward_result[main_rows:].astype(jnp.bfloat16)
    return (y_img, y_txt, d_img, text_input_gradient, control_input_gradient, grad_qkv, grad_out)


def solution(mesh):
    in_specs = (
        P("seq", "tp"),
        P("seq", "tp"),
        P("seq", "tp"),
        P("seq", "tp"),
        P("seq", "tp"),
        P(),
        P(),
        P(),
        P(None, None, "tp"),
        P("tp", None),
        P(None, None, "tp"),
        P("tp", None),
        P(None, None, "tp"),
        P("tp", None),
    )
    out_specs = (
        P("seq", "tp"),
        P("seq", "tp"),
        P("seq", "tp"),
        P("seq", "tp"),
        P("seq", "tp"),
        P("seq", None, "tp"),
        P("tp", "seq"),
    )
    return jax.shard_map(
        per_device, mesh=mesh, in_specs=in_specs, out_specs=out_specs, check_vma=False
    )
```

profile of v0, /device:TPU:0, one launch (start us, length us, event | category | flops | bytes accessed | tf_op | source)
XLA Modules:
  0.0 1740.1 jit_solution(14406740378905065373)
XLA Ops:
  7.2 7.1 all-gather
  17.2 9.5 all_gather.27
  28.1 8.7 copy.201
  43.6 8.8 copy.205
  58.8 9.8 all_gather.29
  71.0 8.7 copy.210
  110.5 14.9 all_gather.31
  148.5 251.4 %all-gather.7.cloned.1.call-done = bf16[8704,768]{1,0:T(8,128)(2,1)} async-done(((bf16[272,768]{1,0:T(8,128)(2,1)}), bf16[8704,768]{1,0:T(8,128)(2,1)}) %all-gather.7.cloned.1.call-update) | async-done | bytes 13369360 | tf_op jit(solution)/shard_map/all_gather | solution.py:187
  399.9 16.9 copy.217
  416.7 35.3 %reshape.449 = bf16[32,272,2,6,64]{1,0,4,3,2:T(8,128)(2,1)} reshape(bf16[8704,768]{0,1:T(8,128)(2,1)} %copy.217) | data formatting | bytes 26738688 | tf_op jit(solution)/shard_map/reshape | solution.py:188
  452.0 7.5 fusion.174
  459.5 10.4 fusion.175
  469.9 222.3 %all-gather.9.cloned.1.call-done = bf16[8704,768]{1,0:T(8,128)(2,1)} async-done(((bf16[272,768]{1,0:T(8,128)(2,1)}), bf16[8704,768]{1,0:T(8,128)(2,1)}) %all-gather.9.cloned.1.call-update) | async-done | bytes 13369360 | tf_op jit(solution)/shard_map/all_gather | solution.py:260
  692.1 16.8 copy.230
  709.0 35.3 %reshape.455 = bf16[32,272,2,6,64]{1,0,4,3,2:T(8,128)(2,1)} reshape(bf16[8704,768]{0,1:T(8,128)(2,1)} %copy.230) | data formatting | bytes 26738688 | tf_op jit(solution)/shard_map/reshape | solution.py:267
  744.2 7.4 slice_bitcast_fusion.2
  751.7 10.4 slice_bitcast_fusion
  762.0 12.0 reshape_squeeze.13
  774.0 12.4 reshape_squeeze.12
  786.4 9.8 fusion.54
  796.2 9.2 exponential_reduce_fusion
  805.4 8.2 multiply_reduce_fusion.2
  839.0 79.2 %all-gather.3 = f32[32,272,6]{1,2,0:T(8,128)S(1)} all-gather(f32[1,272,6]{1,2,0:T(8,128)S(1)} %maximum_bitcast_fusion.3), channel_id=1, replica_groups=mesh['seq'=32,'tp'=4] {'seq'}, dimensions={0}, use_global_device_ids=true | all-gather | bytes 215424 | tf_op jit(solution)/shard_map/all_gather | solution.py:265
  919.1 79.8 %all-gather.2 = f32[32,272,6]{1,2,0:T(8,128)S(1)} all-gather(f32[1,272,6]{1,2,0:T(8,128)S(1)} %maximum_bitcast_fusion.2), channel_id=1, replica_groups=mesh['seq'=32,'tp'=4] {'seq'}, dimensions={0}, use_global_device_ids=true | all-gather | bytes 215424 | tf_op jit(solution)/shard_map/all_gather | solution.py:264
  999.6 11.8 fusion.75
  1011.4 124.0 %while.26 = (s32[]{:T(128)}, f32[6,144,64]{1,2,0:T(8,128)}, bf16[6,144,64]{1,2,0:T(8,128)(2,1)}, bf16[6,32,144,64]{2,1,3,0:T(8,128)(2,1)}, bf16[6,144,64]{1,2,0:...) while((s32[]{:T(128)}, f32[6,144,64]{1,2,0:T(8,128)}, ...), condition=%wide.region_23.24_spmd.clone, body=%wide.region_20.23_spmd.clone.sunk | while | flops 348789440 | bytes 22185032 | solution.py:108
  1145.9 71.0 %while.25 = (s32[]{:T(128)}, f32[6,128,64]{1,2,0:T(8,128)}, bf16[6,128,64]{1,2,0:T(8,128)(2,1)}, bf16[6,32,128,64]{2,1,3,0:T(8,128)(2,1)}, bf16[6,128,64]{1,2,0:...) while((s32[]{:T(128)}, f32[6,128,64]{1,2,0:T(8,128)}, ...), condition=%wide.region_31.32_spmd, body=%wide.region_28.31_spmd.sunk | while | flops 274710528 | bytes 12877957 | solution.py:108
  1217.0 13.5 fusion.115
  1257.7 9.0 copy.241
  1266.7 12.5 copy.242
  1286.0 19.5 %all-reduce.9.cloned.1.call-done = (bf16[144,2432]{1,0:T(8,128)(2,1)}, bf16[272,2432]{1,0:T(8,128)(2,1)}) async-done(((bf16[144,2432]{1,0:T(8,128)(2,1)}, bf16[272,2432]{1,0:T(8,128)(2,1)}), (bf16[144,2432]{1,0:T(8,128)(2,1)}, bf16[272,2432]{1,0:T(8,128)(2,1)})) %all-reduce.9.cloned.1.call-update) | async-done | bytes 2023440 | tf_op jit(solution)/shard_map/psum | solution.py:228
  1316.9 412.7 %all-reduce.7.cloned.1.call-done = (bf16[2432,3,384]{2,1,0:T(4,128)(2,1)}, bf16[384,2432]{1,0:T(8,128)(2,1)}) async-done(((bf16[2432,3,384]{2,1,0:T(4,128)(2,1)}, bf16[384,2432]{1,0:T(8,128)(2,1)}), (bf16[2432,3,384]{2,1,0:T(4,128)(2,1)}, bf16[384,2432]{1,0:T(8,128)(2,1)})) %all-reduce.7.cloned.1.call-update) | async-done | bytes 7471120
  (554 shorter events, 352.1 us)
Async XLA Ops:
  7.2 131.2 %copy-start = (bf16[384,2432]{1,0:T(8,128)(2,1)S(1)}, bf16[384,2432]{1,0:T(8,128)(2,1)}, u32[]{:S(2)}) copy-start(bf16[384,2432]{1,0:T(8,128)(2,1)} %param.31) | copy-start | bytes 5603332
  7.2 392.7 %all-gather.7.cloned.1.call-start = ((), (), s32[]{:S(2)}) async-start(), calls=%async_computation | async-start | bytes 13787136 | tf_op jit(solution)/shard_map/all_gather | solution.py:187
  17.1 19.7 %copy-start.66 = (f32[2432]{0:T(1024)}, f32[2432]{0:T(1024)S(1)}, u32[]{:S(2)}) copy-start(f32[2432]{0:T(1024)S(1)} %get-tuple-element.293) | copy-start | bytes 29188
  17.1 35.2 %copy-start.53 = (f32[2432]{0:T(1024)}, f32[2432]{0:T(1024)S(1)}, u32[]{:S(2)}) copy-start(f32[2432]{0:T(1024)S(1)} %get-tuple-element.291) | copy-start | bytes 29188
  17.1 62.6 %copy-start.42 = (f32[2432]{0:T(1024)}, f32[2432]{0:T(1024)S(1)}, u32[]{:S(2)}) copy-start(f32[2432]{0:T(1024)S(1)} %get-tuple-element.289) | copy-start | bytes 29188
  17.1 62.6 %copy-start.48 = (f32[2432]{0:T(1024)}, f32[2432]{0:T(1024)S(1)}, u32[]{:S(2)}) copy-start(f32[2432]{0:T(1024)S(1)} %get-tuple-element.288) | copy-start | bytes 29188
  17.1 119.0 %copy-start.51 = (f32[2432]{0:T(1024)}, f32[2432]{0:T(1024)S(1)}, u32[]{:S(2)}) copy-start(f32[2432]{0:T(1024)S(1)} %get-tuple-element.294) | copy-start | bytes 29188
  17.1 121.2 %copy-start.44 = (f32[2432]{0:T(1024)}, f32[2432]{0:T(1024)S(1)}, u32[]{:S(2)}) copy-start(f32[2432]{0:T(1024)S(1)} %get-tuple-element.295) | copy-start | bytes 29188
  17.1 121.9 %copy-start.50 = (f32[2432]{0:T(1024)}, f32[2432]{0:T(1024)S(1)}, u32[]{:S(2)}) copy-start(f32[2432]{0:T(1024)S(1)} %get-tuple-element.287) | copy-start | bytes 29188
  56.6 89.7 %copy-start.5 = (f32[16,3,6,64]{0,3,2,1:T(8,128)}, f32[16,3,6,64]{0,3,2,1:T(8,128)S(1)}, u32[]{:S(2)}) copy-start(f32[16,3,6,64]{0,3,2,1:T(8,128)S(1)} %fusion.143) | copy-start | bytes 221188
  85.4 17.4 copy-start.59
  89.3 55.9 %copy-start.62 = (f32[128,6]{0,1:T(8,128)}, f32[128,6]{0,1:T(8,128)S(1)}, u32[]{:S(2)}) copy-start(f32[128,6]{0,1:T(8,128)S(1)} %fusion.151) | copy-start | bytes 9220
  93.2 53.0 %copy-start.61 = (f32[16,6]{0,1:T(8,128)}, f32[16,6]{0,1:T(8,128)S(1)}, u32[]{:S(2)}) copy-start(f32[16,6]{0,1:T(8,128)S(1)} %fusion.152) | copy-start | bytes 1156
  95.1 52.7 %copy-start.63 = (f32[128,6]{0,1:T(8,128)}, f32[128,6]{0,1:T(8,128)S(1)}, u32[]{:S(2)}) copy-start(f32[128,6]{0,1:T(8,128)S(1)} %fusion.153) | copy-start | bytes 9220
  100.6 591.5 %all-gather.9.cloned.1.call-start = ((), (), s32[]{:S(2)}) async-start(), calls=%async_computation.1 | async-start | bytes 13787136 | tf_op jit(solution)/shard_map/all_gather | solution.py:260
  102.7 31.4 %copy-start.85 = (f32[384]{0:T(512)S(1)}, f32[384]{0:T(512)}, u32[]{:S(2)}) copy-start(f32[384]{0:T(512)} %mul.712) | copy-start | bytes 4612
  127.5 17.6 %copy-start.65 = (f32[128,6]{0,1:T(8,128)}, f32[128,6]{0,1:T(8,128)S(1)}, u32[]{:S(2)}) copy-start(f32[128,6]{0,1:T(8,128)S(1)} %fusion.154) | copy-start | bytes 9220
  129.8 16.5 copy-start.64
  140.7 1164.9 %all-reduce.9.cloned.1.call-start = ((), (), s32[]{:S(2)}) async-start(), calls=%async_computation.3 | async-start | bytes 4046848 | tf_op jit(solution)/shard_map/psum | solution.py:228
  142.6 690.0 %copy-start.36 = (bf16[128,384]{0,1:T(8,128)(2,1)}, bf16[128,384]{0,1:T(8,128)(2,1)S(1)}, u32[]{:S(2)}) copy-start(bf16[128,384]{0,1:T(8,128)(2,1)S(1)} %copy.231) | copy-start | bytes 294916
  832.6 86.4 %copy-start.69 = (f32[6,128]{1,0:T(8,128)}, f32[6,128]{1,0:T(8,128)S(1)}, u32[]{:S(2)}) copy-start(f32[6,128]{1,0:T(8,128)S(1)} %log_add_fusion.1) | copy-start | bytes 9220
  838.9 172.5 %copy-start.71 = (f32[128,6]{0,1:T(8,128)}, f32[128,6]{0,1:T(8,128)S(1)}, u32[]{:S(2)}) copy-start(f32[128,6]{0,1:T(8,128)S(1)} %get-tuple-element.384) | copy-start | bytes 9220
  1011.4 124.0 %copy-start.6 = (f32[16,3,6,64]{0,3,2,1:T(8,128)S(1)}, f32[16,3,6,64]{0,3,2,1:T(8,128)}, u32[]{:S(2)}) copy-start(f32[16,3,6,64]{0,3,2,1:T(8,128)} %copy-done.5) | copy-start | bytes 221188
  1011.4 130.9 %copy-start.45 = (f32[2432]{0:T(1024)S(1)}, f32[2432]{0:T(1024)}, u32[]{:S(2)}) copy-start(f32[2432]{0:T(1024)} %copy-done.44) | copy-start | bytes 29188
  1216.9 16.3 copy-start.14
  1216.9 17.4 copy-start.23
  1216.9 18.9 %copy-start.7 = (f32[16,3,6,64]{0,3,2,1:T(8,128)S(1)}, f32[16,3,6,64]{0,3,2,1:T(8,128)}, u32[]{:S(2)}) copy-start(f32[16,3,6,64]{0,3,2,1:T(8,128)} %copy-done.5) | copy-start | bytes 221188
  1217.0 20.8 %copy-start.40 = (bf16[128,6,64]{0,2,1:T(8,128)(2,1)S(1)}, bf16[128,6,64]{0,2,1:T(8,128)(2,1)}, u32[]{:S(2)}) copy-start(bf16[128,6,64]{0,2,1:T(8,128)(2,1)} %slice.284) | copy-start | bytes 294916
  1251.5 478.1 %all-reduce.7.cloned.1.call-start = ((), (), s32[]{:S(2)}) async-start(), calls=%async_computation.2 | async-start | bytes 18677760
  1279.3 30.6 %copy-start.54 = (f32[2432]{0:T(1024)S(1)}, f32[2432]{0:T(1024)}, u32[]{:S(2)}) copy-start(f32[2432]{0:T(1024)} %copy-done.53) | copy-start | bytes 29188
  1279.3 30.6 %copy-start.67 = (f32[2432]{0:T(1024)S(1)}, f32[2432]{0:T(1024)}, u32[]{:S(2)}) copy-start(f32[2432]{0:T(1024)} %copy-done.66) | copy-start | bytes 29188
  1286.0 24.1 %copy-start.20 = (f32[128,2432]{1,0:T(8,128)S(1)}, f32[128,2432]{1,0:T(8,128)}, u32[]{:S(2)}) copy-start(f32[128,2432]{1,0:T(8,128)} %fusion.67) | copy-start | bytes 3735556
  (96 other events, 519.8 us)
Sparse Core Ops, SparseCore 0:
  100.7 299.1 all-gather.6
  401.5 290.5 all-gather.8
  1251.6 53.9 all-reduce.8
  1308.2 421.3 all-reduce.6
where the time goes:
time: 1750 us; the launch traced here: 1740 us
  waiting for transfers between devices  906 us (52%)
  local copies, waits for them, and re-layouts  319 us (18%)
  matrix products  222 us (13%)
  blocking collectives  207 us (12%)
  other arithmetic  68.3 us (4%)
    unnamed x5, waiting for transfers between devices  413 us
    all_gather x1, waiting for transfers between devices, per_device(): kv_all = lax.all_gather(kv_local, 'seq', axis=0, tiled=True)  251 us
    all_gather x1, waiting for transfers between devices, per_device(): lax.all_gather(jnp.concatenate([query_row_values, gradient_rows], 1), 'se...  222 us
    all_gather x1, blocking collectives, per_device(): lax.all_gather(logsumexp_rows, 'seq', axis=0, tiled=True)  79.8 us
    all_gather x1, blocking collectives, per_device(): lax.all_gather(delta_row_values, 'seq', axis=0, tiled=True)  79.2 us
    dot_general x12, matrix products, one_head(): jnp.einsum('nqk,nqd->nkd', dscore, query_head, preferred_element_type=jnp...  54.7 us
    dot_general x12, matrix products, one_head(): jnp.einsum('nqk,nqd->nkd', weights, dout_head, preferred_element_type=jnp...  40.9 us
    dot_general x12, matrix products, one_head(): jnp.einsum('nqd,kd->nqk', query_head, key_head, preferred_element_type=jn...  39.3 us
  transfers between devices with their start and end apart: 4, of which 4 were waited for; matrix products, arithmetic and copies ran while one was open for 8% of the time, Pallas kernels for 0%

commit v1 on v0

v1 whole, which is shorter than its diff:
```python
import jax
import jax.numpy as jnp
from jax import lax
from jax.experimental import pallas as pl
from jax.experimental.pallas import tpu as pltpu
from jax.sharding import Mesh, PartitionSpec as P

EPS = 1e-06
HEAD = 64
HEADS = 6
WIDTH = HEADS * HEAD
D = 2432
SHARE = 608
PIECE = 152
ROWS = 3 * SHARE + PIECE
IMG = 128
TXT = 16
BLOCKS = 32
CHUNK = 192
IMAGE_KEYS = BLOCKS * IMG
TEXT_KEYS = BLOCKS * TXT
MAIN_Q = 48
CTL_Q = 64
MAIN_PARTS = 3
CTL_PARTS = 2
CTL_AT = HEADS * MAIN_PARTS
TQ = 512
TK = 512
F32 = jnp.float32
BF16 = jnp.bfloat16
NT = (((1,), (1,)), ((), ()))
VMEM = pl.BlockSpec(memory_space=pltpu.VMEM)
SMEM = pl.BlockSpec(memory_space=pltpu.SMEM)
ANY = pl.BlockSpec(memory_space=pl.ANY)
HBM = pl.BlockSpec(memory_space=pltpu.HBM)


def params(mib):
    return pltpu.CompilerParams(vmem_limit_bytes=mib * 1024 * 1024)


def dot(a, b):
    return jnp.dot(a, b, preferred_element_type=F32)


def dot_nt(a, b):
    return lax.dot_general(a, b, NT, preferred_element_type=F32)


def head(values, h):
    return values[:, h * HEAD : (h + 1) * HEAD]


def inverse_rms(values):
    return lax.rsqrt(jnp.mean(values * values, axis=-1, keepdims=True) + EPS)


def spread_text(packed):
    return jnp.concatenate([packed] + [pltpu.roll(packed, 128 - 32 * a, 1) for a in (1, 2, 3)], 0)


def pack_text(columns):
    pieces = [columns[PIECE * a : PIECE * (a + 1)] for a in range(4)]
    return pieces[0] + sum(pltpu.roll(pieces[a], 32 * a, 1) for a in (1, 2, 3))


def load_kernel(after, *refs):
    sources, targets, token, sems = refs[0:3], refs[3:6], refs[6], refs[7]
    token[...] = jnp.zeros_like(token)
    copies = [pltpu.make_async_copy(a, b, sems.at[i]) for i, (a, b) in enumerate(zip(sources, targets))]
    for copy in copies:
        copy.start()
    for copy in copies:
        copy.wait()


def load(weights, after):
    return pl.pallas_call(
        load_kernel,
        out_shape=[jax.ShapeDtypeStruct(w.shape, w.dtype) for w in weights] + [jax.ShapeDtypeStruct((8, 128), F32)],
        in_specs=[ANY] + [HBM] * 3,
        out_specs=[VMEM] * 4,
        scratch_shapes=[pltpu.SemaphoreType.DMA((3,))],
        compiler_params=params(40),
        cost_estimate=pl.CostEstimate(flops=0, bytes_accessed=30_000_000, transcendentals=0),
        name="load",
    )(after, *weights)


def order_kernel(x, after, out):
    pass


def ordered(x, after):
    return pl.pallas_call(
        order_kernel,
        out_shape=jax.ShapeDtypeStruct(x.shape, x.dtype),
        in_specs=[ANY] * 2,
        out_specs=ANY,
        input_output_aliases={0: 0},
        compiler_params=params(1),
        name="order",
    )(x, after)


def pack_kernel(img, ctl, dy, txt, dy_txt, out, token, text_rows, sems):
    token[...] = jnp.zeros_like(token)
    copies = [
        pltpu.make_async_copy(part, text_rows.at[i], sems.at[3 + i]) for i, part in enumerate((txt, dy_txt))
    ] + [
        pltpu.make_async_copy(part, out.at[pl.ds(SHARE * i, SHARE)], sems.at[i])
        for i, part in enumerate((img, ctl, dy))
    ]
    for copy in copies:
        copy.start()
    copies[0].wait()
    copies[1].wait()
    text = text_rows[...].reshape(2 * TXT, SHARE).astype(F32)
    text = jnp.concatenate([text, jnp.zeros((IMG - 2 * TXT, SHARE), F32)], 0)
    text = jnp.concatenate([text, jnp.zeros((IMG, 640 - SHARE), F32)], 1)
    out[3 * SHARE :, :] = pack_text(text.T).astype(BF16)
    for copy in copies[2:]:
        copy.wait()


def pre_kernel(
    in0, in1, in2, in3, mod, gains, wq_img, wq_txt, wq_ctl, wo_img, wo_txt, wo_ctl,
    send, proj, xhat, rstd, nz0, nz1, nz2, nz3, ny0, ny1, ny2, ny3,
    gat, nz, ny,
):
    for i, part in enumerate((in0, in1, in2, in3)):
        gat[lax.axis_index("tp") ^ i] = part[...]

    def rows(slab):
        return gat[:, SHARE * slab : SHARE * (slab + 1), :].reshape(D, IMG).T.astype(F32)

    def stream(s, x, e, at):
        count = x.shape[0]
        centered = x - jnp.mean(x, axis=-1, keepdims=True)
        inverse = lax.rsqrt(jnp.mean(centered * centered, axis=-1, keepdims=True) + EPS)
        standard = centered * inverse
        xhat[at : at + count, :] = standard
        rstd[at : at + count, :] = jnp.broadcast_to(inverse, (count, 128))
        n = (standard * (1.0 + mod[s, 1:2, :]) + mod[s, 0:1, :]).astype(BF16)
        wq, wo = ((wq_img, wo_img), (wq_txt, wo_txt), (wq_ctl, wo_ctl))[s]
        pq = dot(n, wq[0])
        pk = dot(n, wq[1])
        pv = dot(n, wq[2])
        proj[at : at + count, 0:WIDTH] = pq
        proj[at : at + count, WIDTH : 2 * WIDTH] = pk
        g = dot_nt(e, wo[...])
        kv, qg = [], []
        for h in range(HEADS):
            q_h, k_h = head(pq, h), head(pk, h)
            q_h = q_h * inverse_rms(q_h) * (gains[s, 0:1, :] * 0.125)
            k_h = k_h * inverse_rms(k_h) * gains[s, 1:2, :]
            kv.append(jnp.concatenate([k_h, head(pv, h)], 1).astype(BF16))
            qg.append(jnp.concatenate([q_h, head(g, h)], 1).astype(BF16))
        return n, kv, qg

    dy = rows(2)
    text = jnp.concatenate([spread_text(gat[c, 3 * SHARE :, :].astype(F32)) for c in range(4)], 0).astype(BF16).T.astype(F32)
    e_img = (mod[0, 2:3, :] * dy).astype(BF16)
    n, kv, qg = stream(0, rows(0), e_img, 0)
    for h in range(HEADS):
        for t in range(MAIN_PARTS):
            to = MAIN_PARTS * h + t
            send[to, 0:IMG, :] = kv[h]
            last = min(IMG, MAIN_Q * (t + 1))
            send[to, IMG + TXT : IMG + TXT + last - MAIN_Q * t, :] = qg[h][MAIN_Q * t : last]
    e_txt = (mod[1, 2:3, :] * text[TXT : 2 * TXT]).astype(BF16)
    n, kv, qg = stream(1, text[0:TXT], e_txt, IMG)
    for h in range(HEADS):
        for t in range(MAIN_PARTS):
            send[MAIN_PARTS * h + t, IMG : IMG + TXT, :] = kv[h]
        send[MAIN_PARTS * h + 2, CHUNK - TXT : CHUNK, :] = qg[h]
    e_ctl = mod[2, 2:3, :] * dy
    n, kv, qg = stream(2, rows(1), e_ctl.astype(BF16), IMG + TXT)
    for h in range(HEADS):
        for u in range(CTL_PARTS):
            to = CTL_AT + CTL_PARTS * h + u
            send[to, 0:IMG, :] = kv[h]
            send[to, IMG:CHUNK, :] = qg[h][CTL_Q * u : CTL_Q * (u + 1)]
    for to in range(CTL_AT + CTL_PARTS * HEADS, BLOCKS):
        send[to] = jnp.zeros((CHUNK, 128), BF16)
    n_t, e_t = n.T, e_ctl.astype(BF16).T
    nz[...] = n_t.reshape(4, SHARE, IMG)
    n_t, e_t = n_t.astype(F32), e_t.astype(F32)
    for y in range(4):
        for j, values in enumerate((n_t, e_t)):
            pieces = [values[SHARE * z + PIECE * y : SHARE * z + PIECE * (y + 1)] for z in range(4)]
            ny[y, j] = jnp.concatenate(pieces, 0).astype(BF16)
    for d, out in enumerate((nz0, nz1, nz2, nz3)):
        out[...] = nz[lax.rem(lax.axis_index("z") + d, 4)]
    for d, out in enumerate((ny0, ny1, ny2, ny3)):
        out[...] = ny[lax.rem(lax.axis_index("y") + d, 4)]


def attention_kernel(role, recv, after, dkv_out, odq, kv, kt, vt, qg, probs, dkv):
    is_main = role[0]
    live = role[1]

    for b in range(BLOCKS):
        kv[IMG * b : IMG * (b + 1), :] = recv[b, 0:IMG, :]

    @pl.when(is_main == 1)
    def _():
        for b in range(BLOCKS):
            kv[IMAGE_KEYS + TXT * b : IMAGE_KEYS + TXT * (b + 1), :] = recv[b, IMG : IMG + TXT, :]
            qg[MAIN_Q * b : MAIN_Q * (b + 1), :] = recv[b, IMG + TXT : CHUNK, :]

    @pl.when(is_main == 0)
    def _():
        kv[IMAGE_KEYS:, :] = jnp.zeros((TEXT_KEYS, 128), BF16)
        for b in range(BLOCKS):
            qg[CTL_Q * b : CTL_Q * (b + 1), :] = recv[b, IMG:CHUNK, :]

    for i in range((IMAGE_KEYS + TEXT_KEYS) // 128):
        block = kv[128 * i : 128 * (i + 1), :].T
        kt[:, 128 * i : 128 * (i + 1)] = block[0:HEAD]
        vt[:, 128 * i : 128 * (i + 1)] = block[HEAD:128]
    dkv[...] = jnp.zeros_like(dkv)
    zeros_half = jnp.zeros((HEAD, TQ), BF16)
    low_lanes = lax.broadcasted_iota(jnp.int32, (TQ, 128), 1) < HEAD

    def q_tile(i, carry):
        q_at = pl.multiple_of(i * TQ, TQ)
        tile = qg[pl.ds(q_at, TQ), :]
        tile_t = tile.T
        g_t = tile_t[HEAD:128].astype(F32)
        q_rhs = jnp.concatenate([tile_t[0:HEAD], zeros_half], 0)
        g_rhs = jnp.concatenate([zeros_half, tile_t[HEAD:128]], 0)
        tile = tile.astype(F32)
        q_only = jnp.where(low_lanes, tile, 0.0).astype(BF16)
        g_only = jnp.where(low_lanes, 0.0, tile).astype(BF16)
        qg_rhs = jnp.concatenate([q_only, g_only], 0)

        def forward(at, state, masked):
            total, o_t = state
            p = jnp.exp(dot(kv[pl.ds(at, TK), :], q_rhs))
            if masked:
                p = jnp.where(lax.broadcasted_iota(jnp.int32, (TK, TQ), 0) < live, p, 0.0)
            probs[pl.ds(at, TK), :] = p
            total = total + jnp.sum(p.reshape(TK // 8, 8, TQ), 0)
            o_t = o_t + dot(vt[:, pl.ds(at, TK)], p.astype(BF16))
            return total, o_t

        state = (jnp.zeros((8, TQ), F32), jnp.zeros((HEAD, TQ), F32))
        state = lax.fori_loop(
            0, IMAGE_KEYS // TK, lambda j, c: forward(pl.multiple_of(j * TK, TK), c, False), state,
            unroll=2,
        )
        total, o_t = lax.fori_loop(0, is_main, lambda j, c: forward(IMAGE_KEYS, c, True), state)
        inverse = 1.0 / jnp.sum(total, axis=0, keepdims=True)
        o_t = (o_t * inverse).astype(BF16).astype(F32)
        delta = jnp.sum(g_t * o_t, axis=0, keepdims=True)

        def backward(at, dq_t):
            p = probs[pl.ds(at, TK), :] * inverse
            ds = (p * (dot(kv[pl.ds(at, TK), :], g_rhs) - delta)).astype(BF16)
            dkv[pl.ds(at, TK), :] += dot(jnp.concatenate([ds, p.astype(BF16)], 1), qg_rhs)
            return dq_t + dot(kt[:, pl.ds(at, TK)], ds)

        dq_t = jnp.zeros((HEAD, TQ), F32)
        dq_t = lax.fori_loop(
            0, IMAGE_KEYS // TK, lambda j, c: backward(pl.multiple_of(j * TK, TK), c), dq_t, unroll=2
        )
        dq_t = lax.fori_loop(0, is_main, lambda j, c: backward(IMAGE_KEYS, c), dq_t)
        odq[pl.ds(q_at, TQ), :] = jnp.concatenate([o_t, dq_t * 0.125], 0).astype(BF16).T
        return carry

    tiles = jnp.where(is_main == 1, BLOCKS * MAIN_Q // TQ, BLOCKS * CTL_Q // TQ)
    lax.fori_loop(0, tiles, q_tile, 0)

    dkv_out[...] = dkv[...].astype(BF16)


def scatter_kernel(role, dkv, odq, after0, after1, after2, after3, after4, out):
    for b in range(BLOCKS):
        out[b, 0:IMG, :] = dkv[IMG * b : IMG * (b + 1), :]

    @pl.when(role[0] == 1)
    def _():
        for b in range(BLOCKS):
            out[b, IMG : IMG + TXT, :] = dkv[IMAGE_KEYS + TXT * b : IMAGE_KEYS + TXT * (b + 1), :]
            out[b, IMG + TXT : CHUNK, :] = odq[MAIN_Q * b : MAIN_Q * (b + 1), :]

    @pl.when(role[0] == 0)
    def _():
        for b in range(BLOCKS):
            out[b, IMG:CHUNK, :] = odq[CTL_Q * b : CTL_Q * (b + 1), :]


def head_norm_back(x, gain, dy):
    inverse = inverse_rms(x)
    dy = dy * gain
    return inverse * dy - x * (inverse * inverse * inverse * jnp.mean(x * dy, axis=-1, keepdims=True))


def head_back(s, at, count, dkv, odq, proj, gains):
    o, dq, dk, dv = [], [], [], []
    for h in range(HEADS):
        x_q = proj[at : at + count, h * HEAD : (h + 1) * HEAD]
        x_k = proj[at : at + count, WIDTH + h * HEAD : WIDTH + (h + 1) * HEAD]
        o.append(odq[h][:, 0:HEAD])
        dq.append(head_norm_back(x_q, gains[s, 0:1, :], odq[h][:, HEAD:128]))
        dk.append(head_norm_back(x_k, gains[s, 1:2, :], dkv[h][:, 0:HEAD]))
        dv.append(dkv[h][:, HEAD:128])
    return [jnp.concatenate(parts, 1).astype(BF16) for parts in (dq, dk, dv, o)]


def head_back_ctl_kernel(recv, proj, gains, by_z, by_y):
    dkv, odq = [], []
    for h in range(HEADS):
        parts = [recv[CTL_AT + CTL_PARTS * h + u].astype(F32) for u in range(CTL_PARTS)]
        dkv.append(parts[0][0:IMG] + parts[1][0:IMG])
        odq.append(jnp.concatenate([parts[0][IMG:], parts[1][IMG:]], 0))
    dq, dk, dv, o = head_back(2, IMG + TXT, IMG, dkv, odq, proj, gains)
    by_z[:, 0:WIDTH] = dq
    by_z[:, WIDTH:] = dk
    by_y[:, 0:WIDTH] = dv
    by_y[:, WIDTH:] = o


def head_back_main(recv, proj, gains, main):
    kv_img, kv_txt, oq_img, oq_txt = [], [], [], []
    for h in range(HEADS):
        parts = [recv[MAIN_PARTS * h + t].astype(F32) for t in range(MAIN_PARTS)]
        kv = parts[0][0 : IMG + TXT] + parts[1][0 : IMG + TXT] + parts[2][0 : IMG + TXT]
        kv_img.append(kv[0:IMG])
        kv_txt.append(kv[IMG:])
        oq_img.append(
            jnp.concatenate(
                [parts[0][IMG + TXT :], parts[1][IMG + TXT :], parts[2][IMG + TXT : CHUNK - TXT]], 0
            )
        )
        oq_txt.append(parts[2][CHUNK - TXT :])
    for j, part in enumerate(head_back(0, 0, IMG, kv_img, oq_img, proj, gains)):
        main[0:IMG, j * WIDTH : (j + 1) * WIDTH] = part
    for j, part in enumerate(head_back(1, IMG, TXT, kv_txt, oq_txt, proj, gains)):
        main[IMG:, j * WIDTH : (j + 1) * WIDTH] = part


def back(s, dq, dk, dv, o, wq, wo, mod, standard, inverse):
    u = dot_nt(dq, wq[0]) + dot_nt(dk, wq[1]) + dot_nt(dv, wq[2])
    u = u * (1.0 + mod[s, 1:2, :])
    u = u - jnp.mean(u, axis=-1, keepdims=True) - standard * jnp.mean(u * standard, axis=-1, keepdims=True)
    return u * inverse, mod[s, 2:3, :] * dot(o, wo[...])


def slab(values):
    return values.astype(BF16).T.reshape(4, SHARE, IMG)


def post_kernel(
    recv, proj, gains, by_z, by_y, xhat, rstd, mod, wq_img, wq_txt, wq_ctl, wo_img, wo_txt, wo_ctl,
    mine0, mine1, theirs0, theirs1, token,
    wq, wo, main, slabs, sems,
):
    token[...] = jnp.zeros_like(token)
    copies = []
    for s, (a, b) in enumerate(((wq_img, wo_img), (wq_txt, wo_txt), (wq_ctl, wo_ctl))):
        copies.append((
            pltpu.make_async_copy(a, wq.at[s], sems.at[s]),
            pltpu.make_async_copy(b, wo.at[s], sems.at[3 + s]),
        ))
    for s in (2, 0, 1):
        copies[s][0].start()
        copies[s][1].start()

    def stream(s, parts, at):
        count = parts[0].shape[0]
        copies[s][0].wait()
        copies[s][1].wait()
        return back(s, *parts, wq.at[s], wo.at[s], mod, xhat[at : at + count, :], rstd[at : at + count, 0:1])

    def joint(at, count):
        return [main[at : at + count, j * WIDTH : (j + 1) * WIDTH] for j in range(4)]

    head_back_main(recv, proj, gains, main)
    u, y_ctl = stream(2, [r[:, j * WIDTH : (j + 1) * WIDTH] for r in (by_z, by_y) for j in range(2)], IMG + TXT)
    slabs[:, 2 * SHARE : 3 * SHARE, :] = slab(u)
    u, y = stream(0, joint(0, IMG), 0)
    slabs[:, SHARE : 2 * SHARE, :] = slab(u)
    slabs[:, 0:SHARE, :] = slab(y + y_ctl)
    u, y = stream(1, joint(IMG, TXT), IMG)
    text = jnp.concatenate([y, u, jnp.zeros((IMG - 2 * TXT, D), F32)], 0).astype(BF16).T.astype(F32)
    for c in range(4):
        slabs[c, 3 * SHARE :, :] = pack_text(text[SHARE * c : SHARE * (c + 1)]).astype(BF16)
    tp = lax.axis_index("tp")
    mine0[...] = slabs[tp]
    mine1[...] = slabs[tp ^ 2]
    theirs0[...] = slabs[tp ^ 1]
    theirs1[...] = slabs[tp ^ 3]


def weight_kernel(
    nz0, nz1, nz2, nz3, ny0, ny1, ny2, ny3, bz0, bz1, bz2, bz3, by0, by1, by2, by3,
    after, out_z, out_y,
):
    nz, ny = (nz0, nz1, nz2, nz3), (ny0, ny1, ny2, ny3)
    bz, by = (bz0, bz1, bz2, bz3), (by0, by1, by2, by3)
    qk = dot(jnp.concatenate([r[...] for r in nz], 1), jnp.concatenate([r[...] for r in bz], 0))
    v = dot(jnp.concatenate([r[0] for r in ny], 1), jnp.concatenate([r[:, 0:WIDTH] for r in by], 0))
    o = dot(jnp.concatenate([r[1] for r in ny], 1), jnp.concatenate([r[:, WIDTH:] for r in by], 0))
    for p in range(4):
        out_z[p] = qk[PIECE * p : PIECE * (p + 1)].astype(BF16)
        out_y[p, :, 0:WIDTH] = v[PIECE * p : PIECE * (p + 1)].astype(BF16)
        out_y[p, :, WIDTH:] = o[PIECE * p : PIECE * (p + 1)].astype(BF16)


def weight_sum_kernel(terms_z, terms_y, mine, theirs):
    half = PIECE // 2
    low = lax.axis_index("w") == 0
    for j, terms in enumerate((terms_z, terms_y)):
        total = terms[0].astype(F32) + terms[1].astype(F32) + terms[2].astype(F32) + terms[3].astype(F32)
        first, second = total[0:half], total[half:]
        columns = slice(2 * WIDTH * j, 2 * WIDTH * (j + 1))
        mine[:, columns] = jnp.where(low, first, second)
        theirs[:, columns] = jnp.where(low, second, first).astype(BF16)


def weight_out_kernel(mine, other, qkv, out):
    for j in range(4):
        columns = slice(WIDTH * j, WIDTH * (j + 1))
        total = mine[:, columns] + other[:, columns].astype(F32)
        if j < 3:
            qkv[j] = total
        else:
            out[...] = total


def final_kernel(img, dy, txt, dy_txt, part0, part1, part2, y_img, d_img, d_ctl, y_txt, d_txt):
    total = part0[...].astype(F32) + part1[...].astype(F32) + part2[...].astype(F32)
    y_img[...] = (img[...].astype(F32) + total[0:SHARE]).astype(BF16)
    d_img[...] = (dy[...].astype(F32) + total[SHARE : 2 * SHARE]).astype(BF16)
    d_ctl[...] = total[2 * SHARE : 3 * SHARE].astype(BF16)
    text = jnp.concatenate([spread_text(total[3 * SHARE :]), jnp.zeros((640 - SHARE, IMG), F32)], 0).T
    y_txt[...] = (txt[...].astype(F32) + text[0:TXT, 0:SHARE]).astype(BF16)
    d_txt[...] = (dy_txt[...].astype(F32) + text[TXT : 2 * TXT, 0:SHARE]).astype(BF16)


def shifted(parts, axis):
    return [parts[0]] + [
        lax.ppermute(parts[d], axis, [(i, (i + d) % 4) for i in range(4)]) for d in (1, 2, 3)
    ]


def per_device(
    img, txt, ctl, dy_img, dy_txt, live_text_length, modulation, query_key_gains,
    w_qkv_img, wo_img, w_qkv_txt, wo_txt, w_qkv_ctl, wo_ctl,
):
    seq = ("z", "y", "w")
    seq_pos = lax.axis_index(seq)
    role = jnp.stack([(seq_pos < CTL_AT).astype(jnp.int32), live_text_length[0]])
    mod, gains = modulation, query_key_gains
    weights = (
        w_qkv_img.transpose(1, 0, 2), w_qkv_txt.transpose(1, 0, 2), w_qkv_ctl.transpose(1, 0, 2),
        wo_img, wo_txt, wo_ctl,
    )
    shape = jax.ShapeDtypeStruct
    rows = shape((ROWS, IMG), BF16)
    other_core = [(i, i ^ 1) for i in range(4)]
    other_chip = [(i, i ^ 2) for i in range(4)]

    own, token = pl.pallas_call(
        pack_kernel,
        out_shape=[rows, shape((8, 128), F32)],
        in_specs=[HBM] * 5,
        out_specs=[VMEM] * 2,
        scratch_shapes=[pltpu.VMEM((2, TXT, SHARE), BF16), pltpu.SemaphoreType.DMA((5,))],
        compiler_params=pltpu.CompilerParams(vmem_limit_bytes=63_400_000),
        name="pack",
    )(img.T, ctl.T, dy_img.T, txt, dy_txt)
    from_chip = lax.ppermute(own, "tp", other_chip)
    from_core = lax.ppermute(own, "tp", other_core)
    *loaded, token = load(weights[0:3], token)
    from_chip = ordered(from_chip, token)
    from_both = lax.ppermute(from_chip, "tp", other_core)

    send, proj, xhat, rstd, *slabs = pl.pallas_call(
        pre_kernel,
        out_shape=[
            shape((BLOCKS, CHUNK, 128), BF16),
            shape((2 * IMG + TXT, 2 * WIDTH), F32),
            shape((2 * IMG + TXT, D), F32),
            shape((2 * IMG + TXT, 128), F32),
        ] + [shape((SHARE, IMG), BF16)] * 4 + [shape((2, SHARE, IMG), BF16)] * 4,
        in_specs=[VMEM] * 12,
        out_specs=[VMEM] * 12,
        scratch_shapes=[
            pltpu.VMEM((4, ROWS, IMG), BF16),
            pltpu.VMEM((4, SHARE, IMG), BF16),
            pltpu.VMEM((4, 2, SHARE, IMG), BF16),
        ],
        compiler_params=params(33),
        name="pre",
    )(own, from_core, from_chip, from_both, mod, gains, *loaded, *weights[3:])

    recv = lax.all_to_all(send, seq, 0, 0, tiled=True)
    nz = shifted(slabs[0:4], "z")
    ny = shifted(slabs[4:8], "y")
    keys = IMAGE_KEYS + TEXT_KEYS
    dkv, odq = pl.pallas_call(
        attention_kernel,
        out_shape=[shape((keys, 128), BF16), shape((BLOCKS * CTL_Q, 128), BF16)],
        in_specs=[SMEM, VMEM, ANY],
        out_specs=[VMEM] * 2,
        scratch_shapes=[
            pltpu.VMEM((keys, 128), BF16),
            pltpu.VMEM((HEAD, keys), BF16),
            pltpu.VMEM((HEAD, keys), BF16),
            pltpu.VMEM((BLOCKS * CTL_Q, 128), BF16),
            pltpu.VMEM((keys, TQ), F32),
            pltpu.VMEM((keys, 128), F32),
        ],
        compiler_params=params(32),
        cost_estimate=pl.CostEstimate(flops=40_000_000_000, bytes_accessed=3_200_000, transcendentals=8_400_000),
        name="attention",
    )(role, recv, nz[3])
    back = pl.pallas_call(
        scatter_kernel,
        out_shape=shape((BLOCKS, CHUNK, 128), BF16),
        in_specs=[SMEM] + [VMEM] * 2 + [ANY] * 5,
        out_specs=VMEM,
        compiler_params=params(16),
        name="scatter",
    )(role, dkv, odq, *nz[1:3], *ny[1:])
    back = lax.all_to_all(back, seq, 0, 0, tiled=True)

    by_z, by_y = pl.pallas_call(
        head_back_ctl_kernel,
        out_shape=[shape((IMG, 2 * WIDTH), BF16)] * 2,
        in_specs=[VMEM] * 3,
        out_specs=[VMEM] * 2,
        compiler_params=params(16),
        name="head_back_ctl",
    )(back, proj, gains)
    blocks_z = shifted([by_z] * 4, "z")
    blocks_y = shifted([by_y] * 4, "y")
    mine0, mine1, theirs0, theirs1, token = pl.pallas_call(
        post_kernel,
        out_shape=[rows] * 4 + [shape((8, 128), F32)],
        in_specs=[VMEM] * 8 + [HBM] * 6,
        out_specs=[VMEM] * 5,
        scratch_shapes=[
            pltpu.VMEM((3, 3, D, WIDTH), BF16),
            pltpu.VMEM((3, WIDTH, D), BF16),
            pltpu.VMEM((IMG + TXT, 4 * WIDTH), BF16),
            pltpu.VMEM((4, ROWS, IMG), BF16),
            pltpu.SemaphoreType.DMA((6,)),
        ],
        compiler_params=params(54),
        cost_estimate=pl.CostEstimate(flops=14_000_000_000, bytes_accessed=30_000_000, transcendentals=0),
        name="post",
    )(back, proj, gains, by_z, by_y, xhat, rstd, mod, *weights)
    got1 = lax.ppermute(theirs1, "tp", other_core)
    got0 = lax.ppermute(theirs0, "tp", other_core)
    passed = (mine1.astype(F32) + got1.astype(F32)).astype(BF16)
    passed = lax.ppermute(passed, "tp", other_chip)

    terms_z, terms_y = pl.pallas_call(
        weight_kernel,
        out_shape=[shape((4, PIECE, 2 * WIDTH), BF16)] * 2,
        in_specs=[VMEM] * 16 + [ANY],
        out_specs=[VMEM] * 2,
        compiler_params=params(20),
        cost_estimate=pl.CostEstimate(flops=3_000_000_000, bytes_accessed=5_000_000, transcendentals=0),
        name="weight",
    )(*nz, *ny, *blocks_z, *blocks_y, token)
    terms_z = lax.all_to_all(terms_z, "y", 0, 0, tiled=True)
    terms_y = lax.all_to_all(terms_y, "z", 0, 0, tiled=True)
    mine, theirs = pl.pallas_call(
        weight_sum_kernel,
        out_shape=[shape((PIECE // 2, 4 * WIDTH), F32), shape((PIECE // 2, 4 * WIDTH), BF16)],
        in_specs=[VMEM] * 2,
        out_specs=[VMEM] * 2,
        compiler_params=params(16),
        name="weight_sum",
    )(terms_z, terms_y)
    theirs = lax.ppermute(theirs, "w", [(0, 1), (1, 0)])
    grad_qkv, grad_out = pl.pallas_call(
        weight_out_kernel,
        out_shape=[shape((3, PIECE // 2, WIDTH), F32), shape((PIECE // 2, WIDTH), F32)],
        in_specs=[VMEM] * 2,
        out_specs=[VMEM] * 2,
        compiler_params=params(16),
        name="weight_out",
    )(mine, theirs)

    y_img, d_img, d_ctl, y_txt, d_txt = pl.pallas_call(
        final_kernel,
        out_shape=[shape((SHARE, IMG), BF16)] * 3 + [shape((TXT, SHARE), BF16)] * 2,
        in_specs=[VMEM] * 7,
        out_specs=[VMEM] * 5,
        compiler_params=params(16),
        name="final",
    )(img.T, dy_img.T, txt, dy_txt, mine0, got0, passed)
    return y_img.T, y_txt, d_img.T, d_txt, d_ctl.T, grad_qkv.transpose(1, 0, 2), grad_out.T


def solution(mesh):
    fine = Mesh(mesh.devices.reshape(4, 4, 2, 4), ("z", "y", "w", "tp"))
    seq = ("z", "y", "w")
    rows = P(seq, "tp")
    qkv = P(None, None, "tp")
    out = P("tp", None)
    in_specs = (rows,) * 5 + (P(), P(), P(), qkv, out, qkv, out, qkv, out)
    out_specs = (rows,) * 5 + (P(seq, None, "tp"), P("tp", seq))
    return jax.shard_map(
        per_device, mesh=fine, in_specs=in_specs, out_specs=out_specs, check_vma=False
    )
```

time: 1750 us -> 207 us (0.12)
  waiting for transfers between devices: 906 us -> 37.9 us
  local copies, waits for them, and re-layouts: 319 us -> 14.4 us
  matrix products: 222 us -> 0 us
  blocking collectives: 207 us -> 33.5 us
  Pallas kernels: 0 us -> 74.9 us
  other arithmetic: 68.3 us -> 2.28 us
  starting transfers between devices: 0.38 us -> 42.2 us
    all_gather x2 -> x0, waiting for transfers between devices: 474 us -> none  [the longest x1 251 us: per_device(): kv_all = lax.all_gather(kv_local, 'seq', axis=0, tiled=True)]
    unnamed x5 -> x0, waiting for transfers between devices: 413 us -> none
    dot_general x56 -> x0, matrix products: 222 us -> none  [the longest x12 54.7 us: one_head(): jnp.einsum('nqk,nqd->nkd', dscore, query_head, preferred_element_type=jnp...]
    all_gather x7 -> x0, blocking collectives: 207 us -> none  [the longest x1 79.8 us: per_device(): lax.all_gather(logsumexp_rows, 'seq', axis=0, tiled=True)]
    pallas_call x0 -> x12, Pallas kernels: none -> 74.9 us  [the longest x1 27.5 us: per_device(): pl.pallas_call(attention_kernel, out_shape=[shape((keys, 128), BF16), sha...]
    reshape x2 -> x0, local copies, waits for them, and re-layouts: 70.6 us -> none  [the longest x1 35.3 us: per_device(): query_all.reshape(sequence_count, every_row, 2, heads_on_shard, HEAD_SIZE)]
    all_gather x5 -> x0, local copies, waits for them, and re-layouts: 36.7 us -> none  [the longest x1 16.9 us: per_device(): kv_all = lax.all_gather(kv_local, 'seq', axis=0, tiled=True)]
    another operation x4 -> x0, local copies, waits for them, and re-layouts: 35.9 us -> none  [the longest x1 12.4 us: per_device(): key_value_reshaped[:, :main_rows, 1]]
  transfers between devices with their start and end apart: 4 -> 22, of which waited for: 4 -> 7; matrix products, arithmetic and copies ran while one was open for 8% -> 1% of each run, Pallas kernels for 0% -> 26%
where the time goes in v1:
time: 207 us
  Pallas kernels  74.9 us (36%)
  starting transfers between devices  42.2 us (20%)
  waiting for transfers between devices  37.9 us (18%)
  blocking collectives  33.5 us (16%)
  local copies, waits for them, and re-layouts  14.4 us (7%)
  other arithmetic  2.28 us (1%)
    all_to_all x1, blocking collectives, per_device(): back = lax.all_to_all(back, seq, 0, 0, tiled=True)  33.5 us
    pallas_call x1, Pallas kernels, per_device(): pl.pallas_call(attention_kernel, out_shape=[shape((keys, 128), BF16), sha...  27.5 us
    ppermute x12, starting transfers between devices, shifted(): lax.ppermute(parts[d], axis, [(i, (i + d) % 4) for i in range(4)])  17.6 us
    ppermute x12, waiting for transfers between devices, shifted(): lax.ppermute(parts[d], axis, [(i, (i + d) % 4) for i in range(4)])  17.1 us
    pallas_call x1, Pallas kernels, per_device(): pl.pallas_call(post_kernel, out_shape=[rows] * 4 + [shape((8, 128), F32)]...  15.2 us
    unnamed x62, local copies, waits for them, and re-layouts  14.4 us
    pallas_call x1, Pallas kernels, per_device(): pl.pallas_call(pre_kernel, out_shape=[shape((BLOCKS, CHUNK, 128), BF16),...  11.8 us
    all_to_all x1, waiting for transfers between devices, per_device(): terms_z = lax.all_to_all(terms_z, 'y', 0, 0, tiled=True)  9.82 us
  transfers between devices with their start and end apart: 22, of which 7 were waited for; matrix products, arithmetic and copies ran while one was open for 1% of the time, Pallas kernels for 26%

profile of v1, /device:TPU:0, one launch (start us, length us, event | category | flops | bytes accessed | tf_op | source)
XLA Modules:
  0.0 206.8 jit_solution(9279867722328196748)
XLA Ops:
  0.6 1.9 pack.1
  2.6 3.2 %collective-permute-start.1 = (bf16[1976,128]{1,0:T(8,128)(2,1)}, bf16[1976,128]{1,0:T(8,128)(2,1)S(1)}, u32[]{:S(2)}, u32[]{:S(2)}) collective-permute-start(bf16[1976,128]{1,0:T(8,128)(2,1)} %get-tuple-element.45.in0), channel_id=1, source_target_pairs={{0,2},{1,3},{2,0},{3,1},{4,6},{5,7},{6,4},{7,5},{8,10},{9,11},{10,... | collective-permute-start | bytes 1517576 | tf_op jit(solution)/shard_map/ppermute | solution.py:475
  6.5 8.5 %load.1 = (bf16[3,2432,384]{2,1,0:T(8,128)(2,1)S(1)}, bf16[3,2432,384]{2,1,0:T(8,128)(2,1)S(1)}, bf16[3,2432,384]{2,1,0:T(8,128)(2,1)}, f32[8,128]{1,0:T(8,128)S(1)}) custom-call(f32[8,128]{1,0:T(8,128)S(1)} %copy-done.14, bf16[3,2432,384]{2,1,0:T(8,128)(2,1)} %bitcast.16, bf16[3,2432,384]{2,1,0:T(8,128)(2,1)} %bitcast.18, bf16[3,2432,384]{2,1,0:T(8,128)(2,1)} %bitcast.20), custom_call_target="tpu_custom_call" | custom-call | bytes 30000000 | tf_op jit(solution)/shard_map/load/pallas_call | solution.py:78
  15.0 2.4 %copy-done.1 = bf16[3,2432,384]{2,1,0:T(8,128)(2,1)} copy-done((bf16[3,2432,384]{2,1,0:T(8,128)(2,1)}, bf16[3,2432,384]{2,1,0:T(8,128)(2,1)S(1)}, u32[]{:S(2)}) %copy-start.1) | copy-done | bytes 5603352
  17.9 1.5 collective-permute-done.2.in3
  19.4 1.5 copy-done.4
  20.9 11.8 %pre.1 = (bf16[32,192,128]{2,1,0:T(8,128)(2,1)}, f32[272,768]{1,0:T(8,128)S(1)}, f32[272,2432]{1,0:T(8,128)S(1)}, f32[272,128]{1,0:T(8,128)S(1)}, bf16[608,128]{...) custom-call(bf16[1976,128]{1,0:T(8,128)(2,1)S(1)} %copy-done.9, ...), custom_call_target="tpu_custom_call" | custom-call | tf_op jit(solution)/shard_map/pre/pallas_call | solution.py:481
  32.7 1.5 copy-done.15
  38.4 9.5 %all-to-all-start = ((bf16[32,192,128]{2,1,0:T(8,128)(2,1)}), bf16[32,192,128]{2,1,0:T(8,128)(2,1)S(1)}, u32[]{:S(2)}, u32[]{:S(2)}) async-start(bf16[32,192,128]{2,1,0:T(8,128)(2,1)} %get-tuple-element.51), calls=%async_computation | async-start | bytes 3145728 | tf_op jit(solution)/shard_map/all_to_all | solution.py:500
  47.9 3.1 %collective-permute-start.3 = (bf16[608,128]{1,0:T(8,128)(2,1)}, bf16[608,128]{1,0:T(8,128)(2,1)S(1)}, u32[]{:S(2)}, u32[]{:S(2)}) collective-permute-start(bf16[608,128]{1,0:T(8,128)(2,1)} %get-tuple-element.52), channel_id=1, source_target_pairs={{0,96},{32,0},{64,32},{96,64},{1,97},{33,1},{65,33},{97,65},{2,98}... | collective-permute-start | bytes 466952 | tf_op jit(solution)/shard_map/ppermute | solution.py:445
  51.7 1.5 collective-permute-start.6
  53.2 2.7 %collective-permute-start.7 = (bf16[2,608,128]{2,1,0:T(8,128)(2,1)}, bf16[2,608,128]{2,1,0:T(8,128)(2,1)S(1)}, u32[]{:S(2)}, u32[]{:S(2)}) collective-permute-start(bf16[2,608,128]{2,1,0:T(8,128)(2,1)} %copy-done.19), channel_id=1, source_target_pairs={{0,16},{8,24},{16,0},{24,8},{1,17},{9,25},{17,1},{25,9},{2,18},{10... | collective-permute-start | bytes 933896 | tf_op jit(solution)/shard_map/ppermute | solution.py:445
  55.9 1.4 collective-permute-start.8
  57.3 13.0 %collective-permute-done.3.after.nz3 = bf16[608,128]{1,0:T(8,128)(2,1)S(1)} collective-permute-done((bf16[608,128]{1,0:T(8,128)(2,1)}, bf16[608,128]{1,0:T(8,128)(2,1)S(1)}, u32[]{:S(2)}, u32[]{:S(2)}) %collective-permute-start.3) | collective-permute-done | bytes 155680 | tf_op jit(solution)/shard_map/ppermute | solution.py:445
  71.0 2.7 %collective-permute-start.5 = (bf16[608,128]{1,0:T(8,128)(2,1)}, bf16[608,128]{1,0:T(8,128)(2,1)S(1)}, u32[]{:S(2)}, u32[]{:S(2)}) collective-permute-start(bf16[608,128]{1,0:T(8,128)(2,1)} %copy-done.27), channel_id=1, source_target_pairs={{0,64},{32,96},{64,0},{96,32},{1,65},{33,97},{65,1},{97,33},{2,66}... | collective-permute-start | bytes 466952 | tf_op jit(solution)/shard_map/ppermute | solution.py:445
  74.6 27.5 %attention.1 = (bf16[4608,128]{1,0:T(8,128)(2,1)S(1)}, bf16[2048,128]{1,0:T(8,128)(2,1)S(1)}) custom-call(s32[2]{0:T(128)S(1)} %pad_add_fusion.role, bf16[32,192,128]{2,1,0:T(8,128)(2,1)S(1)} %all-to-all-done.recv, bf16[608,128]{1,0:T(8,128)(2,1)S(1)} %copy-done.25), custom_call_target="tpu_custom_call" | custom-call | flops 40000000000 | bytes 3200000 | tf_op jit(solution)/shard_map/attention/pallas_call | solution.py:504
  102.9 33.5 %all_to_all.20.recv = bf16[32,192,128]{2,1,0:T(8,128)(2,1)S(1)} all-to-all(bf16[32,192,128]{2,1,0:T(8,128)(2,1)S(1)} %scatter.1), channel_id=1, replica_groups=mesh['z'=4,'y'=4,'w'=2,'tp'=4] {'z','y','w'}, dimensions={0} | all-to-all | bytes 3145728 | tf_op jit(solution)/shard_map/all_to_all | solution.py:529
  136.4 2.5 %head_back_ctl.1 = (bf16[128,768]{1,0:T(8,128)(2,1)S(1)}, bf16[128,768]{1,0:T(8,128)(2,1)S(1)}) custom-call(bf16[32,192,128]{2,1,0:T(8,128)(2,1)S(1)} %all_to_all.20.recv, f32[272,768]{1,0:T(8,128)S(1)} %get-tuple-element.60.proj, f32[3,2,64]{2,1,0:T(2,128)S(1)} %copy-done.13), custom_call_target="tpu_custom_call" | custom-call | tf_op jit(solution)/shard_map/head_back_ctl/pallas_call | solution.py:531
  139.1 2.3 %collective-permute-start.13 = (bf16[128,768]{1,0:T(8,128)(2,1)S(1)}, bf16[128,768]{1,0:T(8,128)(2,1)S(1)}, u32[]{:S(2)}, u32[]{:S(2)}) collective-permute-start(bf16[128,768]{1,0:T(8,128)(2,1)S(1)} %get-tuple-element.61.by_z.bz0), channel_id=1, source_target_pairs={{0,64},{32,96},{64,0},{96,32},{1,65},{33,97},{65,1},{97,33},{2,66}... | collective-permute-start | bytes 589832 | tf_op jit(solution)/shard_map/ppermute | solution.py:445
  141.3 1.1 collective-permute-start.14
  143.0 2.1 %collective-permute-start.16 = (bf16[128,768]{1,0:T(8,128)(2,1)S(1)}, bf16[128,768]{1,0:T(8,128)(2,1)S(1)}, u32[]{:S(2)}, u32[]{:S(2)}) collective-permute-start(bf16[128,768]{1,0:T(8,128)(2,1)S(1)} %get-tuple-element.62.by_y.by0), channel_id=1, source_target_pairs={{0,16},{8,24},{16,0},{24,8},{1,17},{9,25},{17,1},{25,9},{2,18},{10... | collective-permute-start | bytes 589832 | tf_op jit(solution)/shard_map/ppermute | solution.py:445
  145.0 4.1 %collective-permute-done.12.bz1 = bf16[128,768]{1,0:T(8,128)(2,1)S(1)} collective-permute-done((bf16[128,768]{1,0:T(8,128)(2,1)S(1)}, bf16[128,768]{1,0:T(8,128)(2,1)S(1)}, u32[]{:S(2)}, u32[]{:S(2)}) %collective-permute-start.12) | collective-permute-done | bytes 196640 | tf_op jit(solution)/shard_map/ppermute | solution.py:445
  149.2 15.2 %post.1 = (bf16[1976,128]{1,0:T(8,128)(2,1)}, bf16[1976,128]{1,0:T(8,128)(2,1)}, bf16[1976,128]{1,0:T(8,128)(2,1)}, bf16[1976,128]{1,0:T(8,128)(2,1)}, f32[8,128]{1,0:T(8,128)}) custom-call(bf16[32,192,128]{2,1,0:T(8,128)(2,1)} %copy-done, f32[272,768]{1,0:T(8,128)} %copy-done.5, f32[3,2,64]{2,1,0:T(2,128)} %gains.5, bf16[128,768]{1,0:T(8,128)(2,1)} %copy-done.20, ...), custom_call_target="tpu_custom_call" | custom-call | flops 14000000000 | bytes 30000000 | tf_op jit(solution)/shard_map/post/pallas_call | solution.py:541
  167.0 3.4 %weight.1 = (bf16[4,152,768]{2,1,0:T(8,128)(2,1)}, bf16[4,152,768]{2,1,0:T(8,128)(2,1)}) custom-call(bf16[608,128]{1,0:T(8,128)(2,1)S(1)} %get-tuple-element.74.nz0, bf16[608,128]{1,0:T(8,128)(2,1)S(1)} %collective-permute-done.4.after0.nz1, bf16[608,128]{1,0:T(8,128)(2,1)S(1)} %collective-permute-done.5.after1.nz2, bf16[608,128]{1,0:T(8,128)(2,1)S(1)} %copy-done.26, ...), custom_call_target="tpu_custom_call" | custom-call | flops 3000000000 | bytes 5000000 | tf_op jit(solution)/shard_map/weight/pallas_call | solution.py:562
  170.5 3.8 %all-to-all-start.2 = ((bf16[4,152,768]{2,1,0:T(8,128)(2,1)}), bf16[4,152,768]{2,1,0:T(8,128)(2,1)S(1)}, u32[]{:S(2)}, u32[]{:S(2)}) async-start(bf16[4,152,768]{2,1,0:T(8,128)(2,1)} %get-tuple-element.77), calls=%async_computation.2 | async-start | bytes 1867776 | tf_op jit(solution)/shard_map/all_to_all | solution.py:571
  174.7 9.8 %all-to-all-done.2.terms_z = bf16[4,152,768]{2,1,0:T(8,128)(2,1)S(1)} async-done(((bf16[4,152,768]{2,1,0:T(8,128)(2,1)}), bf16[4,152,768]{2,1,0:T(8,128)(2,1)S(1)}, u32[]{:S(2)}, u32[]{:S(2)}) %all-to-all-start.2) | async-done | bytes 933920 | tf_op jit(solution)/shard_map/all_to_all | solution.py:571
  184.5 3.5 %all-to-all-start.3 = ((bf16[4,152,768]{2,1,0:T(8,128)(2,1)}), bf16[4,152,768]{2,1,0:T(8,128)(2,1)S(1)}, u32[]{:S(2)}, u32[]{:S(2)}) async-start(bf16[4,152,768]{2,1,0:T(8,128)(2,1)} %get-tuple-element.78), calls=%async_computation.3 | async-start | bytes 1867776 | tf_op jit(solution)/shard_map/all_to_all | solution.py:572
  188.1 2.2 %add_convert_fusion = bf16[1976,128]{1,0:T(8,128)(2,1)} fusion(bf16[1976,128]{1,0:T(8,128)(2,1)} %collective-permute-done.10, bf16[1976,128]{1,0:T(8,128)(2,1)} %get-tuple-element.67), kind=kLoop, calls=%fused_computation | loop fusion | flops 1011712 | bytes 1517568 | tf_op jit(solution)/shard_map/convert_element_type | solution.py:559
  190.3 2.7 %collective-permute-start.11 = (bf16[1976,128]{1,0:T(8,128)(2,1)}, bf16[1976,128]{1,0:T(8,128)(2,1)}, u32[]{:S(2)}, u32[]{:S(2)}) collective-permute-start(bf16[1976,128]{1,0:T(8,128)(2,1)} %add_convert_fusion), channel_id=1, source_target_pairs={{0,2},{1,3},{2,0},{3,1},{4,6},{5,7},{6,4},{7,5},{8,10},{9,11},{10,... | collective-permute-start | bytes 1517576 | tf_op jit(solution)/shard_map/ppermute | solution.py:560
  193.1 5.3 %all-to-all-done.3.terms_y = bf16[4,152,768]{2,1,0:T(8,128)(2,1)S(1)} async-done(((bf16[4,152,768]{2,1,0:T(8,128)(2,1)}), bf16[4,152,768]{2,1,0:T(8,128)(2,1)S(1)}, u32[]{:S(2)}, u32[]{:S(2)}) %all-to-all-start.3) | async-done | bytes 933920 | tf_op jit(solution)/shard_map/all_to_all | solution.py:572
  199.7 4.0 %collective-permute-done.11.part2 = bf16[1976,128]{1,0:T(8,128)(2,1)} collective-permute-done((bf16[1976,128]{1,0:T(8,128)(2,1)}, bf16[1976,128]{1,0:T(8,128)(2,1)}, u32[]{:S(2)}, u32[]{:S(2)}) %collective-permute-start.11) | collective-permute-done | bytes 505888 | tf_op jit(solution)/shard_map/ppermute | solution.py:560
  203.8 2.2 %final.1 = (bf16[608,128]{1,0:T(8,128)(2,1)}, bf16[608,128]{1,0:T(8,128)(2,1)}, bf16[608,128]{1,0:T(8,128)(2,1)}, bf16[16,608]{1,0:T(8,128)(2,1)}, bf16[16,608]{1,0:T(8,128)(2,1)}) custom-call(bf16[608,128]{1,0:T(8,128)(2,1)S(1)} %bitcast.13, bf16[608,128]{1,0:T(8,128)(2,1)S(1)} %bitcast.15, bf16[16,608]{1,0:T(8,128)(2,1)S(1)} %copy-done.11, ...), custom_call_target="tpu_custom_call" | custom-call | tf_op jit(solution)/shard_map/final/pallas_call | solution.py:591
  (89 shorter events, 13.8 us)
Async XLA Ops:
  2.6 14.9 %collective-permute-start.1 = (bf16[1976,128]{1,0:T(8,128)(2,1)}, bf16[1976,128]{1,0:T(8,128)(2,1)S(1)}, u32[]{:S(2)}, u32[]{:S(2)}) collective-permute-start(bf16[1976,128]{1,0:T(8,128)(2,1)} %get-tuple-element.45.in0), channel_id=1, source_target_pairs={{0,2},{1,3},{2,0},{3,1},{4,6},{5,7},{6,4},{7,5},{8,10},{9,11},{10,... | collective-permute-start | bytes 1517576 | tf_op jit(solution)/shard_map/ppermute | solution.py:475
  5.8 12.1 %collective-permute-start = (bf16[1976,128]{1,0:T(8,128)(2,1)}, bf16[1976,128]{1,0:T(8,128)(2,1)S(1)}, u32[]{:S(2)}, u32[]{:S(2)}) collective-permute-start(bf16[1976,128]{1,0:T(8,128)(2,1)} %get-tuple-element.45.in0), channel_id=1, source_target_pairs={{0,1},{1,0},{2,3},{3,2},{4,5},{5,4},{6,7},{7,6},{8,9},{9,8},{10,11... | collective-permute-start | bytes 1517576 | tf_op jit(solution)/shard_map/ppermute | solution.py:476
  6.5 12.9 %copy-start.10 = (f32[3,3,2432]{2,1,0:T(4,128)S(1)}, f32[3,3,2432]{2,1,0:T(4,128)}, u32[]{:S(2)}) copy-start(f32[3,3,2432]{2,1,0:T(4,128)} %mod.3) | copy-start | bytes 262660
  6.5 12.9 %copy-start.13 = (f32[3,2,64]{2,1,0:T(2,128)S(1)}, f32[3,2,64]{2,1,0:T(2,128)}, u32[]{:S(2)}) copy-start(f32[3,2,64]{2,1,0:T(2,128)} %gains.5) | copy-start | bytes 4612
  17.5 1.9 collective-permute-start.2
  38.4 98.1 %copy-start.5 = (f32[272,768]{1,0:T(8,128)}, f32[272,768]{1,0:T(8,128)S(1)}, u32[]{:S(2)}) copy-start(f32[272,768]{1,0:T(8,128)S(1)} %get-tuple-element.60.proj) | copy-start | bytes 2506756
  38.4 35.4 %all-to-all-start = ((bf16[32,192,128]{2,1,0:T(8,128)(2,1)}), bf16[32,192,128]{2,1,0:T(8,128)(2,1)S(1)}, u32[]{:S(2)}, u32[]{:S(2)}) async-start(bf16[32,192,128]{2,1,0:T(8,128)(2,1)} %get-tuple-element.51), calls=%async_computation | async-start | bytes 3145728 | tf_op jit(solution)/shard_map/all_to_all | solution.py:500
  47.9 22.5 %collective-permute-start.3 = (bf16[608,128]{1,0:T(8,128)(2,1)}, bf16[608,128]{1,0:T(8,128)(2,1)S(1)}, u32[]{:S(2)}, u32[]{:S(2)}) collective-permute-start(bf16[608,128]{1,0:T(8,128)(2,1)} %get-tuple-element.52), channel_id=1, source_target_pairs={{0,96},{32,0},{64,32},{96,64},{1,97},{33,1},{65,33},{97,65},{2,98}... | collective-permute-start | bytes 466952 | tf_op jit(solution)/shard_map/ppermute | solution.py:445
  51.7 50.5 %collective-permute-start.6 = (bf16[2,608,128]{2,1,0:T(8,128)(2,1)}, bf16[2,608,128]{2,1,0:T(8,128)(2,1)S(1)}, u32[]{:S(2)}, u32[]{:S(2)}) collective-permute-start(bf16[2,608,128]{2,1,0:T(8,128)(2,1)} %get-tuple-element.57), channel_id=1, source_target_pairs={{0,8},{8,16},{16,24},{24,0},{1,9},{9,17},{17,25},{25,1},{2,10},{10... | collective-permute-start | bytes 933896 | tf_op jit(solution)/shard_map/ppermute | solution.py:445
  53.2 49.1 %collective-permute-start.7 = (bf16[2,608,128]{2,1,0:T(8,128)(2,1)}, bf16[2,608,128]{2,1,0:T(8,128)(2,1)S(1)}, u32[]{:S(2)}, u32[]{:S(2)}) collective-permute-start(bf16[2,608,128]{2,1,0:T(8,128)(2,1)} %copy-done.19), channel_id=1, source_target_pairs={{0,16},{8,24},{16,0},{24,8},{1,17},{9,25},{17,1},{25,9},{2,18},{10... | collective-permute-start | bytes 933896 | tf_op jit(solution)/shard_map/ppermute | solution.py:445
  55.9 46.4 %collective-permute-start.8 = (bf16[2,608,128]{2,1,0:T(8,128)(2,1)}, bf16[2,608,128]{2,1,0:T(8,128)(2,1)}, u32[]{:S(2)}, u32[]{:S(2)}) collective-permute-start(bf16[2,608,128]{2,1,0:T(8,128)(2,1)} %copy-done.18), channel_id=1, source_target_pairs={{0,24},{8,0},{16,8},{24,16},{1,25},{9,1},{17,9},{25,17},{2,26},{10... | collective-permute-start | bytes 933896 | tf_op jit(solution)/shard_map/ppermute | solution.py:445
  57.3 44.9 %collective-permute-start.4 = (bf16[608,128]{1,0:T(8,128)(2,1)}, bf16[608,128]{1,0:T(8,128)(2,1)S(1)}, u32[]{:S(2)}, u32[]{:S(2)}) collective-permute-start(bf16[608,128]{1,0:T(8,128)(2,1)} %copy-done.28), channel_id=1, source_target_pairs={{0,32},{32,64},{64,96},{96,0},{1,33},{33,65},{65,97},{97,1},{2,34}... | collective-permute-start | bytes 466952 | tf_op jit(solution)/shard_map/ppermute | solution.py:445
  71.0 31.2 %collective-permute-start.5 = (bf16[608,128]{1,0:T(8,128)(2,1)}, bf16[608,128]{1,0:T(8,128)(2,1)S(1)}, u32[]{:S(2)}, u32[]{:S(2)}) collective-permute-start(bf16[608,128]{1,0:T(8,128)(2,1)} %copy-done.27), channel_id=1, source_target_pairs={{0,64},{32,96},{64,0},{96,32},{1,65},{33,97},{65,1},{97,33},{2,66}... | collective-permute-start | bytes 466952 | tf_op jit(solution)/shard_map/ppermute | solution.py:445
  139.0 10.1 %collective-permute-start.12 = (bf16[128,768]{1,0:T(8,128)(2,1)S(1)}, bf16[128,768]{1,0:T(8,128)(2,1)S(1)}, u32[]{:S(2)}, u32[]{:S(2)}) collective-permute-start(bf16[128,768]{1,0:T(8,128)(2,1)S(1)} %get-tuple-element.61.by_z.bz0), channel_id=1, source_target_pairs={{0,32},{32,64},{64,96},{96,0},{1,33},{33,65},{65,97},{97,1},{2,34}... | collective-permute-start | bytes 589832 | tf_op jit(solution)/shard_map/ppermute | solution.py:445
  139.1 25.4 %collective-permute-start.13 = (bf16[128,768]{1,0:T(8,128)(2,1)S(1)}, bf16[128,768]{1,0:T(8,128)(2,1)S(1)}, u32[]{:S(2)}, u32[]{:S(2)}) collective-permute-start(bf16[128,768]{1,0:T(8,128)(2,1)S(1)} %get-tuple-element.61.by_z.bz0), channel_id=1, source_target_pairs={{0,64},{32,96},{64,0},{96,32},{1,65},{33,97},{65,1},{97,33},{2,66}... | collective-permute-start | bytes 589832 | tf_op jit(solution)/shard_map/ppermute | solution.py:445
  141.3 23.1 %collective-permute-start.14 = (bf16[128,768]{1,0:T(8,128)(2,1)S(1)}, bf16[128,768]{1,0:T(8,128)(2,1)S(1)}, u32[]{:S(2)}, u32[]{:S(2)}) collective-permute-start(bf16[128,768]{1,0:T(8,128)(2,1)S(1)} %get-tuple-element.61.by_z.bz0), channel_id=1, source_target_pairs={{0,96},{32,0},{64,32},{96,64},{1,97},{33,1},{65,33},{97,65},{2,98}... | collective-permute-start | bytes 589832 | tf_op jit(solution)/shard_map/ppermute | solution.py:445
  142.5 22.0 %collective-permute-start.15 = (bf16[128,768]{1,0:T(8,128)(2,1)S(1)}, bf16[128,768]{1,0:T(8,128)(2,1)S(1)}, u32[]{:S(2)}, u32[]{:S(2)}) collective-permute-start(bf16[128,768]{1,0:T(8,128)(2,1)S(1)} %get-tuple-element.62.by_y.by0), channel_id=1, source_target_pairs={{0,8},{8,16},{16,24},{24,0},{1,9},{9,17},{17,25},{25,1},{2,10},{10... | collective-permute-start | bytes 589832 | tf_op jit(solution)/shard_map/ppermute | solution.py:445
  143.0 21.5 %collective-permute-start.16 = (bf16[128,768]{1,0:T(8,128)(2,1)S(1)}, bf16[128,768]{1,0:T(8,128)(2,1)S(1)}, u32[]{:S(2)}, u32[]{:S(2)}) collective-permute-start(bf16[128,768]{1,0:T(8,128)(2,1)S(1)} %get-tuple-element.62.by_y.by0), channel_id=1, source_target_pairs={{0,16},{8,24},{16,0},{24,8},{1,17},{9,25},{17,1},{25,9},{2,18},{10... | collective-permute-start | bytes 589832 | tf_op jit(solution)/shard_map/ppermute | solution.py:445
  149.1 15.3 %collective-permute-start.17 = (bf16[128,768]{1,0:T(8,128)(2,1)S(1)}, bf16[128,768]{1,0:T(8,128)(2,1)S(1)}, u32[]{:S(2)}, u32[]{:S(2)}) collective-permute-start(bf16[128,768]{1,0:T(8,128)(2,1)S(1)} %get-tuple-element.62.by_y.by0), channel_id=1, source_target_pairs={{0,24},{8,0},{16,8},{24,16},{1,25},{9,1},{17,9},{25,17},{2,26},{10... | collective-permute-start | bytes 589832 | tf_op jit(solution)/shard_map/ppermute | solution.py:445
  149.2 15.3 %copy-start.17 = (bf16[2,608,128]{2,1,0:T(8,128)(2,1)S(1)}, bf16[2,608,128]{2,1,0:T(8,128)(2,1)}, u32[]{:S(2)}) copy-start(bf16[2,608,128]{2,1,0:T(8,128)(2,1)} %copy-done.16) | copy-start | bytes 933892
  149.2 15.3 %copy-start.26 = (bf16[608,128]{1,0:T(8,128)(2,1)S(1)}, bf16[608,128]{1,0:T(8,128)(2,1)}, u32[]{:S(2)}) copy-start(bf16[608,128]{1,0:T(8,128)(2,1)} %copy-done.24) | copy-start | bytes 466948
  170.5 14.1 %all-to-all-start.2 = ((bf16[4,152,768]{2,1,0:T(8,128)(2,1)}), bf16[4,152,768]{2,1,0:T(8,128)(2,1)S(1)}, u32[]{:S(2)}, u32[]{:S(2)}) async-start(bf16[4,152,768]{2,1,0:T(8,128)(2,1)} %get-tuple-element.77), calls=%async_computation.2 | async-start | bytes 1867776 | tf_op jit(solution)/shard_map/all_to_all | solution.py:571
  174.2 13.9 %collective-permute-start.10 = (bf16[1976,128]{1,0:T(8,128)(2,1)}, bf16[1976,128]{1,0:T(8,128)(2,1)}, u32[]{:S(2)}, u32[]{:S(2)}) collective-permute-start(bf16[1976,128]{1,0:T(8,128)(2,1)} %get-tuple-element.68), channel_id=1, source_target_pairs={{0,1},{1,0},{2,3},{3,2},{4,5},{5,4},{6,7},{7,6},{8,9},{9,8},{10,11... | collective-permute-start | bytes 1517576 | tf_op jit(solution)/shard_map/ppermute | solution.py:557
  174.2 25.5 %collective-permute-start.9 = (bf16[1976,128]{1,0:T(8,128)(2,1)}, bf16[1976,128]{1,0:T(8,128)(2,1)S(1)}, u32[]{:S(2)}, u32[]{:S(2)}) collective-permute-start(bf16[1976,128]{1,0:T(8,128)(2,1)} %get-tuple-element.66), channel_id=1, source_target_pairs={{0,1},{1,0},{2,3},{3,2},{4,5},{5,4},{6,7},{7,6},{8,9},{9,8},{10,11... | collective-permute-start | bytes 1517576 | tf_op jit(solution)/shard_map/ppermute | solution.py:558
  184.5 13.8 %all-to-all-start.3 = ((bf16[4,152,768]{2,1,0:T(8,128)(2,1)}), bf16[4,152,768]{2,1,0:T(8,128)(2,1)S(1)}, u32[]{:S(2)}, u32[]{:S(2)}) async-start(bf16[4,152,768]{2,1,0:T(8,128)(2,1)} %get-tuple-element.78), calls=%async_computation.3 | async-start | bytes 1867776 | tf_op jit(solution)/shard_map/all_to_all | solution.py:572
  188.1 15.7 %copy-start.6 = (bf16[128,608]{0,1:T(8,128)(2,1)S(1)}, bf16[128,608]{0,1:T(8,128)(2,1)}, u32[]{:S(2)}) copy-start(bf16[128,608]{0,1:T(8,128)(2,1)} %param.14) | copy-start | bytes 466948
  188.1 15.7 %copy-start.7 = (bf16[128,608]{0,1:T(8,128)(2,1)S(1)}, bf16[128,608]{0,1:T(8,128)(2,1)}, u32[]{:S(2)}) copy-start(bf16[128,608]{0,1:T(8,128)(2,1)} %param.17) | copy-start | bytes 466948
  188.1 15.7 %copy-start.8 = (bf16[1976,128]{1,0:T(8,128)(2,1)S(1)}, bf16[1976,128]{1,0:T(8,128)(2,1)}, u32[]{:S(2)}) copy-start(bf16[1976,128]{1,0:T(8,128)(2,1)} %get-tuple-element.65.part0) | copy-start | bytes 1517572
  188.1 15.7 %copy-start.11 = (bf16[16,608]{1,0:T(8,128)(2,1)S(1)}, bf16[16,608]{1,0:T(8,128)(2,1)}, u32[]{:S(2)}) copy-start(bf16[16,608]{1,0:T(8,128)(2,1)} %txt.3) | copy-start | bytes 58372
  188.1 15.7 %copy-start.12 = (bf16[16,608]{1,0:T(8,128)(2,1)S(1)}, bf16[16,608]{1,0:T(8,128)(2,1)}, u32[]{:S(2)}) copy-start(bf16[16,608]{1,0:T(8,128)(2,1)} %dy_txt.3) | copy-start | bytes 58372
  190.3 13.4 %collective-permute-start.11 = (bf16[1976,128]{1,0:T(8,128)(2,1)}, bf16[1976,128]{1,0:T(8,128)(2,1)}, u32[]{:S(2)}, u32[]{:S(2)}) collective-permute-start(bf16[1976,128]{1,0:T(8,128)(2,1)} %add_convert_fusion), channel_id=1, source_target_pairs={{0,2},{1,3},{2,0},{3,1},{4,6},{5,7},{6,4},{7,5},{8,10},{9,11},{10,... | collective-permute-start | bytes 1517576 | tf_op jit(solution)/shard_map/ppermute | solution.py:560
  198.7 7.3 %collective-permute-start.18 = (bf16[76,1536]{1,0:T(8,128)(2,1)S(1)}, bf16[76,1536]{1,0:T(8,128)(2,1)S(1)}, u32[]{:S(2)}, u32[]{:S(2)}) collective-permute-start(bf16[76,1536]{1,0:T(8,128)(2,1)S(1)} %get-tuple-element.80), channel_id=1, source_target_pairs={{0,4},{4,0},{1,5},{5,1},{2,6},{6,2},{3,7},{7,3},{8,12},{12,8},{9,1... | collective-permute-start | bytes 700424 | tf_op jit(solution)/shard_map/ppermute | solution.py:581
  (21 other events, 86.4 us)

commit v2 on v1

--- a/solution.py
+++ b/solution.py
@@ -64,47 +64,17 @@
     return pieces[0] + sum(pltpu.roll(pieces[a], 32 * a, 1) for a in (1, 2, 3))
 
 
-def load_kernel(after, *refs):
-    sources, targets, token, sems = refs[0:3], refs[3:6], refs[6], refs[7]
-    token[...] = jnp.zeros_like(token)
-    copies = [pltpu.make_async_copy(a, b, sems.at[i]) for i, (a, b) in enumerate(zip(sources, targets))]
-    for copy in copies:
-        copy.start()
-    for copy in copies:
-        copy.wait()
-
-
-def load(weights, after):
-    return pl.pallas_call(
-        load_kernel,
-        out_shape=[jax.ShapeDtypeStruct(w.shape, w.dtype) for w in weights] + [jax.ShapeDtypeStruct((8, 128), F32)],
-        in_specs=[ANY] + [HBM] * 3,
-        out_specs=[VMEM] * 4,
-        scratch_shapes=[pltpu.SemaphoreType.DMA((3,))],
-        compiler_params=params(40),
-        cost_estimate=pl.CostEstimate(flops=0, bytes_accessed=30_000_000, transcendentals=0),
-        name="load",
-    )(after, *weights)
-
-
-def order_kernel(x, after, out):
-    pass
-
-
-def ordered(x, after):
-    return pl.pallas_call(
-        order_kernel,
-        out_shape=jax.ShapeDtypeStruct(x.shape, x.dtype),
-        in_specs=[ANY] * 2,
-        out_specs=ANY,
-        input_output_aliases={0: 0},
-        compiler_params=params(1),
-        name="order",
-    )(x, after)
-
-
-def pack_kernel(img, ctl, dy, txt, dy_txt, out, token, text_rows, sems):
-    token[...] = jnp.zeros_like(token)
+def weight_copies(sources, wq, wo, sems):
+    return [
+        (
+            pltpu.make_async_copy(sources[s], wq.at[s], sems.at[s]),
+            pltpu.make_async_copy(sources[3 + s], wo.at[s], sems.at[3 + s]),
+        )
+        for s in range(3)
+    ]
+
+
+def pack_kernel(img, ctl, dy, txt, dy_txt, out, text_rows, sems):
     copies = [
         pltpu.make_async_copy(part, text_rows.at[i], sems.at[3 + i]) for i, part in enumerate((txt, dy_txt))
     ] + [
@@ -126,15 +96,18 @@
 def pre_kernel(
     in0, in1, in2, in3, mod, gains, wq_img, wq_txt, wq_ctl, wo_img, wo_txt, wo_ctl,
     send, proj, xhat, rstd, nz0, nz1, nz2, nz3, ny0, ny1, ny2, ny3,
-    gat, nz, ny,
+    wq, wo, gat, nz, ny, sems,
 ):
+    copies = weight_copies((wq_img, wq_txt, wq_ctl, wo_img, wo_txt, wo_ctl), wq, wo, sems)
+    copies[0][0].start()
+
     for i, part in enumerate((in0, in1, in2, in3)):
         gat[lax.axis_index("tp") ^ i] = part[...]
 
     def rows(slab):
         return gat[:, SHARE * slab : SHARE * (slab + 1), :].reshape(D, IMG).T.astype(F32)
 
-    def stream(s, x, e, at):
+    def stream(s, x, e, at, later):
         count = x.shape[0]
         centered = x - jnp.mean(x, axis=-1, keepdims=True)
         inverse = lax.rsqrt(jnp.mean(centered * centered, axis=-1, keepdims=True) + EPS)
@@ -142,13 +115,17 @@
         xhat[at : at + count, :] = standard
         rstd[at : at + count, :] = jnp.broadcast_to(inverse, (count, 128))
         n = (standard * (1.0 + mod[s, 1:2, :]) + mod[s, 0:1, :]).astype(BF16)
-        wq, wo = ((wq_img, wo_img), (wq_txt, wo_txt), (wq_ctl, wo_ctl))[s]
-        pq = dot(n, wq[0])
-        pk = dot(n, wq[1])
-        pv = dot(n, wq[2])
+        copies[s][0].wait()
+        copies[s][1].start()
+        if later is not None:
+            copies[later][0].start()
+        pq = dot(n, wq[s, 0])
+        pk = dot(n, wq[s, 1])
+        pv = dot(n, wq[s, 2])
         proj[at : at + count, 0:WIDTH] = pq
         proj[at : at + count, WIDTH : 2 * WIDTH] = pk
-        g = dot_nt(e, wo[...])
+        copies[s][1].wait()
+        g = dot_nt(e, wo[s])
         kv, qg = [], []
         for h in range(HEADS):
             q_h, k_h = head(pq, h), head(pk, h)
@@ -161,26 +138,26 @@
     dy = rows(2)
     text = jnp.concatenate([spread_text(gat[c, 3 * SHARE :, :].astype(F32)) for c in range(4)], 0).astype(BF16).T.astype(F32)
     e_img = (mod[0, 2:3, :] * dy).astype(BF16)
-    n, kv, qg = stream(0, rows(0), e_img, 0)
+    n, kv, qg = stream(0, rows(0), e_img, 0, 2)
     for h in range(HEADS):
         for t in range(MAIN_PARTS):
             to = MAIN_PARTS * h + t
             send[to, 0:IMG, :] = kv[h]
             last = min(IMG, MAIN_Q * (t + 1))
             send[to, IMG + TXT : IMG + TXT + last - MAIN_Q * t, :] = qg[h][MAIN_Q * t : last]
-    e_txt = (mod[1, 2:3, :] * text[TXT : 2 * TXT]).astype(BF16)
-    n, kv, qg = stream(1, text[0:TXT], e_txt, IMG)
-    for h in range(HEADS):
-        for t in range(MAIN_PARTS):
-            send[MAIN_PARTS * h + t, IMG : IMG + TXT, :] = kv[h]
-        send[MAIN_PARTS * h + 2, CHUNK - TXT : CHUNK, :] = qg[h]
     e_ctl = mod[2, 2:3, :] * dy
-    n, kv, qg = stream(2, rows(1), e_ctl.astype(BF16), IMG + TXT)
+    n, kv, qg = stream(2, rows(1), e_ctl.astype(BF16), IMG + TXT, 1)
     for h in range(HEADS):
         for u in range(CTL_PARTS):
             to = CTL_AT + CTL_PARTS * h + u
             send[to, 0:IMG, :] = kv[h]
             send[to, IMG:CHUNK, :] = qg[h][CTL_Q * u : CTL_Q * (u + 1)]
+    e_txt = (mod[1, 2:3, :] * text[TXT : 2 * TXT]).astype(BF16)
+    unused, kv, qg = stream(1, text[0:TXT], e_txt, IMG, None)
+    for h in range(HEADS):
+        for t in range(MAIN_PARTS):
+            send[MAIN_PARTS * h + t, IMG : IMG + TXT, :] = kv[h]
+        send[MAIN_PARTS * h + 2, CHUNK - TXT : CHUNK, :] = qg[h]
     for to in range(CTL_AT + CTL_PARTS * HEADS, BLOCKS):
         send[to] = jnp.zeros((CHUNK, 128), BF16)
     n_t, e_t = n.T, e_ctl.astype(BF16).T
@@ -248,7 +225,7 @@
         state = (jnp.zeros((8, TQ), F32), jnp.zeros((HEAD, TQ), F32))
         state = lax.fori_loop(
             0, IMAGE_KEYS // TK, lambda j, c: forward(pl.multiple_of(j * TK, TK), c, False), state,
-            unroll=2,
+            unroll=4,
         )
         total, o_t = lax.fori_loop(0, is_main, lambda j, c: forward(IMAGE_KEYS, c, True), state)
         inverse = 1.0 / jnp.sum(total, axis=0, keepdims=True)
@@ -263,7 +240,7 @@
 
         dq_t = jnp.zeros((HEAD, TQ), F32)
         dq_t = lax.fori_loop(
-            0, IMAGE_KEYS // TK, lambda j, c: backward(pl.multiple_of(j * TK, TK), c), dq_t, unroll=2
+            0, IMAGE_KEYS // TK, lambda j, c: backward(pl.multiple_of(j * TK, TK), c), dq_t, unroll=4
         )
         dq_t = lax.fori_loop(0, is_main, lambda j, c: backward(IMAGE_KEYS, c), dq_t)
         odq[pl.ds(q_at, TQ), :] = jnp.concatenate([o_t, dq_t * 0.125], 0).astype(BF16).T
@@ -354,50 +331,46 @@
 
 def post_kernel(
     recv, proj, gains, by_z, by_y, xhat, rstd, mod, wq_img, wq_txt, wq_ctl, wo_img, wo_txt, wo_ctl,
-    mine0, mine1, theirs0, theirs1, token,
-    wq, wo, main, slabs, sems,
+    slabs,
+    wq, wo, main, sems,
 ):
-    token[...] = jnp.zeros_like(token)
-    copies = []
-    for s, (a, b) in enumerate(((wq_img, wo_img), (wq_txt, wo_txt), (wq_ctl, wo_ctl))):
-        copies.append((
-            pltpu.make_async_copy(a, wq.at[s], sems.at[s]),
-            pltpu.make_async_copy(b, wo.at[s], sems.at[3 + s]),
-        ))
-    for s in (2, 0, 1):
-        copies[s][0].start()
-        copies[s][1].start()
-
-    def stream(s, parts, at):
+    copies = weight_copies((wq_img, wq_txt, wq_ctl, wo_img, wo_txt, wo_ctl), wq, wo, sems)
+    for copy in (copies[2][0], copies[2][1], copies[0][0]):
+        copy.start()
+
+    def stream(s, parts, at, later):
         count = parts[0].shape[0]
         copies[s][0].wait()
         copies[s][1].wait()
+        for copy in later:
+            copy.start()
         return back(s, *parts, wq.at[s], wo.at[s], mod, xhat[at : at + count, :], rstd[at : at + count, 0:1])
 
     def joint(at, count):
         return [main[at : at + count, j * WIDTH : (j + 1) * WIDTH] for j in range(4)]
 
     head_back_main(recv, proj, gains, main)
-    u, y_ctl = stream(2, [r[:, j * WIDTH : (j + 1) * WIDTH] for r in (by_z, by_y) for j in range(2)], IMG + TXT)
+    u, y_ctl = stream(2, [r[:, j * WIDTH : (j + 1) * WIDTH] for r in (by_z, by_y) for j in range(2)], IMG + TXT, (copies[0][1], copies[1][0]))
     slabs[:, 2 * SHARE : 3 * SHARE, :] = slab(u)
-    u, y = stream(0, joint(0, IMG), 0)
+    u, y = stream(0, joint(0, IMG), 0, (copies[1][1],))
     slabs[:, SHARE : 2 * SHARE, :] = slab(u)
     slabs[:, 0:SHARE, :] = slab(y + y_ctl)
-    u, y = stream(1, joint(IMG, TXT), IMG)
+    u, y = stream(1, joint(IMG, TXT), IMG, ())
     text = jnp.concatenate([y, u, jnp.zeros((IMG - 2 * TXT, D), F32)], 0).astype(BF16).T.astype(F32)
     for c in range(4):
         slabs[c, 3 * SHARE :, :] = pack_text(text[SHARE * c : SHARE * (c + 1)]).astype(BF16)
+
+
+def weight_kernel(
+    nz0, nz1, nz2, nz3, ny0, ny1, ny2, ny3, bz0, bz1, bz2, bz3, by0, by1, by2, by3,
+    slabs, out_z, out_y0, out_y1, out_y2, out_y3, mine0, mine1, theirs0, theirs1,
+    chunks,
+):
     tp = lax.axis_index("tp")
     mine0[...] = slabs[tp]
     mine1[...] = slabs[tp ^ 2]
     theirs0[...] = slabs[tp ^ 1]
     theirs1[...] = slabs[tp ^ 3]
-
-
-def weight_kernel(
-    nz0, nz1, nz2, nz3, ny0, ny1, ny2, ny3, bz0, bz1, bz2, bz3, by0, by1, by2, by3,
-    after, out_z, out_y,
-):
     nz, ny = (nz0, nz1, nz2, nz3), (ny0, ny1, ny2, ny3)
     bz, by = (bz0, bz1, bz2, bz3), (by0, by1, by2, by3)
     qk = dot(jnp.concatenate([r[...] for r in nz], 1), jnp.concatenate([r[...] for r in bz], 0))
@@ -405,15 +378,17 @@
     o = dot(jnp.concatenate([r[1] for r in ny], 1), jnp.concatenate([r[:, WIDTH:] for r in by], 0))
     for p in range(4):
         out_z[p] = qk[PIECE * p : PIECE * (p + 1)].astype(BF16)
-        out_y[p, :, 0:WIDTH] = v[PIECE * p : PIECE * (p + 1)].astype(BF16)
-        out_y[p, :, WIDTH:] = o[PIECE * p : PIECE * (p + 1)].astype(BF16)
-
-
-def weight_sum_kernel(terms_z, terms_y, mine, theirs):
+        chunks[p, :, 0:WIDTH] = v[PIECE * p : PIECE * (p + 1)].astype(BF16)
+        chunks[p, :, WIDTH:] = o[PIECE * p : PIECE * (p + 1)].astype(BF16)
+    for d, out in enumerate((out_y0, out_y1, out_y2, out_y3)):
+        out[...] = chunks[lax.rem(lax.axis_index("z") + d, 4)]
+
+
+def weight_sum_kernel(terms_z, y0, y1, y2, y3, mine, theirs):
     half = PIECE // 2
     low = lax.axis_index("w") == 0
-    for j, terms in enumerate((terms_z, terms_y)):
-        total = terms[0].astype(F32) + terms[1].astype(F32) + terms[2].astype(F32) + terms[3].astype(F32)
+    for j, terms in enumerate(([terms_z[p] for p in range(4)], [y0[...], y1[...], y2[...], y3[...]])):
+        total = sum(term.astype(F32) for term in terms)
         first, second = total[0:half], total[half:]
         columns = slice(2 * WIDTH * j, 2 * WIDTH * (j + 1))
         mine[:, columns] = jnp.where(low, first, second)
@@ -463,19 +438,17 @@
     other_core = [(i, i ^ 1) for i in range(4)]
     other_chip = [(i, i ^ 2) for i in range(4)]
 
-    own, token = pl.pallas_call(
+    own = pl.pallas_call(
         pack_kernel,
-        out_shape=[rows, shape((8, 128), F32)],
+        out_shape=rows,
         in_specs=[HBM] * 5,
-        out_specs=[VMEM] * 2,
+        out_specs=VMEM,
         scratch_shapes=[pltpu.VMEM((2, TXT, SHARE), BF16), pltpu.SemaphoreType.DMA((5,))],
         compiler_params=pltpu.CompilerParams(vmem_limit_bytes=63_400_000),
         name="pack",
     )(img.T, ctl.T, dy_img.T, txt, dy_txt)
     from_chip = lax.ppermute(own, "tp", other_chip)
     from_core = lax.ppermute(own, "tp", other_core)
-    *loaded, token = load(weights[0:3], token)
-    from_chip = ordered(from_chip, token)
     from_both = lax.ppermute(from_chip, "tp", other_core)
 
     send, proj, xhat, rstd, *slabs = pl.pallas_call(
@@ -486,16 +459,19 @@
             shape((2 * IMG + TXT, D), F32),
             shape((2 * IMG + TXT, 128), F32),
         ] + [shape((SHARE, IMG), BF16)] * 4 + [shape((2, SHARE, IMG), BF16)] * 4,
-        in_specs=[VMEM] * 12,
+        in_specs=[VMEM] * 6 + [HBM] * 6,
         out_specs=[VMEM] * 12,
         scratch_shapes=[
+            pltpu.VMEM((3, 3, D, WIDTH), BF16),
+            pltpu.VMEM((3, WIDTH, D), BF16),
             pltpu.VMEM((4, ROWS, IMG), BF16),
             pltpu.VMEM((4, SHARE, IMG), BF16),
             pltpu.VMEM((4, 2, SHARE, IMG), BF16),
+            pltpu.SemaphoreType.DMA((6,)),
         ],
-        compiler_params=params(33),
+        compiler_params=params(56),
         name="pre",
-    )(own, from_core, from_chip, from_both, mod, gains, *loaded, *weights[3:])
+    )(own, from_core, from_chip, from_both, mod, gains, *weights)
 
     recv = lax.all_to_all(send, seq, 0, 0, tiled=True)
     nz = shifted(slabs[0:4], "z")
@@ -538,46 +514,46 @@
     )(back, proj, gains)
     blocks_z = shifted([by_z] * 4, "z")
     blocks_y = shifted([by_y] * 4, "y")
-    mine0, mine1, theirs0, theirs1, token = pl.pallas_call(
+    slabs = pl.pallas_call(
         post_kernel,
-        out_shape=[rows] * 4 + [shape((8, 128), F32)],
+        out_shape=shape((4, ROWS, IMG), BF16),
         in_specs=[VMEM] * 8 + [HBM] * 6,
-        out_specs=[VMEM] * 5,
+        out_specs=VMEM,
         scratch_shapes=[
             pltpu.VMEM((3, 3, D, WIDTH), BF16),
             pltpu.VMEM((3, WIDTH, D), BF16),
             pltpu.VMEM((IMG + TXT, 4 * WIDTH), BF16),
-            pltpu.VMEM((4, ROWS, IMG), BF16),
             pltpu.SemaphoreType.DMA((6,)),
         ],
         compiler_params=params(54),
         cost_estimate=pl.CostEstimate(flops=14_000_000_000, bytes_accessed=30_000_000, transcendentals=0),
         name="post",
     )(back, proj, gains, by_z, by_y, xhat, rstd, mod, *weights)
+    terms_z, *outs = pl.pallas_call(
+        weight_kernel,
+        out_shape=[shape((4, PIECE, 2 * WIDTH), BF16)] + [shape((PIECE, 2 * WIDTH), BF16)] * 4 + [rows] * 4,
+        in_specs=[VMEM] * 17,
+        out_specs=[VMEM] * 9,
+        scratch_shapes=[pltpu.VMEM((4, PIECE, 2 * WIDTH), BF16)],
+        compiler_params=params(24),
+        cost_estimate=pl.CostEstimate(flops=3_000_000_000, bytes_accessed=5_000_000, transcendentals=0),
+        name="weight",
+    )(*nz, *ny, *blocks_z, *blocks_y, slabs)
+    terms_y, (mine0, mine1, theirs0, theirs1) = outs[0:4], outs[4:8]
     got1 = lax.ppermute(theirs1, "tp", other_core)
     got0 = lax.ppermute(theirs0, "tp", other_core)
     passed = (mine1.astype(F32) + got1.astype(F32)).astype(BF16)
     passed = lax.ppermute(passed, "tp", other_chip)
-
-    terms_z, terms_y = pl.pallas_call(
-        weight_kernel,
-        out_shape=[shape((4, PIECE, 2 * WIDTH), BF16)] * 2,
-        in_specs=[VMEM] * 16 + [ANY],
-        out_specs=[VMEM] * 2,
-        compiler_params=params(20),
-        cost_estimate=pl.CostEstimate(flops=3_000_000_000, bytes_accessed=5_000_000, transcendentals=0),
-        name="weight",
-    )(*nz, *ny, *blocks_z, *blocks_y, token)
+    terms_y = shifted(terms_y, "z")
     terms_z = lax.all_to_all(terms_z, "y", 0, 0, tiled=True)
-    terms_y = lax.all_to_all(terms_y, "z", 0, 0, tiled=True)
     mine, theirs = pl.pallas_call(
         weight_sum_kernel,
         out_shape=[shape((PIECE // 2, 4 * WIDTH), F32), shape((PIECE // 2, 4 * WIDTH), BF16)],
-        in_specs=[VMEM] * 2,
+        in_specs=[VMEM] * 5,
         out_specs=[VMEM] * 2,
         compiler_params=params(16),
         name="weight_sum",
-    )(terms_z, terms_y)
+    )(terms_z, *terms_y)
     theirs = lax.ppermute(theirs, "w", [(0, 1), (1, 0)])
     grad_qkv, grad_out = pl.pallas_call(
         weight_out_kernel,

time: 207 us -> 201 us (0.971)
  waiting for transfers between devices: 37.9 us -> 46.2 us
  Pallas kernels: 74.9 us -> 67.3 us
  local copies, waits for them, and re-layouts: 14.4 us -> 8 us
    ppermute x1, waiting for transfers between devices: 0.15 us -> 11.7 us  [per_device(): from_chip = lax.ppermute(own, 'tp', other_chip)]
    all_to_all x1, waiting for transfers between devices: 9.82 us -> 0.01 us  [per_device(): terms_z = lax.all_to_all(terms_z, 'y', 0, 0, tiled=True)]
    pallas_call x4 -> x2, Pallas kernels: 25.6 us -> 17.1 us  [the longest x1 15.1 us: per_device(): pl.pallas_call(post_kernel, out_shape=shape((4, ROWS, IMG), BF16), in_spe...]
    ppermute x12 -> x15, waiting for transfers between devices: 17.1 us -> 25.4 us  [shifted(): lax.ppermute(parts[d], axis, [(i, (i + d) % 4) for i in range(4)])]
    ppermute x1, waiting for transfers between devices: 0.01 us -> 7.18 us  [per_device(): theirs = lax.ppermute(theirs, 'w', [(0, 1), (1, 0)])]
    unnamed x62 -> x56, local copies, waits for them, and re-layouts: 14.4 us -> 8 us
    all_to_all x1 -> x0, waiting for transfers between devices: 5.25 us -> none  [per_device(): terms_y = lax.all_to_all(terms_y, 'z', 0, 0, tiled=True)]
    ppermute x12 -> x15, starting transfers between devices: 17.6 us -> 22.8 us  [shifted(): lax.ppermute(parts[d], axis, [(i, (i + d) % 4) for i in range(4)])]
  transfers between devices with their start and end apart: 22 -> 24, of which waited for: 7 -> 7; matrix products, arithmetic and copies ran while one was open for 1% -> 1% of each run, Pallas kernels for 26% -> 21%
where the time goes in v2:
time: 201 us; the launch traced here: 200 us
  Pallas kernels  67.3 us (33%)
  waiting for transfers between devices  46.2 us (23%)
  starting transfers between devices  42.6 us (21%)
  blocking collectives  31.9 us (16%)
  local copies, waits for them, and re-layouts  8 us (4%)
  other arithmetic  2.09 us (1%)
    all_to_all x1, blocking collectives, per_device(): back = lax.all_to_all(back, seq, 0, 0, tiled=True)  31.9 us
    pallas_call x1, Pallas kernels, per_device(): pl.pallas_call(attention_kernel, out_shape=[shape((keys, 128), BF16), sha...  25.9 us
    ppermute x15, waiting for transfers between devices, shifted(): lax.ppermute(parts[d], axis, [(i, (i + d) % 4) for i in range(4)])  25.4 us
    ppermute x15, starting transfers between devices, shifted(): lax.ppermute(parts[d], axis, [(i, (i + d) % 4) for i in range(4)])  22.8 us
    pallas_call x1, Pallas kernels, per_device(): pl.pallas_call(pre_kernel, out_shape=[shape((BLOCKS, CHUNK, 128), BF16),...  16.2 us
    pallas_call x1, Pallas kernels, per_device(): pl.pallas_call(post_kernel, out_shape=shape((4, ROWS, IMG), BF16), in_spe...  15.1 us
    ppermute x1, waiting for transfers between devices, per_device(): from_chip = lax.ppermute(own, 'tp', other_chip)  11.7 us
    all_to_all x1, starting transfers between devices, per_device(): recv = lax.all_to_all(send, seq, 0, 0, tiled=True)  9.63 us
  transfers between devices with their start and end apart: 24, of which 7 were waited for; matrix products, arithmetic and copies ran while one was open for 1% of the time, Pallas kernels for 21%

profile of v2, /device:TPU:0, one launch (start us, length us, event | category | flops | bytes accessed | tf_op | source)
XLA Modules:
  0.0 199.7 jit_solution(1627401057185160510)
XLA Ops:
  0.6 1.9 pack.1.in0
  2.6 3.2 %collective-permute-start.1 = (bf16[1976,128]{1,0:T(8,128)(2,1)}, bf16[1976,128]{1,0:T(8,128)(2,1)S(1)}, u32[]{:S(2)}, u32[]{:S(2)}) collective-permute-start(bf16[1976,128]{1,0:T(8,128)(2,1)} %pack.1.in0), channel_id=1, source_target_pairs={{0,2},{1,3},{2,0},{3,1},{4,6},{5,7},{6,4},{7,5},{8,10},{9,11},{10,... | collective-permute-start | bytes 1517576 | tf_op jit(solution)/shard_map/ppermute | solution.py:450
  5.8 11.7 %collective-permute-done.1.in2 = bf16[1976,128]{1,0:T(8,128)(2,1)S(1)} collective-permute-done((bf16[1976,128]{1,0:T(8,128)(2,1)}, bf16[1976,128]{1,0:T(8,128)(2,1)S(1)}, u32[]{:S(2)}, u32[]{:S(2)}) %collective-permute-start.1) | collective-permute-done | bytes 505888 | tf_op jit(solution)/shard_map/ppermute | solution.py:450
  17.5 1.9 collective-permute-done.2.in3
  20.2 16.2 %pre.1 = (bf16[32,192,128]{2,1,0:T(8,128)(2,1)}, f32[272,768]{1,0:T(8,128)}, f32[272,2432]{1,0:T(8,128)}, f32[272,128]{1,0:T(8,128)}, bf16[608,128]{1,0:T(8,128)...) custom-call(bf16[1976,128]{1,0:T(8,128)(2,1)} %pack.1.in0, ...), custom_call_target="tpu_custom_call" | custom-call | tf_op jit(solution)/shard_map/pre/pallas_call | solution.py:454
  36.5 9.6 %all-to-all-start = ((bf16[32,192,128]{2,1,0:T(8,128)(2,1)}), bf16[32,192,128]{2,1,0:T(8,128)(2,1)S(1)}, u32[]{:S(2)}, u32[]{:S(2)}) async-start(bf16[32,192,128]{2,1,0:T(8,128)(2,1)} %get-tuple-element.49), calls=%async_computation | async-start | bytes 3145728 | tf_op jit(solution)/shard_map/all_to_all | solution.py:476
  46.1 3.1 %collective-permute-start.5 = (bf16[608,128]{1,0:T(8,128)(2,1)S(1)}, bf16[608,128]{1,0:T(8,128)(2,1)S(1)}, u32[]{:S(2)}, u32[]{:S(2)}) collective-permute-start(bf16[608,128]{1,0:T(8,128)(2,1)S(1)} %copy-done.27), channel_id=1, source_target_pairs={{0,96},{32,0},{64,32},{96,64},{1,97},{33,1},{65,33},{97,65},{2,98}... | collective-permute-start | bytes 466952 | tf_op jit(solution)/shard_map/ppermute | solution.py:420
  50.0 2.3 %collective-permute-start.4 = (bf16[608,128]{1,0:T(8,128)(2,1)S(1)}, bf16[608,128]{1,0:T(8,128)(2,1)S(1)}, u32[]{:S(2)}, u32[]{:S(2)}) collective-permute-start(bf16[608,128]{1,0:T(8,128)(2,1)S(1)} %copy-done.26), channel_id=1, source_target_pairs={{0,64},{32,96},{64,0},{96,32},{1,65},{33,97},{65,1},{97,33},{2,66}... | collective-permute-start | bytes 466952 | tf_op jit(solution)/shard_map/ppermute | solution.py:420
  52.3 1.5 collective-permute-start.6
  53.7 2.7 %collective-permute-start.7 = (bf16[2,608,128]{2,1,0:T(8,128)(2,1)}, bf16[2,608,128]{2,1,0:T(8,128)(2,1)S(1)}, u32[]{:S(2)}, u32[]{:S(2)}) collective-permute-start(bf16[2,608,128]{2,1,0:T(8,128)(2,1)} %get-tuple-element.47), channel_id=1, source_target_pairs={{0,16},{8,24},{16,0},{24,8},{1,17},{9,25},{17,1},{25,9},{2,18},{10... | collective-permute-start | bytes 933896 | tf_op jit(solution)/shard_map/ppermute | solution.py:420
  56.4 13.3 %collective-permute-done.5.after.nz3 = bf16[608,128]{1,0:T(8,128)(2,1)S(1)} collective-permute-done((bf16[608,128]{1,0:T(8,128)(2,1)S(1)}, bf16[608,128]{1,0:T(8,128)(2,1)S(1)}, u32[]{:S(2)}, u32[]{:S(2)}) %collective-permute-start.5) | collective-permute-done | bytes 155680 | tf_op jit(solution)/shard_map/ppermute | solution.py:420
  69.7 2.6 %collective-permute-start.8 = (bf16[2,608,128]{2,1,0:T(8,128)(2,1)S(1)}, bf16[2,608,128]{2,1,0:T(8,128)(2,1)S(1)}, u32[]{:S(2)}, u32[]{:S(2)}) collective-permute-start(bf16[2,608,128]{2,1,0:T(8,128)(2,1)S(1)} %copy-done.25), channel_id=1, source_target_pairs={{0,24},{8,0},{16,8},{24,16},{1,25},{9,1},{17,9},{25,17},{2,26},{10... | collective-permute-start | bytes 933896 | tf_op jit(solution)/shard_map/ppermute | solution.py:420
  72.3 25.9 %attention.1 = (bf16[4608,128]{1,0:T(8,128)(2,1)S(1)}, bf16[2048,128]{1,0:T(8,128)(2,1)S(1)}) custom-call(s32[2]{0:T(128)S(1)} %pad_add_fusion.role, bf16[32,192,128]{2,1,0:T(8,128)(2,1)S(1)} %all-to-all-done.recv, bf16[608,128]{1,0:T(8,128)(2,1)S(1)} %collective-permute-done.5.after.nz3), custom_call_target="tpu_custom_call" | custom-call | flops 40000000000 | bytes 3200000 | tf_op jit(solution)/shard_map/attention/pallas_call | solution.py:480
  98.9 31.9 %all_to_all.15.recv = bf16[32,192,128]{2,1,0:T(8,128)(2,1)S(1)} all-to-all(bf16[32,192,128]{2,1,0:T(8,128)(2,1)S(1)} %scatter.1), channel_id=1, replica_groups=mesh['z'=4,'y'=4,'w'=2,'tp'=4] {'z','y','w'}, dimensions={0} | all-to-all | bytes 3145728 | tf_op jit(solution)/shard_map/all_to_all | solution.py:505
  130.9 2.5 %head_back_ctl.1 = (bf16[128,768]{1,0:T(8,128)(2,1)S(1)}, bf16[128,768]{1,0:T(8,128)(2,1)S(1)}) custom-call(bf16[32,192,128]{2,1,0:T(8,128)(2,1)S(1)} %all_to_all.15.recv, f32[272,768]{1,0:T(8,128)S(1)} %copy-done.1, f32[3,2,64]{2,1,0:T(2,128)S(1)} %copy-done.10), custom_call_target="tpu_custom_call" | custom-call | tf_op jit(solution)/shard_map/head_back_ctl/pallas_call | solution.py:507
  135.7 1.2 collective-permute-start.14
  136.9 1.4 collective-permute-start.13
  138.3 1.6 collective-permute-done.11.bz3
  140.5 15.1 %post.1.slabs = bf16[4,1976,128]{2,1,0:T(8,128)(2,1)} custom-call(bf16[32,192,128]{2,1,0:T(8,128)(2,1)} %copy-done, f32[272,768]{1,0:T(8,128)} %get-tuple-element.52.proj, f32[3,2,64]{2,1,0:T(2,128)} %gains.5, bf16[128,768]{1,0:T(8,128)(2,1)} %copy-done.14, bf16[128,768]{1,0:T(8,128)(2,1)} %copy-done.16, f32[272,2432]{1,0:T(8,128)} %get-tuple-element.55.xhat, ...), custom_call_target="tpu_custom_call" | custom-call | flops 14000000000 | bytes 30000000 | tf_op jit(solution)/shard_map/post/pallas_call | solution.py:517
  156.7 0.9 copy-done.17
  157.6 1.6 copy-done.21
  159.2 2.6 %weight.1 = (bf16[4,152,768]{2,1,0:T(8,128)(2,1)}, bf16[152,768]{1,0:T(8,128)(2,1)S(1)}, bf16[152,768]{1,0:T(8,128)(2,1)}, bf16[152,768]{1,0:T(8,128)(2,1)S(1)},...) custom-call(bf16[608,128]{1,0:T(8,128)(2,1)S(1)} %copy-done.18, ...), custom_call_target="tpu_custom_call" | custom-call | flops 3000000000 | bytes 5000000 | tf_op jit(solution)/shard_map/weight/pallas_call | solution.py:532
  163.8 4.1 %all-to-all-start.2 = ((bf16[4,152,768]{2,1,0:T(8,128)(2,1)}), bf16[4,152,768]{2,1,0:T(8,128)(2,1)S(1)}, u32[]{:S(2)}, u32[]{:S(2)}) async-start(bf16[4,152,768]{2,1,0:T(8,128)(2,1)} %get-tuple-element.66), calls=%async_computation.2 | async-start | bytes 1867776 | tf_op jit(solution)/shard_map/all_to_all | solution.py:548
  168.0 2.0 %add_convert_fusion = bf16[1976,128]{1,0:T(8,128)(2,1)} fusion(bf16[1976,128]{1,0:T(8,128)(2,1)} %collective-permute-done.16, bf16[1976,128]{1,0:T(8,128)(2,1)S(1)} %get-tuple-element.59), kind=kLoop, calls=%fused_computation | loop fusion | flops 1011712 | bytes 1517568 | tf_op jit(solution)/shard_map/convert_element_type | solution.py:545
  170.0 2.7 %collective-permute-start.17 = (bf16[1976,128]{1,0:T(8,128)(2,1)}, bf16[1976,128]{1,0:T(8,128)(2,1)S(1)}, u32[]{:S(2)}, u32[]{:S(2)}) collective-permute-start(bf16[1976,128]{1,0:T(8,128)(2,1)} %add_convert_fusion), channel_id=1, source_target_pairs={{0,2},{1,3},{2,0},{3,1},{4,6},{5,7},{6,4},{7,5},{8,10},{9,11},{10,... | collective-permute-start | bytes 1517576 | tf_op jit(solution)/shard_map/ppermute | solution.py:546
  172.7 1.1 collective-permute-start.18
  173.8 3.6 %collective-permute-start.19 = (bf16[152,768]{1,0:T(8,128)(2,1)}, bf16[152,768]{1,0:T(8,128)(2,1)S(1)}, u32[]{:S(2)}, u32[]{:S(2)}) collective-permute-start(bf16[152,768]{1,0:T(8,128)(2,1)} %copy-done.13), channel_id=1, source_target_pairs={{0,64},{32,96},{64,0},{96,32},{1,65},{33,97},{65,1},{97,33},{2,66}... | collective-permute-start | bytes 700424 | tf_op jit(solution)/shard_map/ppermute | solution.py:420
  178.0 4.2 %collective-permute-done.18.y1 = bf16[152,768]{1,0:T(8,128)(2,1)S(1)} collective-permute-done((bf16[152,768]{1,0:T(8,128)(2,1)}, bf16[152,768]{1,0:T(8,128)(2,1)S(1)}, u32[]{:S(2)}, u32[]{:S(2)}) %collective-permute-start.18) | collective-permute-done | bytes 233504 | tf_op jit(solution)/shard_map/ppermute | solution.py:420
  182.2 6.2 %collective-permute-done.19.y2 = bf16[152,768]{1,0:T(8,128)(2,1)S(1)} collective-permute-done((bf16[152,768]{1,0:T(8,128)(2,1)}, bf16[152,768]{1,0:T(8,128)(2,1)S(1)}, u32[]{:S(2)}, u32[]{:S(2)}) %collective-permute-start.19) | collective-permute-done | bytes 233504 | tf_op jit(solution)/shard_map/ppermute | solution.py:420
  189.1 0.9 copy-done.7
  190.5 7.2 %collective-permute-done.21.other = bf16[76,1536]{1,0:T(8,128)(2,1)S(1)} collective-permute-done((bf16[76,1536]{1,0:T(8,128)(2,1)S(1)}, bf16[76,1536]{1,0:T(8,128)(2,1)S(1)}, u32[]{:S(2)}, u32[]{:S(2)}) %collective-permute-start.21) | collective-permute-done | bytes 233504 | tf_op jit(solution)/shard_map/ppermute | solution.py:557
  198.6 1.1 final.1
  (85 shorter events, 10.1 us)
Async XLA Ops:
  2.6 14.9 %collective-permute-start.1 = (bf16[1976,128]{1,0:T(8,128)(2,1)}, bf16[1976,128]{1,0:T(8,128)(2,1)S(1)}, u32[]{:S(2)}, u32[]{:S(2)}) collective-permute-start(bf16[1976,128]{1,0:T(8,128)(2,1)} %pack.1.in0), channel_id=1, source_target_pairs={{0,2},{1,3},{2,0},{3,1},{4,6},{5,7},{6,4},{7,5},{8,10},{9,11},{10,... | collective-permute-start | bytes 1517576 | tf_op jit(solution)/shard_map/ppermute | solution.py:450
  5.8 11.7 %collective-permute-start = (bf16[1976,128]{1,0:T(8,128)(2,1)}, bf16[1976,128]{1,0:T(8,128)(2,1)S(1)}, u32[]{:S(2)}, u32[]{:S(2)}) collective-permute-start(bf16[1976,128]{1,0:T(8,128)(2,1)} %pack.1.in0), channel_id=1, source_target_pairs={{0,1},{1,0},{2,3},{3,2},{4,5},{5,4},{6,7},{7,6},{8,9},{9,8},{10,11... | collective-permute-start | bytes 1517576 | tf_op jit(solution)/shard_map/ppermute | solution.py:451
  17.5 1.9 collective-permute-start.2
  36.5 33.3 %copy-start.25 = (bf16[2,608,128]{2,1,0:T(8,128)(2,1)S(1)}, bf16[2,608,128]{2,1,0:T(8,128)(2,1)}, u32[]{:S(2)}) copy-start(bf16[2,608,128]{2,1,0:T(8,128)(2,1)} %get-tuple-element.48) | copy-start | bytes 933892
  36.5 35.8 %all-to-all-start = ((bf16[32,192,128]{2,1,0:T(8,128)(2,1)}), bf16[32,192,128]{2,1,0:T(8,128)(2,1)S(1)}, u32[]{:S(2)}, u32[]{:S(2)}) async-start(bf16[32,192,128]{2,1,0:T(8,128)(2,1)} %get-tuple-element.49), calls=%async_computation | async-start | bytes 3145728 | tf_op jit(solution)/shard_map/all_to_all | solution.py:476
  46.1 23.6 %collective-permute-start.5 = (bf16[608,128]{1,0:T(8,128)(2,1)S(1)}, bf16[608,128]{1,0:T(8,128)(2,1)S(1)}, u32[]{:S(2)}, u32[]{:S(2)}) collective-permute-start(bf16[608,128]{1,0:T(8,128)(2,1)S(1)} %copy-done.27), channel_id=1, source_target_pairs={{0,96},{32,0},{64,32},{96,64},{1,97},{33,1},{65,33},{97,65},{2,98}... | collective-permute-start | bytes 466952 | tf_op jit(solution)/shard_map/ppermute | solution.py:420
  50.0 48.2 %collective-permute-start.3 = (bf16[608,128]{1,0:T(8,128)(2,1)}, bf16[608,128]{1,0:T(8,128)(2,1)S(1)}, u32[]{:S(2)}, u32[]{:S(2)}) collective-permute-start(bf16[608,128]{1,0:T(8,128)(2,1)} %get-tuple-element.42), channel_id=1, source_target_pairs={{0,32},{32,64},{64,96},{96,0},{1,33},{33,65},{65,97},{97,1},{2,34}... | collective-permute-start | bytes 466952 | tf_op jit(solution)/shard_map/ppermute | solution.py:420
  50.0 48.2 %collective-permute-start.4 = (bf16[608,128]{1,0:T(8,128)(2,1)S(1)}, bf16[608,128]{1,0:T(8,128)(2,1)S(1)}, u32[]{:S(2)}, u32[]{:S(2)}) collective-permute-start(bf16[608,128]{1,0:T(8,128)(2,1)S(1)} %copy-done.26), channel_id=1, source_target_pairs={{0,64},{32,96},{64,0},{96,32},{1,65},{33,97},{65,1},{97,33},{2,66}... | collective-permute-start | bytes 466952 | tf_op jit(solution)/shard_map/ppermute | solution.py:420
  52.3 46.0 %collective-permute-start.6 = (bf16[2,608,128]{2,1,0:T(8,128)(2,1)}, bf16[2,608,128]{2,1,0:T(8,128)(2,1)S(1)}, u32[]{:S(2)}, u32[]{:S(2)}) collective-permute-start(bf16[2,608,128]{2,1,0:T(8,128)(2,1)} %get-tuple-element.46), channel_id=1, source_target_pairs={{0,8},{8,16},{16,24},{24,0},{1,9},{9,17},{17,25},{25,1},{2,10},{10... | collective-permute-start | bytes 933896 | tf_op jit(solution)/shard_map/ppermute | solution.py:420
  53.7 44.5 %collective-permute-start.7 = (bf16[2,608,128]{2,1,0:T(8,128)(2,1)}, bf16[2,608,128]{2,1,0:T(8,128)(2,1)S(1)}, u32[]{:S(2)}, u32[]{:S(2)}) collective-permute-start(bf16[2,608,128]{2,1,0:T(8,128)(2,1)} %get-tuple-element.47), channel_id=1, source_target_pairs={{0,16},{8,24},{16,0},{24,8},{1,17},{9,25},{17,1},{25,9},{2,18},{10... | collective-permute-start | bytes 933896 | tf_op jit(solution)/shard_map/ppermute | solution.py:420
  69.7 28.5 %copy-start.19 = (bf16[608,128]{1,0:T(8,128)(2,1)}, bf16[608,128]{1,0:T(8,128)(2,1)S(1)}, u32[]{:S(2)}) copy-start(bf16[608,128]{1,0:T(8,128)(2,1)S(1)} %collective-permute-done.5.after.nz3) | copy-start | bytes 466948
  69.7 28.5 %collective-permute-start.8 = (bf16[2,608,128]{2,1,0:T(8,128)(2,1)S(1)}, bf16[2,608,128]{2,1,0:T(8,128)(2,1)S(1)}, u32[]{:S(2)}, u32[]{:S(2)}) collective-permute-start(bf16[2,608,128]{2,1,0:T(8,128)(2,1)S(1)} %copy-done.25), channel_id=1, source_target_pairs={{0,24},{8,0},{16,8},{24,16},{1,25},{9,1},{17,9},{25,17},{2,26},{10... | collective-permute-start | bytes 933896 | tf_op jit(solution)/shard_map/ppermute | solution.py:420
  98.9 31.9 %copy-start.1 = (f32[272,768]{1,0:T(8,128)S(1)}, f32[272,768]{1,0:T(8,128)}, u32[]{:S(2)}) copy-start(f32[272,768]{1,0:T(8,128)} %get-tuple-element.52.proj) | copy-start | bytes 2506756
  98.9 31.9 %copy-start.10 = (f32[3,2,64]{2,1,0:T(2,128)S(1)}, f32[3,2,64]{2,1,0:T(2,128)}, u32[]{:S(2)}) copy-start(f32[3,2,64]{2,1,0:T(2,128)} %gains.5) | copy-start | bytes 4612
  133.4 6.5 %collective-permute-start.11 = (bf16[128,768]{1,0:T(8,128)(2,1)S(1)}, bf16[128,768]{1,0:T(8,128)(2,1)S(1)}, u32[]{:S(2)}, u32[]{:S(2)}) collective-permute-start(bf16[128,768]{1,0:T(8,128)(2,1)S(1)} %get-tuple-element.53.by_z.bz0), channel_id=1, source_target_pairs={{0,96},{32,0},{64,32},{96,64},{1,97},{33,1},{65,33},{97,65},{2,98}... | collective-permute-start | bytes 589832 | tf_op jit(solution)/shard_map/ppermute | solution.py:420
  134.3 21.4 %collective-permute-start.10 = (bf16[128,768]{1,0:T(8,128)(2,1)S(1)}, bf16[128,768]{1,0:T(8,128)(2,1)S(1)}, u32[]{:S(2)}, u32[]{:S(2)}) collective-permute-start(bf16[128,768]{1,0:T(8,128)(2,1)S(1)} %get-tuple-element.53.by_z.bz0), channel_id=1, source_target_pairs={{0,64},{32,96},{64,0},{96,32},{1,65},{33,97},{65,1},{97,33},{2,66}... | collective-permute-start | bytes 589832 | tf_op jit(solution)/shard_map/ppermute | solution.py:420
  134.8 20.9 %collective-permute-start.9 = (bf16[128,768]{1,0:T(8,128)(2,1)S(1)}, bf16[128,768]{1,0:T(8,128)(2,1)S(1)}, u32[]{:S(2)}, u32[]{:S(2)}) collective-permute-start(bf16[128,768]{1,0:T(8,128)(2,1)S(1)} %get-tuple-element.53.by_z.bz0), channel_id=1, source_target_pairs={{0,32},{32,64},{64,96},{96,0},{1,33},{33,65},{65,97},{97,1},{2,34}... | collective-permute-start | bytes 589832 | tf_op jit(solution)/shard_map/ppermute | solution.py:420
  135.7 20.0 %collective-permute-start.14 = (bf16[128,768]{1,0:T(8,128)(2,1)S(1)}, bf16[128,768]{1,0:T(8,128)(2,1)S(1)}, u32[]{:S(2)}, u32[]{:S(2)}) collective-permute-start(bf16[128,768]{1,0:T(8,128)(2,1)S(1)} %get-tuple-element.54.by_y.by0), channel_id=1, source_target_pairs={{0,24},{8,0},{16,8},{24,16},{1,25},{9,1},{17,9},{25,17},{2,26},{10... | collective-permute-start | bytes 589832 | tf_op jit(solution)/shard_map/ppermute | solution.py:420
  136.9 18.8 %collective-permute-start.13 = (bf16[128,768]{1,0:T(8,128)(2,1)S(1)}, bf16[128,768]{1,0:T(8,128)(2,1)S(1)}, u32[]{:S(2)}, u32[]{:S(2)}) collective-permute-start(bf16[128,768]{1,0:T(8,128)(2,1)S(1)} %get-tuple-element.54.by_y.by0), channel_id=1, source_target_pairs={{0,16},{8,24},{16,0},{24,8},{1,17},{9,25},{17,1},{25,9},{2,18},{10... | collective-permute-start | bytes 589832 | tf_op jit(solution)/shard_map/ppermute | solution.py:420
  139.9 15.8 %collective-permute-start.12 = (bf16[128,768]{1,0:T(8,128)(2,1)S(1)}, bf16[128,768]{1,0:T(8,128)(2,1)S(1)}, u32[]{:S(2)}, u32[]{:S(2)}) collective-permute-start(bf16[128,768]{1,0:T(8,128)(2,1)S(1)} %get-tuple-element.54.by_y.by0), channel_id=1, source_target_pairs={{0,8},{8,16},{16,24},{24,0},{1,9},{9,17},{17,25},{25,1},{2,10},{10... | collective-permute-start | bytes 589832 | tf_op jit(solution)/shard_map/ppermute | solution.py:420
  163.8 4.2 %collective-permute-start.16 = (bf16[1976,128]{1,0:T(8,128)(2,1)}, bf16[1976,128]{1,0:T(8,128)(2,1)}, u32[]{:S(2)}, u32[]{:S(2)}) collective-permute-start(bf16[1976,128]{1,0:T(8,128)(2,1)} %get-tuple-element.60), channel_id=1, source_target_pairs={{0,1},{1,0},{2,3},{3,2},{4,5},{5,4},{6,7},{7,6},{8,9},{9,8},{10,11... | collective-permute-start | bytes 1517576 | tf_op jit(solution)/shard_map/ppermute | solution.py:543
  163.8 25.3 %all-to-all-start.2 = ((bf16[4,152,768]{2,1,0:T(8,128)(2,1)}), bf16[4,152,768]{2,1,0:T(8,128)(2,1)S(1)}, u32[]{:S(2)}, u32[]{:S(2)}) async-start(bf16[4,152,768]{2,1,0:T(8,128)(2,1)} %get-tuple-element.66), calls=%async_computation.2 | async-start | bytes 1867776 | tf_op jit(solution)/shard_map/all_to_all | solution.py:548
  167.9 30.6 %collective-permute-start.15 = (bf16[1976,128]{1,0:T(8,128)(2,1)}, bf16[1976,128]{1,0:T(8,128)(2,1)S(1)}, u32[]{:S(2)}, u32[]{:S(2)}) collective-permute-start(bf16[1976,128]{1,0:T(8,128)(2,1)} %get-tuple-element.58), channel_id=1, source_target_pairs={{0,1},{1,0},{2,3},{3,2},{4,5},{5,4},{6,7},{7,6},{8,9},{9,8},{10,11... | collective-permute-start | bytes 1517576 | tf_op jit(solution)/shard_map/ppermute | solution.py:544
  168.0 30.5 %copy-start.2 = (bf16[128,608]{0,1:T(8,128)(2,1)S(1)}, bf16[128,608]{0,1:T(8,128)(2,1)}, u32[]{:S(2)}) copy-start(bf16[128,608]{0,1:T(8,128)(2,1)} %param.14) | copy-start | bytes 466948
  168.0 30.5 %copy-start.3 = (bf16[128,608]{0,1:T(8,128)(2,1)S(1)}, bf16[128,608]{0,1:T(8,128)(2,1)}, u32[]{:S(2)}) copy-start(bf16[128,608]{0,1:T(8,128)(2,1)} %param.17) | copy-start | bytes 466948
  168.0 30.5 %copy-start.8 = (bf16[16,608]{1,0:T(8,128)(2,1)S(1)}, bf16[16,608]{1,0:T(8,128)(2,1)}, u32[]{:S(2)}) copy-start(bf16[16,608]{1,0:T(8,128)(2,1)} %txt.3) | copy-start | bytes 58372
  168.0 30.5 %copy-start.9 = (bf16[16,608]{1,0:T(8,128)(2,1)S(1)}, bf16[16,608]{1,0:T(8,128)(2,1)}, u32[]{:S(2)}) copy-start(bf16[16,608]{1,0:T(8,128)(2,1)} %dy_txt.3) | copy-start | bytes 58372
  170.0 28.5 %collective-permute-start.17 = (bf16[1976,128]{1,0:T(8,128)(2,1)}, bf16[1976,128]{1,0:T(8,128)(2,1)S(1)}, u32[]{:S(2)}, u32[]{:S(2)}) collective-permute-start(bf16[1976,128]{1,0:T(8,128)(2,1)} %add_convert_fusion), channel_id=1, source_target_pairs={{0,2},{1,3},{2,0},{3,1},{4,6},{5,7},{6,4},{7,5},{8,10},{9,11},{10,... | collective-permute-start | bytes 1517576 | tf_op jit(solution)/shard_map/ppermute | solution.py:546
  172.7 9.5 %collective-permute-start.18 = (bf16[152,768]{1,0:T(8,128)(2,1)}, bf16[152,768]{1,0:T(8,128)(2,1)S(1)}, u32[]{:S(2)}, u32[]{:S(2)}) collective-permute-start(bf16[152,768]{1,0:T(8,128)(2,1)} %get-tuple-element.68), channel_id=1, source_target_pairs={{0,32},{32,64},{64,96},{96,0},{1,33},{33,65},{65,97},{97,1},{2,34}... | collective-permute-start | bytes 700424 | tf_op jit(solution)/shard_map/ppermute | solution.py:420
  173.8 14.6 %collective-permute-start.19 = (bf16[152,768]{1,0:T(8,128)(2,1)}, bf16[152,768]{1,0:T(8,128)(2,1)S(1)}, u32[]{:S(2)}, u32[]{:S(2)}) collective-permute-start(bf16[152,768]{1,0:T(8,128)(2,1)} %copy-done.13), channel_id=1, source_target_pairs={{0,64},{32,96},{64,0},{96,32},{1,65},{33,97},{65,1},{97,33},{2,66}... | collective-permute-start | bytes 700424 | tf_op jit(solution)/shard_map/ppermute | solution.py:420
  177.5 10.9 %collective-permute-start.20 = (bf16[152,768]{1,0:T(8,128)(2,1)}, bf16[152,768]{1,0:T(8,128)(2,1)S(1)}, u32[]{:S(2)}, u32[]{:S(2)}) collective-permute-start(bf16[152,768]{1,0:T(8,128)(2,1)} %copy-done.12), channel_id=1, source_target_pairs={{0,96},{32,0},{64,32},{96,64},{1,97},{33,1},{65,33},{97,65},{2,98}... | collective-permute-start | bytes 700424 | tf_op jit(solution)/shard_map/ppermute | solution.py:420
  190.4 7.3 %collective-permute-start.21 = (bf16[76,1536]{1,0:T(8,128)(2,1)S(1)}, bf16[76,1536]{1,0:T(8,128)(2,1)S(1)}, u32[]{:S(2)}, u32[]{:S(2)}) collective-permute-start(bf16[76,1536]{1,0:T(8,128)(2,1)S(1)} %get-tuple-element.72), channel_id=1, source_target_pairs={{0,4},{4,0},{1,5},{5,1},{2,6},{6,2},{3,7},{7,3},{8,12},{12,8},{9,1... | collective-permute-start | bytes 700424 | tf_op jit(solution)/shard_map/ppermute | solution.py:557
  (20 other events, 129.7 us)

commit v3 on v2

--- a/solution.py
+++ b/solution.py
@@ -93,16 +93,37 @@
         copy.wait()
 
 
+class Results:
+    def __init__(self, sems):
+        self.sems, self.copies = sems, []
+
+    def send(self, source, target):
+        copy = pltpu.make_async_copy(source, target, self.sems.at[len(self.copies)])
+        copy.start()
+        self.copies.append(copy)
+
+    def finish(self):
+        for copy in self.copies:
+            copy.wait()
+
+
 def pre_kernel(
     in0, in1, in2, in3, mod, gains, wq_img, wq_txt, wq_ctl, wo_img, wo_txt, wo_ctl,
-    send, proj, xhat, rstd, nz0, nz1, nz2, nz3, ny0, ny1, ny2, ny3,
-    wq, wo, gat, nz, ny, sems,
+    send_out, proj_out, xhat_out, rstd_out, nz0, nz1, nz2, nz3, ny0, ny1, ny2, ny3,
+    wq, wo, gat, send, send_ctl, proj, xhat, rstd, nz, ny, sems, in_sems, out_sems,
 ):
+    arrivals = [
+        pltpu.make_async_copy(part, gat.at[lax.axis_index("tp") ^ i], in_sems.at[i])
+        for i, part in enumerate((in0, in1, in2, in3))
+    ]
+    for copy in arrivals:
+        copy.start()
     copies = weight_copies((wq_img, wq_txt, wq_ctl, wo_img, wo_txt, wo_ctl), wq, wo, sems)
-    copies[0][0].start()
-
-    for i, part in enumerate((in0, in1, in2, in3)):
-        gat[lax.axis_index("tp") ^ i] = part[...]
+    for copy in (copies[0][0], copies[0][1], copies[2][0]):
+        copy.start()
+    results = Results(out_sems)
+    for copy in arrivals:
+        copy.wait()
 
     def rows(slab):
         return gat[:, SHARE * slab : SHARE * (slab + 1), :].reshape(D, IMG).T.astype(F32)
@@ -116,14 +137,15 @@
         rstd[at : at + count, :] = jnp.broadcast_to(inverse, (count, 128))
         n = (standard * (1.0 + mod[s, 1:2, :]) + mod[s, 0:1, :]).astype(BF16)
         copies[s][0].wait()
-        copies[s][1].start()
-        if later is not None:
-            copies[later][0].start()
+        for copy in later:
+            copy.start()
         pq = dot(n, wq[s, 0])
         pk = dot(n, wq[s, 1])
         pv = dot(n, wq[s, 2])
         proj[at : at + count, 0:WIDTH] = pq
         proj[at : at + count, WIDTH : 2 * WIDTH] = pk
+        for source, target in ((proj, proj_out), (xhat, xhat_out), (rstd, rstd_out)):
+            results.send(source.at[pl.ds(at, count)], target.at[pl.ds(at, count)])
         copies[s][1].wait()
         g = dot_nt(e, wo[s])
         kv, qg = [], []
@@ -138,7 +160,7 @@
     dy = rows(2)
     text = jnp.concatenate([spread_text(gat[c, 3 * SHARE :, :].astype(F32)) for c in range(4)], 0).astype(BF16).T.astype(F32)
     e_img = (mod[0, 2:3, :] * dy).astype(BF16)
-    n, kv, qg = stream(0, rows(0), e_img, 0, 2)
+    n, kv, qg = stream(0, rows(0), e_img, 0, (copies[2][1], copies[1][0]))
     for h in range(HEADS):
         for t in range(MAIN_PARTS):
             to = MAIN_PARTS * h + t
@@ -146,20 +168,15 @@
             last = min(IMG, MAIN_Q * (t + 1))
             send[to, IMG + TXT : IMG + TXT + last - MAIN_Q * t, :] = qg[h][MAIN_Q * t : last]
     e_ctl = mod[2, 2:3, :] * dy
-    n, kv, qg = stream(2, rows(1), e_ctl.astype(BF16), IMG + TXT, 1)
+    n, kv, qg = stream(2, rows(1), e_ctl.astype(BF16), IMG + TXT, (copies[1][1],))
     for h in range(HEADS):
         for u in range(CTL_PARTS):
-            to = CTL_AT + CTL_PARTS * h + u
-            send[to, 0:IMG, :] = kv[h]
-            send[to, IMG:CHUNK, :] = qg[h][CTL_Q * u : CTL_Q * (u + 1)]
-    e_txt = (mod[1, 2:3, :] * text[TXT : 2 * TXT]).astype(BF16)
-    unused, kv, qg = stream(1, text[0:TXT], e_txt, IMG, None)
-    for h in range(HEADS):
-        for t in range(MAIN_PARTS):
-            send[MAIN_PARTS * h + t, IMG : IMG + TXT, :] = kv[h]
-        send[MAIN_PARTS * h + 2, CHUNK - TXT : CHUNK, :] = qg[h]
-    for to in range(CTL_AT + CTL_PARTS * HEADS, BLOCKS):
-        send[to] = jnp.zeros((CHUNK, 128), BF16)
+            to = CTL_PARTS * h + u
+            send_ctl[to, 0:IMG, :] = kv[h]
+            send_ctl[to, IMG:CHUNK, :] = qg[h][CTL_Q * u : CTL_Q * (u + 1)]
+    for to in range(CTL_PARTS * HEADS, BLOCKS - CTL_AT):
+        send_ctl[to] = jnp.zeros((CHUNK, 128), BF16)
+    results.send(send_ctl, send_out.at[pl.ds(CTL_AT, BLOCKS - CTL_AT)])
     n_t, e_t = n.T, e_ctl.astype(BF16).T
     nz[...] = n_t.reshape(4, SHARE, IMG)
     n_t, e_t = n_t.astype(F32), e_t.astype(F32)
@@ -168,9 +185,17 @@
             pieces = [values[SHARE * z + PIECE * y : SHARE * z + PIECE * (y + 1)] for z in range(4)]
             ny[y, j] = jnp.concatenate(pieces, 0).astype(BF16)
     for d, out in enumerate((nz0, nz1, nz2, nz3)):
-        out[...] = nz[lax.rem(lax.axis_index("z") + d, 4)]
+        results.send(nz.at[lax.rem(lax.axis_index("z") + d, 4)], out)
     for d, out in enumerate((ny0, ny1, ny2, ny3)):
-        out[...] = ny[lax.rem(lax.axis_index("y") + d, 4)]
+        results.send(ny.at[lax.rem(lax.axis_index("y") + d, 4)], out)
+    e_txt = (mod[1, 2:3, :] * text[TXT : 2 * TXT]).astype(BF16)
+    unused, kv, qg = stream(1, text[0:TXT], e_txt, IMG, ())
+    for h in range(HEADS):
+        for t in range(MAIN_PARTS):
+            send[MAIN_PARTS * h + t, IMG : IMG + TXT, :] = kv[h]
+        send[MAIN_PARTS * h + 2, CHUNK - TXT : CHUNK, :] = qg[h]
+    results.send(send, send_out.at[pl.ds(0, CTL_AT)])
+    results.finish()
 
 
 def attention_kernel(role, recv, after, dkv_out, odq, kv, kt, vt, qg, probs, dkv):
@@ -225,7 +250,7 @@
         state = (jnp.zeros((8, TQ), F32), jnp.zeros((HEAD, TQ), F32))
         state = lax.fori_loop(
             0, IMAGE_KEYS // TK, lambda j, c: forward(pl.multiple_of(j * TK, TK), c, False), state,
-            unroll=4,
+            unroll=8,
         )
         total, o_t = lax.fori_loop(0, is_main, lambda j, c: forward(IMAGE_KEYS, c, True), state)
         inverse = 1.0 / jnp.sum(total, axis=0, keepdims=True)
@@ -240,7 +265,7 @@
 
         dq_t = jnp.zeros((HEAD, TQ), F32)
         dq_t = lax.fori_loop(
-            0, IMAGE_KEYS // TK, lambda j, c: backward(pl.multiple_of(j * TK, TK), c), dq_t, unroll=4
+            0, IMAGE_KEYS // TK, lambda j, c: backward(pl.multiple_of(j * TK, TK), c), dq_t, unroll=8
         )
         dq_t = lax.fori_loop(0, is_main, lambda j, c: backward(IMAGE_KEYS, c), dq_t)
         odq[pl.ds(q_at, TQ), :] = jnp.concatenate([o_t, dq_t * 0.125], 0).astype(BF16).T
@@ -330,10 +355,17 @@
 
 
 def post_kernel(
-    recv, proj, gains, by_z, by_y, xhat, rstd, mod, wq_img, wq_txt, wq_ctl, wo_img, wo_txt, wo_ctl,
-    slabs,
-    wq, wo, main, sems,
+    recv, proj, gains, by_z, by_y, xhat_in, rstd_in, mod, wq_img, wq_txt, wq_ctl, wo_img, wo_txt, wo_ctl,
+    mine0, mine1, theirs0, theirs1,
+    wq, wo, main, xhat, rstd, slabs, sems, in_sems, out_sems,
 ):
+    arrivals = [
+        pltpu.make_async_copy(xhat_in, xhat, in_sems.at[0]),
+        pltpu.make_async_copy(rstd_in, rstd, in_sems.at[1]),
+    ]
+    for copy in arrivals:
+        copy.start()
+    results = Results(out_sems)
     copies = weight_copies((wq_img, wq_txt, wq_ctl, wo_img, wo_txt, wo_ctl), wq, wo, sems)
     for copy in (copies[2][0], copies[2][1], copies[0][0]):
         copy.start()
@@ -349,28 +381,33 @@
     def joint(at, count):
         return [main[at : at + count, j * WIDTH : (j + 1) * WIDTH] for j in range(4)]
 
+    def leave(at, count):
+        for other, out in enumerate((mine0, theirs0, mine1, theirs1)):
+            results.send(slabs.at[lax.axis_index("tp") ^ other, pl.ds(at, count)], out.at[pl.ds(at, count)])
+
     head_back_main(recv, proj, gains, main)
+    for copy in arrivals:
+        copy.wait()
     u, y_ctl = stream(2, [r[:, j * WIDTH : (j + 1) * WIDTH] for r in (by_z, by_y) for j in range(2)], IMG + TXT, (copies[0][1], copies[1][0]))
     slabs[:, 2 * SHARE : 3 * SHARE, :] = slab(u)
+    leave(2 * SHARE, SHARE)
     u, y = stream(0, joint(0, IMG), 0, (copies[1][1],))
     slabs[:, SHARE : 2 * SHARE, :] = slab(u)
     slabs[:, 0:SHARE, :] = slab(y + y_ctl)
+    leave(0, 2 * SHARE)
     u, y = stream(1, joint(IMG, TXT), IMG, ())
     text = jnp.concatenate([y, u, jnp.zeros((IMG - 2 * TXT, D), F32)], 0).astype(BF16).T.astype(F32)
     for c in range(4):
         slabs[c, 3 * SHARE :, :] = pack_text(text[SHARE * c : SHARE * (c + 1)]).astype(BF16)
+    leave(3 * SHARE, PIECE)
+    results.finish()
 
 
 def weight_kernel(
     nz0, nz1, nz2, nz3, ny0, ny1, ny2, ny3, bz0, bz1, bz2, bz3, by0, by1, by2, by3,
-    slabs, out_z, out_y0, out_y1, out_y2, out_y3, mine0, mine1, theirs0, theirs1,
+    theirs0, theirs1, out_z, out_y0, out_y1, out_y2, out_y3, same0, same1,
     chunks,
 ):
-    tp = lax.axis_index("tp")
-    mine0[...] = slabs[tp]
-    mine1[...] = slabs[tp ^ 2]
-    theirs0[...] = slabs[tp ^ 1]
-    theirs1[...] = slabs[tp ^ 3]
     nz, ny = (nz0, nz1, nz2, nz3), (ny0, ny1, ny2, ny3)
     bz, by = (bz0, bz1, bz2, bz3), (by0, by1, by2, by3)
     qk = dot(jnp.concatenate([r[...] for r in nz], 1), jnp.concatenate([r[...] for r in bz], 0))
@@ -459,15 +496,22 @@
             shape((2 * IMG + TXT, D), F32),
             shape((2 * IMG + TXT, 128), F32),
         ] + [shape((SHARE, IMG), BF16)] * 4 + [shape((2, SHARE, IMG), BF16)] * 4,
-        in_specs=[VMEM] * 6 + [HBM] * 6,
-        out_specs=[VMEM] * 12,
+        in_specs=[HBM] * 4 + [VMEM] * 2 + [HBM] * 6,
+        out_specs=[ANY] * 12,
         scratch_shapes=[
             pltpu.VMEM((3, 3, D, WIDTH), BF16),
             pltpu.VMEM((3, WIDTH, D), BF16),
             pltpu.VMEM((4, ROWS, IMG), BF16),
+            pltpu.VMEM((CTL_AT, CHUNK, 128), BF16),
+            pltpu.VMEM((BLOCKS - CTL_AT, CHUNK, 128), BF16),
+            pltpu.VMEM((2 * IMG + TXT, 2 * WIDTH), F32),
+            pltpu.VMEM((2 * IMG + TXT, D), F32),
+            pltpu.VMEM((2 * IMG + TXT, 128), F32),
             pltpu.VMEM((4, SHARE, IMG), BF16),
             pltpu.VMEM((4, 2, SHARE, IMG), BF16),
             pltpu.SemaphoreType.DMA((6,)),
+            pltpu.SemaphoreType.DMA((4,)),
+            pltpu.SemaphoreType.DMA((19,)),
         ],
         compiler_params=params(56),
         name="pre",
@@ -514,16 +558,21 @@
     )(back, proj, gains)
     blocks_z = shifted([by_z] * 4, "z")
     blocks_y = shifted([by_y] * 4, "y")
-    slabs = pl.pallas_call(
+    mine0, mine1, theirs0, theirs1 = pl.pallas_call(
         post_kernel,
-        out_shape=shape((4, ROWS, IMG), BF16),
-        in_specs=[VMEM] * 8 + [HBM] * 6,
-        out_specs=VMEM,
+        out_shape=[rows] * 4,
+        in_specs=[VMEM] * 5 + [HBM] * 2 + [VMEM] + [HBM] * 6,
+        out_specs=[ANY] * 4,
         scratch_shapes=[
             pltpu.VMEM((3, 3, D, WIDTH), BF16),
             pltpu.VMEM((3, WIDTH, D), BF16),
             pltpu.VMEM((IMG + TXT, 4 * WIDTH), BF16),
+            pltpu.VMEM((2 * IMG + TXT, D), F32),
+            pltpu.VMEM((2 * IMG + TXT, 128), F32),
+            pltpu.VMEM((4, ROWS, IMG), BF16),
             pltpu.SemaphoreType.DMA((6,)),
+            pltpu.SemaphoreType.DMA((2,)),
+            pltpu.SemaphoreType.DMA((12,)),
         ],
         compiler_params=params(54),
         cost_estimate=pl.CostEstimate(flops=14_000_000_000, bytes_accessed=30_000_000, transcendentals=0),
@@ -531,15 +580,16 @@
     )(back, proj, gains, by_z, by_y, xhat, rstd, mod, *weights)
     terms_z, *outs = pl.pallas_call(
         weight_kernel,
-        out_shape=[shape((4, PIECE, 2 * WIDTH), BF16)] + [shape((PIECE, 2 * WIDTH), BF16)] * 4 + [rows] * 4,
-        in_specs=[VMEM] * 17,
-        out_specs=[VMEM] * 9,
+        out_shape=[shape((4, PIECE, 2 * WIDTH), BF16)] + [shape((PIECE, 2 * WIDTH), BF16)] * 4 + [rows] * 2,
+        in_specs=[VMEM] * 16 + [ANY] * 2,
+        out_specs=[VMEM] * 5 + [ANY] * 2,
+        input_output_aliases={16: 5, 17: 6},
         scratch_shapes=[pltpu.VMEM((4, PIECE, 2 * WIDTH), BF16)],
         compiler_params=params(24),
         cost_estimate=pl.CostEstimate(flops=3_000_000_000, bytes_accessed=5_000_000, transcendentals=0),
         name="weight",
-    )(*nz, *ny, *blocks_z, *blocks_y, slabs)
-    terms_y, (mine0, mine1, theirs0, theirs1) = outs[0:4], outs[4:8]
+    )(*nz, *ny, *blocks_z, *blocks_y, theirs0, theirs1)
+    terms_y, (theirs0, theirs1) = outs[0:4], outs[4:6]
     got1 = lax.ppermute(theirs1, "tp", other_core)
     got0 = lax.ppermute(theirs0, "tp", other_core)
     passed = (mine1.astype(F32) + got1.astype(F32)).astype(BF16)

time: 201 us -> 196 us (0.975)
  Pallas kernels: 67.3 us -> 64.5 us
    unnamed x56 -> x52, local copies, waits for them, and re-layouts: 8 us -> 6.57 us
  transfers between devices with their start and end apart: 24 -> 24, of which waited for: 7 -> 7; matrix products, arithmetic and copies ran while one was open for 1% -> 1% of each run, Pallas kernels for 21% -> 20%
where the time goes in v3:
time: 196 us; the launch traced here: 195 us
  Pallas kernels  64.5 us (33%)
  waiting for transfers between devices  46.1 us (24%)
  starting transfers between devices  42.6 us (22%)
  blocking collectives  31.5 us (16%)
  local copies, waits for them, and re-layouts  6.57 us (3%)
  other arithmetic  2.11 us (1%)
    all_to_all x1, blocking collectives, per_device(): back = lax.all_to_all(back, seq, 0, 0, tiled=True)  31.5 us
    ppermute x15, waiting for transfers between devices, shifted(): lax.ppermute(parts[d], axis, [(i, (i + d) % 4) for i in range(4)])  25.3 us
    pallas_call x1, Pallas kernels, per_device(): pl.pallas_call(attention_kernel, out_shape=[shape((keys, 128), BF16), sha...  24.8 us
    ppermute x15, starting transfers between devices, shifted(): lax.ppermute(parts[d], axis, [(i, (i + d) % 4) for i in range(4)])  22.9 us
    pallas_call x1, Pallas kernels, per_device(): pl.pallas_call(pre_kernel, out_shape=[shape((BLOCKS, CHUNK, 128), BF16),...  16.3 us
    pallas_call x1, Pallas kernels, per_device(): pl.pallas_call(post_kernel, out_shape=[rows] * 4, in_specs=[VMEM] * 5 + [...  13.8 us
    ppermute x1, waiting for transfers between devices, per_device(): from_chip = lax.ppermute(own, 'tp', other_chip)  11.7 us
    all_to_all x1, starting transfers between devices, per_device(): recv = lax.all_to_all(send, seq, 0, 0, tiled=True)  9.63 us
  transfers between devices with their start and end apart: 24, of which 7 were waited for; matrix products, arithmetic and copies ran while one was open for 1% of the time, Pallas kernels for 20%

profile of v3, /device:TPU:0, one launch (start us, length us, event | category | flops | bytes accessed | tf_op | source)
XLA Modules:
  0.0 195.1 jit_solution(7732569778655363498)
XLA Ops:
  0.6 1.9 pack.1.in0
  2.6 3.2 %collective-permute-start.1 = (bf16[1976,128]{1,0:T(8,128)(2,1)}, bf16[1976,128]{1,0:T(8,128)(2,1)S(1)}, u32[]{:S(2)}, u32[]{:S(2)}) collective-permute-start(bf16[1976,128]{1,0:T(8,128)(2,1)} %pack.1.in0), channel_id=1, source_target_pairs={{0,2},{1,3},{2,0},{3,1},{4,6},{5,7},{6,4},{7,5},{8,10},{9,11},{10,... | collective-permute-start | bytes 1517576 | tf_op jit(solution)/shard_map/ppermute | solution.py:487
  5.8 11.7 %collective-permute-done.1.in2 = bf16[1976,128]{1,0:T(8,128)(2,1)S(1)} collective-permute-done((bf16[1976,128]{1,0:T(8,128)(2,1)}, bf16[1976,128]{1,0:T(8,128)(2,1)S(1)}, u32[]{:S(2)}, u32[]{:S(2)}) %collective-permute-start.1) | collective-permute-done | bytes 505888 | tf_op jit(solution)/shard_map/ppermute | solution.py:487
  17.5 1.9 collective-permute-done.2.in3
  20.2 16.3 %pre.1 = (bf16[32,192,128]{2,1,0:T(8,128)(2,1)}, f32[272,768]{1,0:T(8,128)}, f32[272,2432]{1,0:T(8,128)}, f32[272,128]{1,0:T(8,128)}, bf16[608,128]{1,0:T(8,128)...) custom-call(bf16[1976,128]{1,0:T(8,128)(2,1)} %pack.1.in0, ...), custom_call_target="tpu_custom_call" | custom-call | tf_op jit(solution)/shard_map/pre/pallas_call | solution.py:491
  36.5 9.6 %all-to-all-start = ((bf16[32,192,128]{2,1,0:T(8,128)(2,1)}), bf16[32,192,128]{2,1,0:T(8,128)(2,1)S(1)}, u32[]{:S(2)}, u32[]{:S(2)}) async-start(bf16[32,192,128]{2,1,0:T(8,128)(2,1)} %get-tuple-element.43), calls=%async_computation | async-start | bytes 3145728 | tf_op jit(solution)/shard_map/all_to_all | solution.py:520
  46.2 3.1 %collective-permute-start.3 = (bf16[608,128]{1,0:T(8,128)(2,1)S(1)}, bf16[608,128]{1,0:T(8,128)(2,1)S(1)}, u32[]{:S(2)}, u32[]{:S(2)}) collective-permute-start(bf16[608,128]{1,0:T(8,128)(2,1)S(1)} %copy-done.25), channel_id=1, source_target_pairs={{0,96},{32,0},{64,32},{96,64},{1,97},{33,1},{65,33},{97,65},{2,98}... | collective-permute-start | bytes 466952 | tf_op jit(solution)/shard_map/ppermute | solution.py:457
  50.0 2.3 %collective-permute-start.5 = (bf16[608,128]{1,0:T(8,128)(2,1)S(1)}, bf16[608,128]{1,0:T(8,128)(2,1)S(1)}, u32[]{:S(2)}, u32[]{:S(2)}) collective-permute-start(bf16[608,128]{1,0:T(8,128)(2,1)S(1)} %copy-done.24), channel_id=1, source_target_pairs={{0,64},{32,96},{64,0},{96,32},{1,65},{33,97},{65,1},{97,33},{2,66}... | collective-permute-start | bytes 466952 | tf_op jit(solution)/shard_map/ppermute | solution.py:457
  52.3 1.5 collective-permute-start.6
  53.8 2.7 %collective-permute-start.7 = (bf16[2,608,128]{2,1,0:T(8,128)(2,1)}, bf16[2,608,128]{2,1,0:T(8,128)(2,1)S(1)}, u32[]{:S(2)}, u32[]{:S(2)}) collective-permute-start(bf16[2,608,128]{2,1,0:T(8,128)(2,1)} %get-tuple-element.50), channel_id=1, source_target_pairs={{0,16},{8,24},{16,0},{24,8},{1,17},{9,25},{17,1},{25,9},{2,18},{10... | collective-permute-start | bytes 933896 | tf_op jit(solution)/shard_map/ppermute | solution.py:457
  56.5 13.3 %collective-permute-done.3.after.nz3 = bf16[608,128]{1,0:T(8,128)(2,1)S(1)} collective-permute-done((bf16[608,128]{1,0:T(8,128)(2,1)S(1)}, bf16[608,128]{1,0:T(8,128)(2,1)S(1)}, u32[]{:S(2)}, u32[]{:S(2)}) %collective-permute-start.3) | collective-permute-done | bytes 155680 | tf_op jit(solution)/shard_map/ppermute | solution.py:457
  69.8 2.6 %collective-permute-start.8 = (bf16[2,608,128]{2,1,0:T(8,128)(2,1)S(1)}, bf16[2,608,128]{2,1,0:T(8,128)(2,1)S(1)}, u32[]{:S(2)}, u32[]{:S(2)}) collective-permute-start(bf16[2,608,128]{2,1,0:T(8,128)(2,1)S(1)} %copy-done.23), channel_id=1, source_target_pairs={{0,24},{8,0},{16,8},{24,16},{1,25},{9,1},{17,9},{25,17},{2,26},{10... | collective-permute-start | bytes 933896 | tf_op jit(solution)/shard_map/ppermute | solution.py:457
  72.4 24.8 %attention.1 = (bf16[4608,128]{1,0:T(8,128)(2,1)S(1)}, bf16[2048,128]{1,0:T(8,128)(2,1)S(1)}) custom-call(s32[2]{0:T(128)S(1)} %pad_add_fusion.role, bf16[32,192,128]{2,1,0:T(8,128)(2,1)S(1)} %all-to-all-done.recv, bf16[608,128]{1,0:T(8,128)(2,1)S(1)} %collective-permute-done.3.after.nz3), custom_call_target="tpu_custom_call" | custom-call | flops 40000000000 | bytes 3200000 | tf_op jit(solution)/shard_map/attention/pallas_call | solution.py:524
  97.9 31.5 %all_to_all.15.recv = bf16[32,192,128]{2,1,0:T(8,128)(2,1)S(1)} all-to-all(bf16[32,192,128]{2,1,0:T(8,128)(2,1)S(1)} %scatter.1), channel_id=1, replica_groups=mesh['z'=4,'y'=4,'w'=2,'tp'=4] {'z','y','w'}, dimensions={0} | all-to-all | bytes 3145728 | tf_op jit(solution)/shard_map/all_to_all | solution.py:549
  129.4 2.5 %head_back_ctl.1 = (bf16[128,768]{1,0:T(8,128)(2,1)S(1)}, bf16[128,768]{1,0:T(8,128)(2,1)S(1)}) custom-call(bf16[32,192,128]{2,1,0:T(8,128)(2,1)S(1)} %all_to_all.15.recv, f32[272,768]{1,0:T(8,128)S(1)} %copy-done.1, f32[3,2,64]{2,1,0:T(2,128)S(1)} %copy-done.9), custom_call_target="tpu_custom_call" | custom-call | tf_op jit(solution)/shard_map/head_back_ctl/pallas_call | solution.py:551
  134.2 1.2 collective-permute-start.14
  135.5 1.4 collective-permute-start.13
  136.8 1.6 collective-permute-done.11.bz3
  139.1 13.8 %post.1 = (bf16[1976,128]{1,0:T(8,128)(2,1)}, bf16[1976,128]{1,0:T(8,128)(2,1)}, bf16[1976,128]{1,0:T(8,128)(2,1)}, bf16[1976,128]{1,0:T(8,128)(2,1)}) custom-call(bf16[32,192,128]{2,1,0:T(8,128)(2,1)} %copy-done, f32[272,768]{1,0:T(8,128)} %get-tuple-element.52.proj, f32[3,2,64]{2,1,0:T(2,128)} %gains.5, bf16[128,768]{1,0:T(8,128)(2,1)} %copy-done.13, ...), custom_call_target="tpu_custom_call" | custom-call | flops 14000000000 | bytes 30000000 | tf_op jit(solution)/shard_map/post/pallas_call | solution.py:561
  152.9 0.9 copy-done.14
  153.9 0.9 copy-done.16
  154.8 2.2 %weight.1 = (bf16[4,152,768]{2,1,0:T(8,128)(2,1)}, bf16[152,768]{1,0:T(8,128)(2,1)S(1)}, bf16[152,768]{1,0:T(8,128)(2,1)}, bf16[152,768]{1,0:T(8,128)(2,1)S(1)},...) custom-call(bf16[608,128]{1,0:T(8,128)(2,1)S(1)} %copy-done.17, ...), custom_call_target="tpu_custom_call", output_to_operand_aliasing={{5}: (16, {}), {6}: (17, {})} | custom-call | flops 3000000000 | bytes 5000000 | tf_op jit(solution)/shard_map/weight/pallas_call | solution.py:581
  158.4 4.1 %all-to-all-start.2 = ((bf16[4,152,768]{2,1,0:T(8,128)(2,1)}), bf16[4,152,768]{2,1,0:T(8,128)(2,1)S(1)}, u32[]{:S(2)}, u32[]{:S(2)}) async-start(bf16[4,152,768]{2,1,0:T(8,128)(2,1)} %get-tuple-element.70), calls=%async_computation.2 | async-start | bytes 1867776 | tf_op jit(solution)/shard_map/all_to_all | solution.py:598
  163.4 2.0 %add_convert_fusion = bf16[1976,128]{1,0:T(8,128)(2,1)} fusion(bf16[1976,128]{1,0:T(8,128)(2,1)} %copy-done.22, bf16[1976,128]{1,0:T(8,128)(2,1)S(1)} %copy-done.18), kind=kLoop, calls=%fused_computation | loop fusion | flops 1011712 | bytes 1517568 | tf_op jit(solution)/shard_map/convert_element_type | solution.py:595
  165.5 2.7 %collective-permute-start.17 = (bf16[1976,128]{1,0:T(8,128)(2,1)}, bf16[1976,128]{1,0:T(8,128)(2,1)S(1)}, u32[]{:S(2)}, u32[]{:S(2)}) collective-permute-start(bf16[1976,128]{1,0:T(8,128)(2,1)} %add_convert_fusion), channel_id=1, source_target_pairs={{0,2},{1,3},{2,0},{3,1},{4,6},{5,7},{6,4},{7,5},{8,10},{9,11},{10,... | collective-permute-start | bytes 1517576 | tf_op jit(solution)/shard_map/ppermute | solution.py:596
  168.1 1.1 collective-permute-start.18
  169.2 3.6 %collective-permute-start.19 = (bf16[152,768]{1,0:T(8,128)(2,1)}, bf16[152,768]{1,0:T(8,128)(2,1)S(1)}, u32[]{:S(2)}, u32[]{:S(2)}) collective-permute-start(bf16[152,768]{1,0:T(8,128)(2,1)} %copy-done.12), channel_id=1, source_target_pairs={{0,64},{32,96},{64,0},{96,32},{1,65},{33,97},{65,1},{97,33},{2,66}... | collective-permute-start | bytes 700424 | tf_op jit(solution)/shard_map/ppermute | solution.py:457
  173.4 4.2 %collective-permute-done.18.y1 = bf16[152,768]{1,0:T(8,128)(2,1)S(1)} collective-permute-done((bf16[152,768]{1,0:T(8,128)(2,1)}, bf16[152,768]{1,0:T(8,128)(2,1)S(1)}, u32[]{:S(2)}, u32[]{:S(2)}) %collective-permute-start.18) | collective-permute-done | bytes 233504 | tf_op jit(solution)/shard_map/ppermute | solution.py:457
  177.6 6.2 %collective-permute-done.19.y2 = bf16[152,768]{1,0:T(8,128)(2,1)S(1)} collective-permute-done((bf16[152,768]{1,0:T(8,128)(2,1)}, bf16[152,768]{1,0:T(8,128)(2,1)S(1)}, u32[]{:S(2)}, u32[]{:S(2)}) %collective-permute-start.19) | collective-permute-done | bytes 233504 | tf_op jit(solution)/shard_map/ppermute | solution.py:457
  184.5 0.9 copy-done.6
  185.9 7.2 %collective-permute-done.21.other = bf16[76,1536]{1,0:T(8,128)(2,1)S(1)} collective-permute-done((bf16[76,1536]{1,0:T(8,128)(2,1)S(1)}, bf16[76,1536]{1,0:T(8,128)(2,1)S(1)}, u32[]{:S(2)}, u32[]{:S(2)}) %collective-permute-start.21) | collective-permute-done | bytes 233504 | tf_op jit(solution)/shard_map/ppermute | solution.py:607
  193.9 1.1 final.1
  (81 shorter events, 9.4 us)
Async XLA Ops:
  2.6 14.9 %collective-permute-start.1 = (bf16[1976,128]{1,0:T(8,128)(2,1)}, bf16[1976,128]{1,0:T(8,128)(2,1)S(1)}, u32[]{:S(2)}, u32[]{:S(2)}) collective-permute-start(bf16[1976,128]{1,0:T(8,128)(2,1)} %pack.1.in0), channel_id=1, source_target_pairs={{0,2},{1,3},{2,0},{3,1},{4,6},{5,7},{6,4},{7,5},{8,10},{9,11},{10,... | collective-permute-start | bytes 1517576 | tf_op jit(solution)/shard_map/ppermute | solution.py:487
  5.8 11.7 %collective-permute-start = (bf16[1976,128]{1,0:T(8,128)(2,1)}, bf16[1976,128]{1,0:T(8,128)(2,1)S(1)}, u32[]{:S(2)}, u32[]{:S(2)}) collective-permute-start(bf16[1976,128]{1,0:T(8,128)(2,1)} %pack.1.in0), channel_id=1, source_target_pairs={{0,1},{1,0},{2,3},{3,2},{4,5},{5,4},{6,7},{7,6},{8,9},{9,8},{10,11... | collective-permute-start | bytes 1517576 | tf_op jit(solution)/shard_map/ppermute | solution.py:488
  17.5 1.9 collective-permute-start.2
  36.5 33.3 %copy-start.23 = (bf16[2,608,128]{2,1,0:T(8,128)(2,1)S(1)}, bf16[2,608,128]{2,1,0:T(8,128)(2,1)}, u32[]{:S(2)}) copy-start(bf16[2,608,128]{2,1,0:T(8,128)(2,1)} %get-tuple-element.51) | copy-start | bytes 933892
  36.5 35.8 %all-to-all-start = ((bf16[32,192,128]{2,1,0:T(8,128)(2,1)}), bf16[32,192,128]{2,1,0:T(8,128)(2,1)S(1)}, u32[]{:S(2)}, u32[]{:S(2)}) async-start(bf16[32,192,128]{2,1,0:T(8,128)(2,1)} %get-tuple-element.43), calls=%async_computation | async-start | bytes 3145728 | tf_op jit(solution)/shard_map/all_to_all | solution.py:520
  46.2 23.6 %collective-permute-start.3 = (bf16[608,128]{1,0:T(8,128)(2,1)S(1)}, bf16[608,128]{1,0:T(8,128)(2,1)S(1)}, u32[]{:S(2)}, u32[]{:S(2)}) collective-permute-start(bf16[608,128]{1,0:T(8,128)(2,1)S(1)} %copy-done.25), channel_id=1, source_target_pairs={{0,96},{32,0},{64,32},{96,64},{1,97},{33,1},{65,33},{97,65},{2,98}... | collective-permute-start | bytes 466952 | tf_op jit(solution)/shard_map/ppermute | solution.py:457
  50.0 47.1 %collective-permute-start.4 = (bf16[608,128]{1,0:T(8,128)(2,1)}, bf16[608,128]{1,0:T(8,128)(2,1)S(1)}, u32[]{:S(2)}, u32[]{:S(2)}) collective-permute-start(bf16[608,128]{1,0:T(8,128)(2,1)} %get-tuple-element.47), channel_id=1, source_target_pairs={{0,32},{32,64},{64,96},{96,0},{1,33},{33,65},{65,97},{97,1},{2,34}... | collective-permute-start | bytes 466952 | tf_op jit(solution)/shard_map/ppermute | solution.py:457
  50.0 47.1 %collective-permute-start.5 = (bf16[608,128]{1,0:T(8,128)(2,1)S(1)}, bf16[608,128]{1,0:T(8,128)(2,1)S(1)}, u32[]{:S(2)}, u32[]{:S(2)}) collective-permute-start(bf16[608,128]{1,0:T(8,128)(2,1)S(1)} %copy-done.24), channel_id=1, source_target_pairs={{0,64},{32,96},{64,0},{96,32},{1,65},{33,97},{65,1},{97,33},{2,66}... | collective-permute-start | bytes 466952 | tf_op jit(solution)/shard_map/ppermute | solution.py:457
  52.3 44.8 %collective-permute-start.6 = (bf16[2,608,128]{2,1,0:T(8,128)(2,1)}, bf16[2,608,128]{2,1,0:T(8,128)(2,1)S(1)}, u32[]{:S(2)}, u32[]{:S(2)}) collective-permute-start(bf16[2,608,128]{2,1,0:T(8,128)(2,1)} %get-tuple-element.49), channel_id=1, source_target_pairs={{0,8},{8,16},{16,24},{24,0},{1,9},{9,17},{17,25},{25,1},{2,10},{10... | collective-permute-start | bytes 933896 | tf_op jit(solution)/shard_map/ppermute | solution.py:457
  53.8 43.4 %collective-permute-start.7 = (bf16[2,608,128]{2,1,0:T(8,128)(2,1)}, bf16[2,608,128]{2,1,0:T(8,128)(2,1)S(1)}, u32[]{:S(2)}, u32[]{:S(2)}) collective-permute-start(bf16[2,608,128]{2,1,0:T(8,128)(2,1)} %get-tuple-element.50), channel_id=1, source_target_pairs={{0,16},{8,24},{16,0},{24,8},{1,17},{9,25},{17,1},{25,9},{2,18},{10... | collective-permute-start | bytes 933896 | tf_op jit(solution)/shard_map/ppermute | solution.py:457
  69.8 27.4 %collective-permute-start.8 = (bf16[2,608,128]{2,1,0:T(8,128)(2,1)S(1)}, bf16[2,608,128]{2,1,0:T(8,128)(2,1)S(1)}, u32[]{:S(2)}, u32[]{:S(2)}) collective-permute-start(bf16[2,608,128]{2,1,0:T(8,128)(2,1)S(1)} %copy-done.23), channel_id=1, source_target_pairs={{0,24},{8,0},{16,8},{24,16},{1,25},{9,1},{17,9},{25,17},{2,26},{10... | collective-permute-start | bytes 933896 | tf_op jit(solution)/shard_map/ppermute | solution.py:457
  97.8 31.6 %copy-start.1 = (f32[272,768]{1,0:T(8,128)S(1)}, f32[272,768]{1,0:T(8,128)}, u32[]{:S(2)}) copy-start(f32[272,768]{1,0:T(8,128)} %get-tuple-element.52.proj) | copy-start | bytes 2506756
  97.9 31.6 %copy-start.9 = (f32[3,2,64]{2,1,0:T(2,128)S(1)}, f32[3,2,64]{2,1,0:T(2,128)}, u32[]{:S(2)}) copy-start(f32[3,2,64]{2,1,0:T(2,128)} %gains.5) | copy-start | bytes 4612
  132.0 6.5 %collective-permute-start.11 = (bf16[128,768]{1,0:T(8,128)(2,1)S(1)}, bf16[128,768]{1,0:T(8,128)(2,1)S(1)}, u32[]{:S(2)}, u32[]{:S(2)}) collective-permute-start(bf16[128,768]{1,0:T(8,128)(2,1)S(1)} %get-tuple-element.53.by_z.bz0), channel_id=1, source_target_pairs={{0,96},{32,0},{64,32},{96,64},{1,97},{33,1},{65,33},{97,65},{2,98}... | collective-permute-start | bytes 589832 | tf_op jit(solution)/shard_map/ppermute | solution.py:457
  132.8 20.0 %collective-permute-start.10 = (bf16[128,768]{1,0:T(8,128)(2,1)S(1)}, bf16[128,768]{1,0:T(8,128)(2,1)S(1)}, u32[]{:S(2)}, u32[]{:S(2)}) collective-permute-start(bf16[128,768]{1,0:T(8,128)(2,1)S(1)} %get-tuple-element.53.by_z.bz0), channel_id=1, source_target_pairs={{0,64},{32,96},{64,0},{96,32},{1,65},{33,97},{65,1},{97,33},{2,66}... | collective-permute-start | bytes 589832 | tf_op jit(solution)/shard_map/ppermute | solution.py:457
  133.4 19.5 %collective-permute-start.9 = (bf16[128,768]{1,0:T(8,128)(2,1)S(1)}, bf16[128,768]{1,0:T(8,128)(2,1)S(1)}, u32[]{:S(2)}, u32[]{:S(2)}) collective-permute-start(bf16[128,768]{1,0:T(8,128)(2,1)S(1)} %get-tuple-element.53.by_z.bz0), channel_id=1, source_target_pairs={{0,32},{32,64},{64,96},{96,0},{1,33},{33,65},{65,97},{97,1},{2,34}... | collective-permute-start | bytes 589832 | tf_op jit(solution)/shard_map/ppermute | solution.py:457
  134.2 18.6 %collective-permute-start.14 = (bf16[128,768]{1,0:T(8,128)(2,1)S(1)}, bf16[128,768]{1,0:T(8,128)(2,1)S(1)}, u32[]{:S(2)}, u32[]{:S(2)}) collective-permute-start(bf16[128,768]{1,0:T(8,128)(2,1)S(1)} %get-tuple-element.54.by_y.by0), channel_id=1, source_target_pairs={{0,24},{8,0},{16,8},{24,16},{1,25},{9,1},{17,9},{25,17},{2,26},{10... | collective-permute-start | bytes 589832 | tf_op jit(solution)/shard_map/ppermute | solution.py:457
  135.5 17.4 %collective-permute-start.13 = (bf16[128,768]{1,0:T(8,128)(2,1)S(1)}, bf16[128,768]{1,0:T(8,128)(2,1)S(1)}, u32[]{:S(2)}, u32[]{:S(2)}) collective-permute-start(bf16[128,768]{1,0:T(8,128)(2,1)S(1)} %get-tuple-element.54.by_y.by0), channel_id=1, source_target_pairs={{0,16},{8,24},{16,0},{24,8},{1,17},{9,25},{17,1},{25,9},{2,18},{10... | collective-permute-start | bytes 589832 | tf_op jit(solution)/shard_map/ppermute | solution.py:457
  138.5 14.4 %collective-permute-start.12 = (bf16[128,768]{1,0:T(8,128)(2,1)S(1)}, bf16[128,768]{1,0:T(8,128)(2,1)S(1)}, u32[]{:S(2)}, u32[]{:S(2)}) collective-permute-start(bf16[128,768]{1,0:T(8,128)(2,1)S(1)} %get-tuple-element.54.by_y.by0), channel_id=1, source_target_pairs={{0,8},{8,16},{16,24},{24,0},{1,9},{9,17},{17,25},{25,1},{2,10},{10... | collective-permute-start | bytes 589832 | tf_op jit(solution)/shard_map/ppermute | solution.py:457
  158.4 4.2 %collective-permute-start.16 = (bf16[1976,128]{1,0:T(8,128)(2,1)}, bf16[1976,128]{1,0:T(8,128)(2,1)S(1)}, u32[]{:S(2)}, u32[]{:S(2)}) collective-permute-start(bf16[1976,128]{1,0:T(8,128)(2,1)} %get-tuple-element.64), channel_id=1, source_target_pairs={{0,1},{1,0},{2,3},{3,2},{4,5},{5,4},{6,7},{7,6},{8,9},{9,8},{10,11... | collective-permute-start | bytes 1517576 | tf_op jit(solution)/shard_map/ppermute | solution.py:593
  158.4 26.1 %all-to-all-start.2 = ((bf16[4,152,768]{2,1,0:T(8,128)(2,1)}), bf16[4,152,768]{2,1,0:T(8,128)(2,1)S(1)}, u32[]{:S(2)}, u32[]{:S(2)}) async-start(bf16[4,152,768]{2,1,0:T(8,128)(2,1)} %get-tuple-element.70), calls=%async_computation.2 | async-start | bytes 1867776 | tf_op jit(solution)/shard_map/all_to_all | solution.py:598
  162.5 31.4 %collective-permute-start.15 = (bf16[1976,128]{1,0:T(8,128)(2,1)}, bf16[1976,128]{1,0:T(8,128)(2,1)S(1)}, u32[]{:S(2)}, u32[]{:S(2)}) collective-permute-start(bf16[1976,128]{1,0:T(8,128)(2,1)} %get-tuple-element.62), channel_id=1, source_target_pairs={{0,1},{1,0},{2,3},{3,2},{4,5},{5,4},{6,7},{7,6},{8,9},{9,8},{10,11... | collective-permute-start | bytes 1517576 | tf_op jit(solution)/shard_map/ppermute | solution.py:594
  163.4 30.5 %copy-start.2 = (bf16[128,608]{0,1:T(8,128)(2,1)S(1)}, bf16[128,608]{0,1:T(8,128)(2,1)}, u32[]{:S(2)}) copy-start(bf16[128,608]{0,1:T(8,128)(2,1)} %param.14) | copy-start | bytes 466948
  163.4 30.5 %copy-start.3 = (bf16[128,608]{0,1:T(8,128)(2,1)S(1)}, bf16[128,608]{0,1:T(8,128)(2,1)}, u32[]{:S(2)}) copy-start(bf16[128,608]{0,1:T(8,128)(2,1)} %param.17) | copy-start | bytes 466948
  163.4 30.5 %copy-start.4 = (bf16[1976,128]{1,0:T(8,128)(2,1)S(1)}, bf16[1976,128]{1,0:T(8,128)(2,1)}, u32[]{:S(2)}) copy-start(bf16[1976,128]{1,0:T(8,128)(2,1)} %get-tuple-element.57.part0) | copy-start | bytes 1517572
  163.4 30.5 %copy-start.7 = (bf16[16,608]{1,0:T(8,128)(2,1)S(1)}, bf16[16,608]{1,0:T(8,128)(2,1)}, u32[]{:S(2)}) copy-start(bf16[16,608]{1,0:T(8,128)(2,1)} %txt.3) | copy-start | bytes 58372
  163.4 30.5 %copy-start.8 = (bf16[16,608]{1,0:T(8,128)(2,1)S(1)}, bf16[16,608]{1,0:T(8,128)(2,1)}, u32[]{:S(2)}) copy-start(bf16[16,608]{1,0:T(8,128)(2,1)} %dy_txt.3) | copy-start | bytes 58372
  165.5 28.4 %collective-permute-start.17 = (bf16[1976,128]{1,0:T(8,128)(2,1)}, bf16[1976,128]{1,0:T(8,128)(2,1)S(1)}, u32[]{:S(2)}, u32[]{:S(2)}) collective-permute-start(bf16[1976,128]{1,0:T(8,128)(2,1)} %add_convert_fusion), channel_id=1, source_target_pairs={{0,2},{1,3},{2,0},{3,1},{4,6},{5,7},{6,4},{7,5},{8,10},{9,11},{10,... | collective-permute-start | bytes 1517576 | tf_op jit(solution)/shard_map/ppermute | solution.py:596
  168.1 9.5 %collective-permute-start.18 = (bf16[152,768]{1,0:T(8,128)(2,1)}, bf16[152,768]{1,0:T(8,128)(2,1)S(1)}, u32[]{:S(2)}, u32[]{:S(2)}) collective-permute-start(bf16[152,768]{1,0:T(8,128)(2,1)} %get-tuple-element.72), channel_id=1, source_target_pairs={{0,32},{32,64},{64,96},{96,0},{1,33},{33,65},{65,97},{97,1},{2,34}... | collective-permute-start | bytes 700424 | tf_op jit(solution)/shard_map/ppermute | solution.py:457
  169.2 14.6 %collective-permute-start.19 = (bf16[152,768]{1,0:T(8,128)(2,1)}, bf16[152,768]{1,0:T(8,128)(2,1)S(1)}, u32[]{:S(2)}, u32[]{:S(2)}) collective-permute-start(bf16[152,768]{1,0:T(8,128)(2,1)} %copy-done.12), channel_id=1, source_target_pairs={{0,64},{32,96},{64,0},{96,32},{1,65},{33,97},{65,1},{97,33},{2,66}... | collective-permute-start | bytes 700424 | tf_op jit(solution)/shard_map/ppermute | solution.py:457
  172.9 10.9 %collective-permute-start.20 = (bf16[152,768]{1,0:T(8,128)(2,1)}, bf16[152,768]{1,0:T(8,128)(2,1)S(1)}, u32[]{:S(2)}, u32[]{:S(2)}) collective-permute-start(bf16[152,768]{1,0:T(8,128)(2,1)} %copy-done.11), channel_id=1, source_target_pairs={{0,96},{32,0},{64,32},{96,64},{1,97},{33,1},{65,33},{97,65},{2,98}... | collective-permute-start | bytes 700424 | tf_op jit(solution)/shard_map/ppermute | solution.py:457
  185.8 7.3 %collective-permute-start.21 = (bf16[76,1536]{1,0:T(8,128)(2,1)S(1)}, bf16[76,1536]{1,0:T(8,128)(2,1)S(1)}, u32[]{:S(2)}, u32[]{:S(2)}) collective-permute-start(bf16[76,1536]{1,0:T(8,128)(2,1)S(1)} %get-tuple-element.76), channel_id=1, source_target_pairs={{0,4},{4,0},{1,5},{5,1},{2,6},{6,2},{3,7},{7,3},{8,12},{12,8},{9,1... | collective-permute-start | bytes 700424 | tf_op jit(solution)/shard_map/ppermute | solution.py:607
  (18 other events, 90.1 us)

commit v4 on v3

--- a/solution.py
+++ b/solution.py
@@ -66,10 +66,8 @@
 
 def weight_copies(sources, wq, wo, sems):
     return [
-        (
-            pltpu.make_async_copy(sources[s], wq.at[s], sems.at[s]),
-            pltpu.make_async_copy(sources[3 + s], wo.at[s], sems.at[3 + s]),
-        )
+        [pltpu.make_async_copy(sources[s].at[j], wq.at[s, j], sems.at[4 * s + j]) for j in range(3)]
+        + [pltpu.make_async_copy(sources[3 + s], wo.at[s], sems.at[4 * s + 3])]
         for s in range(3)
     ]
 
@@ -109,8 +107,8 @@
 
 def pre_kernel(
     in0, in1, in2, in3, mod, gains, wq_img, wq_txt, wq_ctl, wo_img, wo_txt, wo_ctl,
-    send_out, proj_out, xhat_out, rstd_out, nz0, nz1, nz2, nz3, ny0, ny1, ny2, ny3,
-    wq, wo, gat, send, send_ctl, proj, xhat, rstd, nz, ny, sems, in_sems, out_sems,
+    send_out, proj_out, xhat_out, rstd_out, nz0, nz1, nz2, nz3,
+    wq, wo, gat, send, send_ctl, proj, xhat, rstd, nz, sems, in_sems, out_sems,
 ):
     arrivals = [
         pltpu.make_async_copy(part, gat.at[lax.axis_index("tp") ^ i], in_sems.at[i])
@@ -119,8 +117,9 @@
     for copy in arrivals:
         copy.start()
     copies = weight_copies((wq_img, wq_txt, wq_ctl, wo_img, wo_txt, wo_ctl), wq, wo, sems)
-    for copy in (copies[0][0], copies[0][1], copies[2][0]):
-        copy.start()
+    for s in (0, 2, 1):
+        for copy in copies[s]:
+            copy.start()
     results = Results(out_sems)
     for copy in arrivals:
         copy.wait()
@@ -128,7 +127,7 @@
     def rows(slab):
         return gat[:, SHARE * slab : SHARE * (slab + 1), :].reshape(D, IMG).T.astype(F32)
 
-    def stream(s, x, e, at, later):
+    def stream(s, x, e, at):
         count = x.shape[0]
         centered = x - jnp.mean(x, axis=-1, keepdims=True)
         inverse = lax.rsqrt(jnp.mean(centered * centered, axis=-1, keepdims=True) + EPS)
@@ -137,16 +136,16 @@
         rstd[at : at + count, :] = jnp.broadcast_to(inverse, (count, 128))
         n = (standard * (1.0 + mod[s, 1:2, :]) + mod[s, 0:1, :]).astype(BF16)
         copies[s][0].wait()
-        for copy in later:
-            copy.start()
         pq = dot(n, wq[s, 0])
+        copies[s][1].wait()
         pk = dot(n, wq[s, 1])
+        copies[s][2].wait()
         pv = dot(n, wq[s, 2])
         proj[at : at + count, 0:WIDTH] = pq
         proj[at : at + count, WIDTH : 2 * WIDTH] = pk
         for source, target in ((proj, proj_out), (xhat, xhat_out), (rstd, rstd_out)):
             results.send(source.at[pl.ds(at, count)], target.at[pl.ds(at, count)])
-        copies[s][1].wait()
+        copies[s][3].wait()
         g = dot_nt(e, wo[s])
         kv, qg = [], []
         for h in range(HEADS):
@@ -160,7 +159,7 @@
     dy = rows(2)
     text = jnp.concatenate([spread_text(gat[c, 3 * SHARE :, :].astype(F32)) for c in range(4)], 0).astype(BF16).T.astype(F32)
     e_img = (mod[0, 2:3, :] * dy).astype(BF16)
-    n, kv, qg = stream(0, rows(0), e_img, 0, (copies[2][1], copies[1][0]))
+    n, kv, qg = stream(0, rows(0), e_img, 0)
     for h in range(HEADS):
         for t in range(MAIN_PARTS):
             to = MAIN_PARTS * h + t
@@ -168,7 +167,7 @@
             last = min(IMG, MAIN_Q * (t + 1))
             send[to, IMG + TXT : IMG + TXT + last - MAIN_Q * t, :] = qg[h][MAIN_Q * t : last]
     e_ctl = mod[2, 2:3, :] * dy
-    n, kv, qg = stream(2, rows(1), e_ctl.astype(BF16), IMG + TXT, (copies[1][1],))
+    n, kv, qg = stream(2, rows(1), e_ctl.astype(BF16), IMG + TXT)
     for h in range(HEADS):
         for u in range(CTL_PARTS):
             to = CTL_PARTS * h + u
@@ -177,19 +176,12 @@
     for to in range(CTL_PARTS * HEADS, BLOCKS - CTL_AT):
         send_ctl[to] = jnp.zeros((CHUNK, 128), BF16)
     results.send(send_ctl, send_out.at[pl.ds(CTL_AT, BLOCKS - CTL_AT)])
-    n_t, e_t = n.T, e_ctl.astype(BF16).T
-    nz[...] = n_t.reshape(4, SHARE, IMG)
-    n_t, e_t = n_t.astype(F32), e_t.astype(F32)
-    for y in range(4):
-        for j, values in enumerate((n_t, e_t)):
-            pieces = [values[SHARE * z + PIECE * y : SHARE * z + PIECE * (y + 1)] for z in range(4)]
-            ny[y, j] = jnp.concatenate(pieces, 0).astype(BF16)
+    nz[:, 0] = n.T.reshape(4, SHARE, IMG)
+    nz[:, 1] = e_ctl.astype(BF16).T.reshape(4, SHARE, IMG)
     for d, out in enumerate((nz0, nz1, nz2, nz3)):
         results.send(nz.at[lax.rem(lax.axis_index("z") + d, 4)], out)
-    for d, out in enumerate((ny0, ny1, ny2, ny3)):
-        results.send(ny.at[lax.rem(lax.axis_index("y") + d, 4)], out)
     e_txt = (mod[1, 2:3, :] * text[TXT : 2 * TXT]).astype(BF16)
-    unused, kv, qg = stream(1, text[0:TXT], e_txt, IMG, ())
+    unused, kv, qg = stream(1, text[0:TXT], e_txt, IMG)
     for h in range(HEADS):
         for t in range(MAIN_PARTS):
             send[MAIN_PARTS * h + t, IMG : IMG + TXT, :] = kv[h]
@@ -277,7 +269,7 @@
     dkv_out[...] = dkv[...].astype(BF16)
 
 
-def scatter_kernel(role, dkv, odq, after0, after1, after2, after3, after4, out):
+def scatter_kernel(role, dkv, odq, after0, after1, out):
     for b in range(BLOCKS):
         out[b, 0:IMG, :] = dkv[IMG * b : IMG * (b + 1), :]
 
@@ -311,17 +303,14 @@
     return [jnp.concatenate(parts, 1).astype(BF16) for parts in (dq, dk, dv, o)]
 
 
-def head_back_ctl_kernel(recv, proj, gains, by_z, by_y):
+def head_back_ctl_kernel(recv, proj, gains, out):
     dkv, odq = [], []
     for h in range(HEADS):
         parts = [recv[CTL_AT + CTL_PARTS * h + u].astype(F32) for u in range(CTL_PARTS)]
         dkv.append(parts[0][0:IMG] + parts[1][0:IMG])
         odq.append(jnp.concatenate([parts[0][IMG:], parts[1][IMG:]], 0))
-    dq, dk, dv, o = head_back(2, IMG + TXT, IMG, dkv, odq, proj, gains)
-    by_z[:, 0:WIDTH] = dq
-    by_z[:, WIDTH:] = dk
-    by_y[:, 0:WIDTH] = dv
-    by_y[:, WIDTH:] = o
+    for j, part in enumerate(head_back(2, IMG + TXT, IMG, dkv, odq, proj, gains)):
+        out[:, j * WIDTH : (j + 1) * WIDTH] = part
 
 
 def head_back_main(recv, proj, gains, main):
@@ -355,7 +344,7 @@
 
 
 def post_kernel(
-    recv, proj, gains, by_z, by_y, xhat_in, rstd_in, mod, wq_img, wq_txt, wq_ctl, wo_img, wo_txt, wo_ctl,
+    recv, proj, gains, ctl_rows, xhat_in, rstd_in, mod, wq_img, wq_txt, wq_ctl, wo_img, wo_txt, wo_ctl,
     mine0, mine1, theirs0, theirs1,
     wq, wo, main, xhat, rstd, slabs, sems, in_sems, out_sems,
 ):
@@ -367,15 +356,14 @@
         copy.start()
     results = Results(out_sems)
     copies = weight_copies((wq_img, wq_txt, wq_ctl, wo_img, wo_txt, wo_ctl), wq, wo, sems)
-    for copy in (copies[2][0], copies[2][1], copies[0][0]):
-        copy.start()
-
-    def stream(s, parts, at, later):
+    for s in (2, 0, 1):
+        for copy in copies[s]:
+            copy.start()
+
+    def stream(s, parts, at):
         count = parts[0].shape[0]
-        copies[s][0].wait()
-        copies[s][1].wait()
-        for copy in later:
-            copy.start()
+        for copy in copies[s]:
+            copy.wait()
         return back(s, *parts, wq.at[s], wo.at[s], mod, xhat[at : at + count, :], rstd[at : at + count, 0:1])
 
     def joint(at, count):
@@ -388,14 +376,14 @@
     head_back_main(recv, proj, gains, main)
     for copy in arrivals:
         copy.wait()
-    u, y_ctl = stream(2, [r[:, j * WIDTH : (j + 1) * WIDTH] for r in (by_z, by_y) for j in range(2)], IMG + TXT, (copies[0][1], copies[1][0]))
+    u, y_ctl = stream(2, [ctl_rows[:, j * WIDTH : (j + 1) * WIDTH] for j in range(4)], IMG + TXT)
     slabs[:, 2 * SHARE : 3 * SHARE, :] = slab(u)
     leave(2 * SHARE, SHARE)
-    u, y = stream(0, joint(0, IMG), 0, (copies[1][1],))
+    u, y = stream(0, joint(0, IMG), 0)
     slabs[:, SHARE : 2 * SHARE, :] = slab(u)
     slabs[:, 0:SHARE, :] = slab(y + y_ctl)
     leave(0, 2 * SHARE)
-    u, y = stream(1, joint(IMG, TXT), IMG, ())
+    u, y = stream(1, joint(IMG, TXT), IMG)
     text = jnp.concatenate([y, u, jnp.zeros((IMG - 2 * TXT, D), F32)], 0).astype(BF16).T.astype(F32)
     for c in range(4):
         slabs[c, 3 * SHARE :, :] = pack_text(text[SHARE * c : SHARE * (c + 1)]).astype(BF16)
@@ -403,33 +391,29 @@
     results.finish()
 
 
-def weight_kernel(
-    nz0, nz1, nz2, nz3, ny0, ny1, ny2, ny3, bz0, bz1, bz2, bz3, by0, by1, by2, by3,
-    theirs0, theirs1, out_z, out_y0, out_y1, out_y2, out_y3, same0, same1,
-    chunks,
-):
-    nz, ny = (nz0, nz1, nz2, nz3), (ny0, ny1, ny2, ny3)
-    bz, by = (bz0, bz1, bz2, bz3), (by0, by1, by2, by3)
-    qk = dot(jnp.concatenate([r[...] for r in nz], 1), jnp.concatenate([r[...] for r in bz], 0))
-    v = dot(jnp.concatenate([r[0] for r in ny], 1), jnp.concatenate([r[:, 0:WIDTH] for r in by], 0))
-    o = dot(jnp.concatenate([r[1] for r in ny], 1), jnp.concatenate([r[:, WIDTH:] for r in by], 0))
+def weight_kernel(nz0, nz1, nz2, nz3, b0, b1, b2, b3, out):
+    nz, blocks = (nz0, nz1, nz2, nz3), (b0, b1, b2, b3)
+    total = jnp.concatenate(
+        [
+            dot(
+                jnp.concatenate([r[j] for r in nz], 1),
+                jnp.concatenate([r[:, 3 * j * WIDTH : (3 + j) * WIDTH] for r in blocks], 0),
+            )
+            for j in range(2)
+        ],
+        1,
+    )
     for p in range(4):
-        out_z[p] = qk[PIECE * p : PIECE * (p + 1)].astype(BF16)
-        chunks[p, :, 0:WIDTH] = v[PIECE * p : PIECE * (p + 1)].astype(BF16)
-        chunks[p, :, WIDTH:] = o[PIECE * p : PIECE * (p + 1)].astype(BF16)
-    for d, out in enumerate((out_y0, out_y1, out_y2, out_y3)):
-        out[...] = chunks[lax.rem(lax.axis_index("z") + d, 4)]
-
-
-def weight_sum_kernel(terms_z, y0, y1, y2, y3, mine, theirs):
+        out[p] = total[PIECE * p : PIECE * (p + 1)].astype(BF16)
+
+
+def weight_sum_kernel(terms, mine, theirs):
     half = PIECE // 2
     low = lax.axis_index("w") == 0
-    for j, terms in enumerate(([terms_z[p] for p in range(4)], [y0[...], y1[...], y2[...], y3[...]])):
-        total = sum(term.astype(F32) for term in terms)
-        first, second = total[0:half], total[half:]
-        columns = slice(2 * WIDTH * j, 2 * WIDTH * (j + 1))
-        mine[:, columns] = jnp.where(low, first, second)
-        theirs[:, columns] = jnp.where(low, second, first).astype(BF16)
+    total = sum(terms[p].astype(F32) for p in range(4))
+    first, second = total[0:half], total[half:]
+    mine[...] = jnp.where(low, first, second)
+    theirs[...] = jnp.where(low, second, first).astype(BF16)
 
 
 def weight_out_kernel(mine, other, qkv, out):
@@ -495,9 +479,9 @@
             shape((2 * IMG + TXT, 2 * WIDTH), F32),
             shape((2 * IMG + TXT, D), F32),
             shape((2 * IMG + TXT, 128), F32),
-        ] + [shape((SHARE, IMG), BF16)] * 4 + [shape((2, SHARE, IMG), BF16)] * 4,
+        ] + [shape((2, SHARE, IMG), BF16)] * 4,
         in_specs=[HBM] * 4 + [VMEM] * 2 + [HBM] * 6,
-        out_specs=[ANY] * 12,
+        out_specs=[ANY] * 8,
         scratch_shapes=[
             pltpu.VMEM((3, 3, D, WIDTH), BF16),
             pltpu.VMEM((3, WIDTH, D), BF16),
@@ -507,19 +491,17 @@
             pltpu.VMEM((2 * IMG + TXT, 2 * WIDTH), F32),
             pltpu.VMEM((2 * IMG + TXT, D), F32),
             pltpu.VMEM((2 * IMG + TXT, 128), F32),
-            pltpu.VMEM((4, SHARE, IMG), BF16),
             pltpu.VMEM((4, 2, SHARE, IMG), BF16),
-            pltpu.SemaphoreType.DMA((6,)),
+            pltpu.SemaphoreType.DMA((12,)),
             pltpu.SemaphoreType.DMA((4,)),
-            pltpu.SemaphoreType.DMA((19,)),
+            pltpu.SemaphoreType.DMA((15,)),
         ],
         compiler_params=params(56),
         name="pre",
     )(own, from_core, from_chip, from_both, mod, gains, *weights)
 
     recv = lax.all_to_all(send, seq, 0, 0, tiled=True)
-    nz = shifted(slabs[0:4], "z")
-    ny = shifted(slabs[4:8], "y")
+    nz = shifted(slabs, "z")
     keys = IMAGE_KEYS + TEXT_KEYS
     dkv, odq = pl.pallas_call(
         attention_kernel,
@@ -541,27 +523,26 @@
     back = pl.pallas_call(
         scatter_kernel,
         out_shape=shape((BLOCKS, CHUNK, 128), BF16),
-        in_specs=[SMEM] + [VMEM] * 2 + [ANY] * 5,
+        in_specs=[SMEM] + [VMEM] * 2 + [ANY] * 2,
         out_specs=VMEM,
         compiler_params=params(16),
         name="scatter",
-    )(role, dkv, odq, *nz[1:3], *ny[1:])
+    )(role, dkv, odq, *nz[1:3])
     back = lax.all_to_all(back, seq, 0, 0, tiled=True)
 
-    by_z, by_y = pl.pallas_call(
+    ctl_rows = pl.pallas_call(
         head_back_ctl_kernel,
-        out_shape=[shape((IMG, 2 * WIDTH), BF16)] * 2,
+        out_shape=shape((IMG, 4 * WIDTH), BF16),
         in_specs=[VMEM] * 3,
-        out_specs=[VMEM] * 2,
+        out_specs=VMEM,
         compiler_params=params(16),
         name="head_back_ctl",
     )(back, proj, gains)
-    blocks_z = shifted([by_z] * 4, "z")
-    blocks_y = shifted([by_y] * 4, "y")
+    blocks = shifted([ctl_rows] * 4, "z")
     mine0, mine1, theirs0, theirs1 = pl.pallas_call(
         post_kernel,
         out_shape=[rows] * 4,
-        in_specs=[VMEM] * 5 + [HBM] * 2 + [VMEM] + [HBM] * 6,
+        in_specs=[VMEM] * 4 + [HBM] * 2 + [VMEM] + [HBM] * 6,
         out_specs=[ANY] * 4,
         scratch_shapes=[
             pltpu.VMEM((3, 3, D, WIDTH), BF16),
@@ -570,40 +551,36 @@
             pltpu.VMEM((2 * IMG + TXT, D), F32),
             pltpu.VMEM((2 * IMG + TXT, 128), F32),
             pltpu.VMEM((4, ROWS, IMG), BF16),
-            pltpu.SemaphoreType.DMA((6,)),
+            pltpu.SemaphoreType.DMA((12,)),
             pltpu.SemaphoreType.DMA((2,)),
             pltpu.SemaphoreType.DMA((12,)),
         ],
         compiler_params=params(54),
         cost_estimate=pl.CostEstimate(flops=14_000_000_000, bytes_accessed=30_000_000, transcendentals=0),
         name="post",
-    )(back, proj, gains, by_z, by_y, xhat, rstd, mod, *weights)
-    terms_z, *outs = pl.pallas_call(
+    )(back, proj, gains, ctl_rows, xhat, rstd, mod, *weights)
+    terms = pl.pallas_call(
         weight_kernel,
-        out_shape=[shape((4, PIECE, 2 * WIDTH), BF16)] + [shape((PIECE, 2 * WIDTH), BF16)] * 4 + [rows] * 2,
-        in_specs=[VMEM] * 16 + [ANY] * 2,
-        out_specs=[VMEM] * 5 + [ANY] * 2,
-        input_output_aliases={16: 5, 17: 6},
-        scratch_shapes=[pltpu.VMEM((4, PIECE, 2 * WIDTH), BF16)],
+        out_shape=shape((4, PIECE, 4 * WIDTH), BF16),
+        in_specs=[VMEM] * 8,
+        out_specs=VMEM,
         compiler_params=params(24),
         cost_estimate=pl.CostEstimate(flops=3_000_000_000, bytes_accessed=5_000_000, transcendentals=0),
         name="weight",
-    )(*nz, *ny, *blocks_z, *blocks_y, theirs0, theirs1)
-    terms_y, (theirs0, theirs1) = outs[0:4], outs[4:6]
+    )(*nz, *blocks)
     got1 = lax.ppermute(theirs1, "tp", other_core)
     got0 = lax.ppermute(theirs0, "tp", other_core)
     passed = (mine1.astype(F32) + got1.astype(F32)).astype(BF16)
     passed = lax.ppermute(passed, "tp", other_chip)
-    terms_y = shifted(terms_y, "z")
-    terms_z = lax.all_to_all(terms_z, "y", 0, 0, tiled=True)
+    terms = lax.all_to_all(terms, "y", 0, 0, tiled=True)
     mine, theirs = pl.pallas_call(
         weight_sum_kernel,
         out_shape=[shape((PIECE // 2, 4 * WIDTH), F32), shape((PIECE // 2, 4 * WIDTH), BF16)],
-        in_specs=[VMEM] * 5,
+        in_specs=[VMEM],
         out_specs=[VMEM] * 2,
         compiler_params=params(16),
         name="weight_sum",
-    )(terms_z, *terms_y)
+    )(terms)
     theirs = lax.ppermute(theirs, "w", [(0, 1), (1, 0)])
     grad_qkv, grad_out = pl.pallas_call(
         weight_out_kernel,

time: 196 us -> 208 us (1.061)
  waiting for transfers between devices: 46.1 us -> 66.9 us
  starting transfers between devices: 42.6 us -> 28.3 us
  Pallas kernels: 64.5 us -> 72.1 us
  local copies, waits for them, and re-layouts: 6.57 us -> 2.85 us
    ppermute x15 -> x6, starting transfers between devices: 22.9 us -> 7.67 us  [shifted(): lax.ppermute(parts[d], axis, [(i, (i + d) % 4) for i in range(4)])]
    ppermute x1, waiting for transfers between devices: 0.01 us -> 12.4 us  [per_device(): passed = lax.ppermute(passed, 'tp', other_chip)]
    ppermute x15 -> x6, waiting for transfers between devices: 25.3 us -> 37.6 us  [shifted(): lax.ppermute(parts[d], axis, [(i, (i + d) % 4) for i in range(4)])]
    ppermute x1, waiting for transfers between devices: 7.18 us -> 1.7 us  [per_device(): theirs = lax.ppermute(theirs, 'w', [(0, 1), (1, 0)])]
    pallas_call x1, Pallas kernels: 16.3 us -> 20.1 us  [per_device(): pl.pallas_call(pre_kernel, out_shape=[shape((BLOCKS, CHUNK, 128), BF16),...]
    unnamed x52 -> x42, local copies, waits for them, and re-layouts: 6.57 us -> 2.85 us
    pallas_call x3, Pallas kernels: 18.5 us -> 21.2 us  [the longest x1 17.4 us: per_device(): pl.pallas_call(post_kernel, out_shape=[rows] * 4, in_specs=[VMEM] * 4 + [...]
  transfers between devices with their start and end apart: 24 -> 15, of which waited for: 7 -> 9; matrix products, arithmetic and copies ran while one was open for 1% -> 1% of each run, Pallas kernels for 20% -> 22%
where the time goes in v4:
time: 208 us; the launch traced here: 207 us
  Pallas kernels  72.1 us (35%)
  waiting for transfers between devices  66.9 us (32%)
  blocking collectives  33.1 us (16%)
  starting transfers between devices  28.3 us (14%)
  local copies, waits for them, and re-layouts  2.85 us (1%)
    ppermute x6, waiting for transfers between devices, shifted(): lax.ppermute(parts[d], axis, [(i, (i + d) % 4) for i in range(4)])  37.6 us
    all_to_all x1, blocking collectives, per_device(): back = lax.all_to_all(back, seq, 0, 0, tiled=True)  33.1 us
    pallas_call x1, Pallas kernels, per_device(): pl.pallas_call(attention_kernel, out_shape=[shape((keys, 128), BF16), sha...  24.8 us
    pallas_call x1, Pallas kernels, per_device(): pl.pallas_call(pre_kernel, out_shape=[shape((BLOCKS, CHUNK, 128), BF16),...  20.1 us
    pallas_call x1, Pallas kernels, per_device(): pl.pallas_call(post_kernel, out_shape=[rows] * 4, in_specs=[VMEM] * 4 + [...  17.4 us
    ppermute x1, waiting for transfers between devices, per_device(): passed = lax.ppermute(passed, 'tp', other_chip)  12.4 us
    ppermute x1, waiting for transfers between devices, per_device(): from_chip = lax.ppermute(own, 'tp', other_chip)  11.7 us
    all_to_all x1, starting transfers between devices, per_device(): recv = lax.all_to_all(send, seq, 0, 0, tiled=True)  9.63 us
  transfers between devices with their start and end apart: 15, of which 9 were waited for; matrix products, arithmetic and copies ran while one was open for 1% of the time, Pallas kernels for 22%

profile of v4, /device:TPU:0, one launch (start us, length us, event | category | flops | bytes accessed | tf_op | source)
XLA Modules:
  0.0 206.9 jit_solution(10758906139678372219)
XLA Ops:
  0.6 1.9 pack.1.in0
  2.6 3.2 %collective-permute-start.1 = (bf16[1976,128]{1,0:T(8,128)(2,1)}, bf16[1976,128]{1,0:T(8,128)(2,1)S(1)}, u32[]{:S(2)}, u32[]{:S(2)}) collective-permute-start(bf16[1976,128]{1,0:T(8,128)(2,1)} %pack.1.in0), channel_id=1, source_target_pairs={{0,2},{1,3},{2,0},{3,1},{4,6},{5,7},{6,4},{7,5},{8,10},{9,11},{10,... | collective-permute-start | bytes 1517576 | tf_op jit(solution)/shard_map/ppermute | solution.py:471
  5.8 11.7 %collective-permute-done.1.in2 = bf16[1976,128]{1,0:T(8,128)(2,1)S(1)} collective-permute-done((bf16[1976,128]{1,0:T(8,128)(2,1)}, bf16[1976,128]{1,0:T(8,128)(2,1)S(1)}, u32[]{:S(2)}, u32[]{:S(2)}) %collective-permute-start.1) | collective-permute-done | bytes 505888 | tf_op jit(solution)/shard_map/ppermute | solution.py:471
  17.5 1.9 collective-permute-done.2.in3
  19.4 0.8 copy-done.17
  20.2 20.1 %pre.1 = (bf16[32,192,128]{2,1,0:T(8,128)(2,1)}, f32[272,768]{1,0:T(8,128)}, f32[272,2432]{1,0:T(8,128)}, f32[272,128]{1,0:T(8,128)}, bf16[2,608,128]{2,1,0:T(8,...) custom-call(bf16[1976,128]{1,0:T(8,128)(2,1)} %pack.1.in0, ...), custom_call_target="tpu_custom_call" | custom-call | tf_op jit(solution)/shard_map/pre/pallas_call | solution.py:475
  40.4 9.6 %all-to-all-start = ((bf16[32,192,128]{2,1,0:T(8,128)(2,1)}), bf16[32,192,128]{2,1,0:T(8,128)(2,1)S(1)}, u32[]{:S(2)}, u32[]{:S(2)}) async-start(bf16[32,192,128]{2,1,0:T(8,128)(2,1)} %get-tuple-element.30), calls=%async_computation | async-start | bytes 3145728 | tf_op jit(solution)/shard_map/all_to_all | solution.py:503
  50.0 3.1 %collective-permute-start.3 = (bf16[2,608,128]{2,1,0:T(8,128)(2,1)S(1)}, bf16[2,608,128]{2,1,0:T(8,128)(2,1)S(1)}, u32[]{:S(2)}, u32[]{:S(2)}) collective-permute-start(bf16[2,608,128]{2,1,0:T(8,128)(2,1)S(1)} %copy-done.20), channel_id=1, source_target_pairs={{0,96},{32,0},{64,32},{96,64},{1,97},{33,1},{65,33},{97,65},{2,98}... | collective-permute-start | bytes 933896 | tf_op jit(solution)/shard_map/ppermute | solution.py:441
  53.9 2.3 %collective-permute-start.5 = (bf16[2,608,128]{2,1,0:T(8,128)(2,1)S(1)}, bf16[2,608,128]{2,1,0:T(8,128)(2,1)S(1)}, u32[]{:S(2)}, u32[]{:S(2)}) collective-permute-start(bf16[2,608,128]{2,1,0:T(8,128)(2,1)S(1)} %copy-done.18), channel_id=1, source_target_pairs={{0,64},{32,96},{64,0},{96,32},{1,65},{33,97},{65,1},{97,33},{2,66}... | collective-permute-start | bytes 933896 | tf_op jit(solution)/shard_map/ppermute | solution.py:441
  56.2 20.8 %collective-permute-done.3.after.nz3 = bf16[2,608,128]{2,1,0:T(8,128)(2,1)S(1)} collective-permute-done((bf16[2,608,128]{2,1,0:T(8,128)(2,1)S(1)}, bf16[2,608,128]{2,1,0:T(8,128)(2,1)S(1)}, u32[]{:S(2)}, u32[]{:S(2)}) %collective-permute-start.3) | collective-permute-done | bytes 311328 | tf_op jit(solution)/shard_map/ppermute | solution.py:441
  77.0 24.8 %attention.1 = (bf16[4608,128]{1,0:T(8,128)(2,1)S(1)}, bf16[2048,128]{1,0:T(8,128)(2,1)S(1)}) custom-call(s32[2]{0:T(128)S(1)} %pad_add_fusion.role, bf16[32,192,128]{2,1,0:T(8,128)(2,1)S(1)} %all-to-all-done.recv, bf16[2,608,128]{2,1,0:T(8,128)(2,1)S(1)} %collective-permute-done.3.after.nz3), custom_call_target="tpu_custom_call" | custom-call | flops 40000000000 | bytes 3200000 | tf_op jit(solution)/shard_map/attention/pallas_call | solution.py:506
  101.8 0.7 scatter.1
  102.4 0.7 copy-done.7
  103.2 33.1 %all_to_all.15.recv = bf16[32,192,128]{2,1,0:T(8,128)(2,1)S(1)} all-to-all(bf16[32,192,128]{2,1,0:T(8,128)(2,1)S(1)} %scatter.1), channel_id=1, replica_groups=mesh['z'=4,'y'=4,'w'=2,'tp'=4] {'z','y','w'}, dimensions={0} | all-to-all | bytes 3145728 | tf_op jit(solution)/shard_map/all_to_all | solution.py:531
  136.3 2.5 %head_back_ctl.1.ctl_rows.b0 = bf16[128,1536]{1,0:T(8,128)(2,1)S(1)} custom-call(bf16[32,192,128]{2,1,0:T(8,128)(2,1)S(1)} %all_to_all.15.recv, f32[272,768]{1,0:T(8,128)S(1)} %copy-done.2, f32[3,2,64]{2,1,0:T(2,128)S(1)} %copy-done.11), custom_call_target="tpu_custom_call" | custom-call | tf_op jit(solution)/shard_map/head_back_ctl/pallas_call | solution.py:533
  138.8 0.9 collective-permute-start.11
  140.2 0.9 collective-permute-start.9
  141.1 9.8 %collective-permute-done.11.b3 = bf16[128,1536]{1,0:T(8,128)(2,1)S(1)} collective-permute-done((bf16[128,1536]{1,0:T(8,128)(2,1)S(1)}, bf16[128,1536]{1,0:T(8,128)(2,1)S(1)}, u32[]{:S(2)}, u32[]{:S(2)}) %collective-permute-start.11) | collective-permute-done | bytes 393248 | tf_op jit(solution)/shard_map/ppermute | solution.py:441
  151.0 2.3 %collective-permute-done.10.b2 = bf16[128,1536]{1,0:T(8,128)(2,1)S(1)} collective-permute-done((bf16[128,1536]{1,0:T(8,128)(2,1)S(1)}, bf16[128,1536]{1,0:T(8,128)(2,1)S(1)}, u32[]{:S(2)}, u32[]{:S(2)}) %collective-permute-start.10) | collective-permute-done | bytes 393248 | tf_op jit(solution)/shard_map/ppermute | solution.py:441
  153.3 4.7 %collective-permute-done.9.b1 = bf16[128,1536]{1,0:T(8,128)(2,1)S(1)} collective-permute-done((bf16[128,1536]{1,0:T(8,128)(2,1)S(1)}, bf16[128,1536]{1,0:T(8,128)(2,1)S(1)}, u32[]{:S(2)}, u32[]{:S(2)}) %collective-permute-start.9) | collective-permute-done | bytes 393248 | tf_op jit(solution)/shard_map/ppermute | solution.py:441
  157.9 1.3 weight.1
  159.3 1.3 copy-done.1
  160.5 3.8 %all-to-all-start.2 = ((bf16[4,152,1536]{2,1,0:T(8,128)(2,1)}), bf16[4,152,1536]{2,1,0:T(8,128)(2,1)S(1)}, u32[]{:S(2)}, u32[]{:S(2)}) async-start(bf16[4,152,1536]{2,1,0:T(8,128)(2,1)} %copy-done.1), calls=%async_computation.2 | async-start | bytes 3735552 | tf_op jit(solution)/shard_map/all_to_all | solution.py:575
  164.3 17.4 %post.1 = (bf16[1976,128]{1,0:T(8,128)(2,1)}, bf16[1976,128]{1,0:T(8,128)(2,1)}, bf16[1976,128]{1,0:T(8,128)(2,1)}, bf16[1976,128]{1,0:T(8,128)(2,1)}) custom-call(bf16[32,192,128]{2,1,0:T(8,128)(2,1)} %copy-done, f32[272,768]{1,0:T(8,128)} %get-tuple-element.36.proj, f32[3,2,64]{2,1,0:T(2,128)} %gains.5, bf16[128,1536]{1,0:T(8,128)(2,1)} %copy-done.6, ...), custom_call_target="tpu_custom_call" | custom-call | flops 14000000000 | bytes 30000000 | tf_op jit(solution)/shard_map/post/pallas_call | solution.py:542
  182.4 1.6 collective-permute-done.7
  184.0 2.0 add_convert_fusion
  186.0 2.8 %collective-permute-start.8 = (bf16[1976,128]{1,0:T(8,128)(2,1)}, bf16[1976,128]{1,0:T(8,128)(2,1)}, u32[]{:S(2)}, u32[]{:S(2)}) collective-permute-start(bf16[1976,128]{1,0:T(8,128)(2,1)} %add_convert_fusion), channel_id=1, source_target_pairs={{0,2},{1,3},{2,0},{3,1},{4,6},{5,7},{6,4},{7,5},{8,10},{9,11},{10,... | collective-permute-start | bytes 1517576 | tf_op jit(solution)/shard_map/ppermute | solution.py:574
  189.1 0.7 collective-permute-start.12
  189.8 12.4 %collective-permute-done.8.part2 = bf16[1976,128]{1,0:T(8,128)(2,1)} collective-permute-done((bf16[1976,128]{1,0:T(8,128)(2,1)}, bf16[1976,128]{1,0:T(8,128)(2,1)}, u32[]{:S(2)}, u32[]{:S(2)}) %collective-permute-start.8) | collective-permute-done | bytes 505888 | tf_op jit(solution)/shard_map/ppermute | solution.py:574
  202.2 2.2 %final.1 = (bf16[608,128]{1,0:T(8,128)(2,1)}, bf16[608,128]{1,0:T(8,128)(2,1)}, bf16[608,128]{1,0:T(8,128)(2,1)}, bf16[16,608]{1,0:T(8,128)(2,1)}, bf16[16,608]{1,0:T(8,128)(2,1)}) custom-call(bf16[608,128]{1,0:T(8,128)(2,1)S(1)} %bitcast.13, bf16[608,128]{1,0:T(8,128)(2,1)S(1)} %bitcast.15, bf16[16,608]{1,0:T(8,128)(2,1)S(1)} %copy-done.9, ...), custom_call_target="tpu_custom_call" | custom-call | tf_op jit(solution)/shard_map/final/pallas_call | solution.py:594
  204.4 1.7 collective-permute-done.12.other
  206.1 0.8 weight_out.1
  (53 shorter events, 1.7 us)
Async XLA Ops:
  2.6 14.9 %collective-permute-start.1 = (bf16[1976,128]{1,0:T(8,128)(2,1)}, bf16[1976,128]{1,0:T(8,128)(2,1)S(1)}, u32[]{:S(2)}, u32[]{:S(2)}) collective-permute-start(bf16[1976,128]{1,0:T(8,128)(2,1)} %pack.1.in0), channel_id=1, source_target_pairs={{0,2},{1,3},{2,0},{3,1},{4,6},{5,7},{6,4},{7,5},{8,10},{9,11},{10,... | collective-permute-start | bytes 1517576 | tf_op jit(solution)/shard_map/ppermute | solution.py:471
  5.8 11.7 %collective-permute-start = (bf16[1976,128]{1,0:T(8,128)(2,1)}, bf16[1976,128]{1,0:T(8,128)(2,1)S(1)}, u32[]{:S(2)}, u32[]{:S(2)}) collective-permute-start(bf16[1976,128]{1,0:T(8,128)(2,1)} %pack.1.in0), channel_id=1, source_target_pairs={{0,1},{1,0},{2,3},{3,2},{4,5},{5,4},{6,7},{7,6},{8,9},{9,8},{10,11... | collective-permute-start | bytes 1517576 | tf_op jit(solution)/shard_map/ppermute | solution.py:472
  17.5 1.9 copy-start.15
  17.5 1.9 collective-permute-start.2
  40.3 9.7 %copy-start.20 = (bf16[2,608,128]{2,1,0:T(8,128)(2,1)S(1)}, bf16[2,608,128]{2,1,0:T(8,128)(2,1)}, u32[]{:S(2)}) copy-start(bf16[2,608,128]{2,1,0:T(8,128)(2,1)} %get-tuple-element.31) | copy-start | bytes 933892
  40.3 13.5 %copy-start.19 = (bf16[2,608,128]{2,1,0:T(8,128)(2,1)S(1)}, bf16[2,608,128]{2,1,0:T(8,128)(2,1)}, u32[]{:S(2)}) copy-start(bf16[2,608,128]{2,1,0:T(8,128)(2,1)} %get-tuple-element.34) | copy-start | bytes 933892
  40.4 13.5 %copy-start.18 = (bf16[2,608,128]{2,1,0:T(8,128)(2,1)S(1)}, bf16[2,608,128]{2,1,0:T(8,128)(2,1)}, u32[]{:S(2)}) copy-start(bf16[2,608,128]{2,1,0:T(8,128)(2,1)} %get-tuple-element.35) | copy-start | bytes 933892
  40.4 36.6 %all-to-all-start = ((bf16[32,192,128]{2,1,0:T(8,128)(2,1)}), bf16[32,192,128]{2,1,0:T(8,128)(2,1)S(1)}, u32[]{:S(2)}, u32[]{:S(2)}) async-start(bf16[32,192,128]{2,1,0:T(8,128)(2,1)} %get-tuple-element.30), calls=%async_computation | async-start | bytes 3145728 | tf_op jit(solution)/shard_map/all_to_all | solution.py:503
  50.0 27.0 %collective-permute-start.3 = (bf16[2,608,128]{2,1,0:T(8,128)(2,1)S(1)}, bf16[2,608,128]{2,1,0:T(8,128)(2,1)S(1)}, u32[]{:S(2)}, u32[]{:S(2)}) collective-permute-start(bf16[2,608,128]{2,1,0:T(8,128)(2,1)S(1)} %copy-done.20), channel_id=1, source_target_pairs={{0,96},{32,0},{64,32},{96,64},{1,97},{33,1},{65,33},{97,65},{2,98}... | collective-permute-start | bytes 933896 | tf_op jit(solution)/shard_map/ppermute | solution.py:441
  53.8 47.9 %collective-permute-start.4 = (bf16[2,608,128]{2,1,0:T(8,128)(2,1)S(1)}, bf16[2,608,128]{2,1,0:T(8,128)(2,1)S(1)}, u32[]{:S(2)}, u32[]{:S(2)}) collective-permute-start(bf16[2,608,128]{2,1,0:T(8,128)(2,1)S(1)} %copy-done.19), channel_id=1, source_target_pairs={{0,32},{32,64},{64,96},{96,0},{1,33},{33,65},{65,97},{97,1},{2,34}... | collective-permute-start | bytes 933896 | tf_op jit(solution)/shard_map/ppermute | solution.py:441
  53.9 47.9 %collective-permute-start.5 = (bf16[2,608,128]{2,1,0:T(8,128)(2,1)S(1)}, bf16[2,608,128]{2,1,0:T(8,128)(2,1)S(1)}, u32[]{:S(2)}, u32[]{:S(2)}) collective-permute-start(bf16[2,608,128]{2,1,0:T(8,128)(2,1)S(1)} %copy-done.18), channel_id=1, source_target_pairs={{0,64},{32,96},{64,0},{96,32},{1,65},{33,97},{65,1},{97,33},{2,66}... | collective-permute-start | bytes 933896 | tf_op jit(solution)/shard_map/ppermute | solution.py:441
  77.0 24.8 %copy-start.13 = (bf16[2,608,128]{2,1,0:T(8,128)(2,1)}, bf16[2,608,128]{2,1,0:T(8,128)(2,1)S(1)}, u32[]{:S(2)}) copy-start(bf16[2,608,128]{2,1,0:T(8,128)(2,1)S(1)} %collective-permute-done.3.after.nz3) | copy-start | bytes 933892
  103.2 33.1 %copy-start.2 = (f32[272,768]{1,0:T(8,128)S(1)}, f32[272,768]{1,0:T(8,128)}, u32[]{:S(2)}) copy-start(f32[272,768]{1,0:T(8,128)} %get-tuple-element.36.proj) | copy-start | bytes 2506756
  103.2 33.1 %copy-start.11 = (f32[3,2,64]{2,1,0:T(2,128)S(1)}, f32[3,2,64]{2,1,0:T(2,128)}, u32[]{:S(2)}) copy-start(f32[3,2,64]{2,1,0:T(2,128)} %gains.5) | copy-start | bytes 4612
  136.3 23.0 %copy-start = (bf16[32,192,128]{2,1,0:T(8,128)(2,1)}, bf16[32,192,128]{2,1,0:T(8,128)(2,1)S(1)}, u32[]{:S(2)}) copy-start(bf16[32,192,128]{2,1,0:T(8,128)(2,1)S(1)} %all_to_all.15.recv) | copy-start | bytes 4718596
  136.3 21.6 %copy-start.8 = (bf16[2,608,128]{2,1,0:T(8,128)(2,1)S(1)}, bf16[2,608,128]{2,1,0:T(8,128)(2,1)}, u32[]{:S(2)}) copy-start(bf16[2,608,128]{2,1,0:T(8,128)(2,1)} %copy-done.7) | copy-start | bytes 933892
  136.3 21.6 %copy-start.12 = (bf16[2,608,128]{2,1,0:T(8,128)(2,1)S(1)}, bf16[2,608,128]{2,1,0:T(8,128)(2,1)}, u32[]{:S(2)}) copy-start(bf16[2,608,128]{2,1,0:T(8,128)(2,1)} %get-tuple-element.48.nz0) | copy-start | bytes 933892
  136.3 21.6 %copy-start.14 = (bf16[2,608,128]{2,1,0:T(8,128)(2,1)S(1)}, bf16[2,608,128]{2,1,0:T(8,128)(2,1)}, u32[]{:S(2)}) copy-start(bf16[2,608,128]{2,1,0:T(8,128)(2,1)} %copy-done.13) | copy-start | bytes 933892
  138.8 20.4 %copy-start.6 = (bf16[128,1536]{1,0:T(8,128)(2,1)}, bf16[128,1536]{1,0:T(8,128)(2,1)S(1)}, u32[]{:S(2)}) copy-start(bf16[128,1536]{1,0:T(8,128)(2,1)S(1)} %head_back_ctl.1.ctl_rows.b0) | copy-start | bytes 1179652
  138.8 12.1 %collective-permute-start.11 = (bf16[128,1536]{1,0:T(8,128)(2,1)S(1)}, bf16[128,1536]{1,0:T(8,128)(2,1)S(1)}, u32[]{:S(2)}, u32[]{:S(2)}) collective-permute-start(bf16[128,1536]{1,0:T(8,128)(2,1)S(1)} %head_back_ctl.1.ctl_rows.b0), channel_id=1, source_target_pairs={{0,96},{32,0},{64,32},{96,64},{1,97},{33,1},{65,33},{97,65},{2,98}... | collective-permute-start | bytes 1179656 | tf_op jit(solution)/shard_map/ppermute | solution.py:441
  139.7 13.6 %collective-permute-start.10 = (bf16[128,1536]{1,0:T(8,128)(2,1)S(1)}, bf16[128,1536]{1,0:T(8,128)(2,1)S(1)}, u32[]{:S(2)}, u32[]{:S(2)}) collective-permute-start(bf16[128,1536]{1,0:T(8,128)(2,1)S(1)} %head_back_ctl.1.ctl_rows.b0), channel_id=1, source_target_pairs={{0,64},{32,96},{64,0},{96,32},{1,65},{33,97},{65,1},{97,33},{2,66}... | collective-permute-start | bytes 1179656 | tf_op jit(solution)/shard_map/ppermute | solution.py:441
  140.2 17.7 %collective-permute-start.9 = (bf16[128,1536]{1,0:T(8,128)(2,1)S(1)}, bf16[128,1536]{1,0:T(8,128)(2,1)S(1)}, u32[]{:S(2)}, u32[]{:S(2)}) collective-permute-start(bf16[128,1536]{1,0:T(8,128)(2,1)S(1)} %head_back_ctl.1.ctl_rows.b0), channel_id=1, source_target_pairs={{0,32},{32,64},{64,96},{96,0},{1,33},{33,65},{65,97},{97,1},{2,34}... | collective-permute-start | bytes 1179656 | tf_op jit(solution)/shard_map/ppermute | solution.py:441
  160.5 28.2 %all-to-all-start.2 = ((bf16[4,152,1536]{2,1,0:T(8,128)(2,1)}), bf16[4,152,1536]{2,1,0:T(8,128)(2,1)S(1)}, u32[]{:S(2)}, u32[]{:S(2)}) async-start(bf16[4,152,1536]{2,1,0:T(8,128)(2,1)} %copy-done.1), calls=%async_computation.2 | async-start | bytes 3735552 | tf_op jit(solution)/shard_map/all_to_all | solution.py:575
  181.8 20.4 %copy-start.3 = (bf16[128,608]{0,1:T(8,128)(2,1)S(1)}, bf16[128,608]{0,1:T(8,128)(2,1)}, u32[]{:S(2)}) copy-start(bf16[128,608]{0,1:T(8,128)(2,1)} %param.14) | copy-start | bytes 466948
  181.8 20.4 %copy-start.4 = (bf16[128,608]{0,1:T(8,128)(2,1)S(1)}, bf16[128,608]{0,1:T(8,128)(2,1)}, u32[]{:S(2)}) copy-start(bf16[128,608]{0,1:T(8,128)(2,1)} %param.17) | copy-start | bytes 466948
  181.8 20.4 %copy-start.5 = (bf16[1976,128]{1,0:T(8,128)(2,1)S(1)}, bf16[1976,128]{1,0:T(8,128)(2,1)}, u32[]{:S(2)}) copy-start(bf16[1976,128]{1,0:T(8,128)(2,1)} %get-tuple-element.39.part0) | copy-start | bytes 1517572
  181.8 20.4 %copy-start.9 = (bf16[16,608]{1,0:T(8,128)(2,1)S(1)}, bf16[16,608]{1,0:T(8,128)(2,1)}, u32[]{:S(2)}) copy-start(bf16[16,608]{1,0:T(8,128)(2,1)} %txt.3) | copy-start | bytes 58372
  181.8 20.4 %copy-start.10 = (bf16[16,608]{1,0:T(8,128)(2,1)S(1)}, bf16[16,608]{1,0:T(8,128)(2,1)}, u32[]{:S(2)}) copy-start(bf16[16,608]{1,0:T(8,128)(2,1)} %dy_txt.3) | copy-start | bytes 58372
  181.8 2.2 %collective-permute-start.7 = (bf16[1976,128]{1,0:T(8,128)(2,1)}, bf16[1976,128]{1,0:T(8,128)(2,1)S(1)}, u32[]{:S(2)}, u32[]{:S(2)}) collective-permute-start(bf16[1976,128]{1,0:T(8,128)(2,1)} %get-tuple-element.42), channel_id=1, source_target_pairs={{0,1},{1,0},{2,3},{3,2},{4,5},{5,4},{6,7},{7,6},{8,9},{9,8},{10,11... | collective-permute-start | bytes 1517576 | tf_op jit(solution)/shard_map/ppermute | solution.py:571
  181.9 7.9 %collective-permute-start.6 = (bf16[1976,128]{1,0:T(8,128)(2,1)}, bf16[1976,128]{1,0:T(8,128)(2,1)S(1)}, u32[]{:S(2)}, u32[]{:S(2)}) collective-permute-start(bf16[1976,128]{1,0:T(8,128)(2,1)} %get-tuple-element.40), channel_id=1, source_target_pairs={{0,1},{1,0},{2,3},{3,2},{4,5},{5,4},{6,7},{7,6},{8,9},{9,8},{10,11... | collective-permute-start | bytes 1517576 | tf_op jit(solution)/shard_map/ppermute | solution.py:572
  186.0 16.2 %collective-permute-start.8 = (bf16[1976,128]{1,0:T(8,128)(2,1)}, bf16[1976,128]{1,0:T(8,128)(2,1)}, u32[]{:S(2)}, u32[]{:S(2)}) collective-permute-start(bf16[1976,128]{1,0:T(8,128)(2,1)} %add_convert_fusion), channel_id=1, source_target_pairs={{0,2},{1,3},{2,0},{3,1},{4,6},{5,7},{6,4},{7,5},{8,10},{9,11},{10,... | collective-permute-start | bytes 1517576 | tf_op jit(solution)/shard_map/ppermute | solution.py:574
  189.1 17.0 %collective-permute-start.12 = (bf16[76,1536]{1,0:T(8,128)(2,1)S(1)}, bf16[76,1536]{1,0:T(8,128)(2,1)S(1)}, u32[]{:S(2)}, u32[]{:S(2)}) collective-permute-start(bf16[76,1536]{1,0:T(8,128)(2,1)S(1)} %get-tuple-element.50), channel_id=1, source_target_pairs={{0,4},{4,0},{1,5},{5,1},{2,6},{6,2},{3,7},{7,3},{8,12},{12,8},{9,1... | collective-permute-start | bytes 700424 | tf_op jit(solution)/shard_map/ppermute | solution.py:584
  (4 other events, 4.7 us)

commit v5 on v4

--- a/solution.py
+++ b/solution.py
@@ -66,8 +66,10 @@
 
 def weight_copies(sources, wq, wo, sems):
     return [
-        [pltpu.make_async_copy(sources[s].at[j], wq.at[s, j], sems.at[4 * s + j]) for j in range(3)]
-        + [pltpu.make_async_copy(sources[3 + s], wo.at[s], sems.at[4 * s + 3])]
+        (
+            pltpu.make_async_copy(sources[s], wq.at[s], sems.at[s]),
+            pltpu.make_async_copy(sources[3 + s], wo.at[s], sems.at[3 + s]),
+        )
         for s in range(3)
     ]
 
@@ -107,22 +109,16 @@
 
 def pre_kernel(
     in0, in1, in2, in3, mod, gains, wq_img, wq_txt, wq_ctl, wo_img, wo_txt, wo_ctl,
-    send_out, proj_out, xhat_out, rstd_out, nz0, nz1, nz2, nz3,
-    wq, wo, gat, send, send_ctl, proj, xhat, rstd, nz, sems, in_sems, out_sems,
+    send, proj, xhat, rstd, nz0, nz1, nz2, nz3,
+    wq, wo, gat, nz, sems,
 ):
-    arrivals = [
-        pltpu.make_async_copy(part, gat.at[lax.axis_index("tp") ^ i], in_sems.at[i])
-        for i, part in enumerate((in0, in1, in2, in3))
-    ]
-    for copy in arrivals:
-        copy.start()
     copies = weight_copies((wq_img, wq_txt, wq_ctl, wo_img, wo_txt, wo_ctl), wq, wo, sems)
-    for s in (0, 2, 1):
-        for copy in copies[s]:
-            copy.start()
-    results = Results(out_sems)
-    for copy in arrivals:
-        copy.wait()
+    for s in range(3):
+        copies[s][0].start()
+        copies[s][1].start()
+
+    for i, part in enumerate((in0, in1, in2, in3)):
+        gat[lax.axis_index("tp") ^ i] = part[...]
 
     def rows(slab):
         return gat[:, SHARE * slab : SHARE * (slab + 1), :].reshape(D, IMG).T.astype(F32)
@@ -137,15 +133,11 @@
         n = (standard * (1.0 + mod[s, 1:2, :]) + mod[s, 0:1, :]).astype(BF16)
         copies[s][0].wait()
         pq = dot(n, wq[s, 0])
-        copies[s][1].wait()
         pk = dot(n, wq[s, 1])
-        copies[s][2].wait()
         pv = dot(n, wq[s, 2])
         proj[at : at + count, 0:WIDTH] = pq
         proj[at : at + count, WIDTH : 2 * WIDTH] = pk
-        for source, target in ((proj, proj_out), (xhat, xhat_out), (rstd, rstd_out)):
-            results.send(source.at[pl.ds(at, count)], target.at[pl.ds(at, count)])
-        copies[s][3].wait()
+        copies[s][1].wait()
         g = dot_nt(e, wo[s])
         kv, qg = [], []
         for h in range(HEADS):
@@ -166,28 +158,25 @@
             send[to, 0:IMG, :] = kv[h]
             last = min(IMG, MAIN_Q * (t + 1))
             send[to, IMG + TXT : IMG + TXT + last - MAIN_Q * t, :] = qg[h][MAIN_Q * t : last]
+    e_txt = (mod[1, 2:3, :] * text[TXT : 2 * TXT]).astype(BF16)
+    n, kv, qg = stream(1, text[0:TXT], e_txt, IMG)
+    for h in range(HEADS):
+        for t in range(MAIN_PARTS):
+            send[MAIN_PARTS * h + t, IMG : IMG + TXT, :] = kv[h]
+        send[MAIN_PARTS * h + 2, CHUNK - TXT : CHUNK, :] = qg[h]
     e_ctl = mod[2, 2:3, :] * dy
     n, kv, qg = stream(2, rows(1), e_ctl.astype(BF16), IMG + TXT)
     for h in range(HEADS):
         for u in range(CTL_PARTS):
-            to = CTL_PARTS * h + u
-            send_ctl[to, 0:IMG, :] = kv[h]
-            send_ctl[to, IMG:CHUNK, :] = qg[h][CTL_Q * u : CTL_Q * (u + 1)]
-    for to in range(CTL_PARTS * HEADS, BLOCKS - CTL_AT):
-        send_ctl[to] = jnp.zeros((CHUNK, 128), BF16)
-    results.send(send_ctl, send_out.at[pl.ds(CTL_AT, BLOCKS - CTL_AT)])
+            to = CTL_AT + CTL_PARTS * h + u
+            send[to, 0:IMG, :] = kv[h]
+            send[to, IMG:CHUNK, :] = qg[h][CTL_Q * u : CTL_Q * (u + 1)]
+    for to in range(CTL_AT + CTL_PARTS * HEADS, BLOCKS):
+        send[to] = jnp.zeros((CHUNK, 128), BF16)
     nz[:, 0] = n.T.reshape(4, SHARE, IMG)
     nz[:, 1] = e_ctl.astype(BF16).T.reshape(4, SHARE, IMG)
     for d, out in enumerate((nz0, nz1, nz2, nz3)):
-        results.send(nz.at[lax.rem(lax.axis_index("z") + d, 4)], out)
-    e_txt = (mod[1, 2:3, :] * text[TXT : 2 * TXT]).astype(BF16)
-    unused, kv, qg = stream(1, text[0:TXT], e_txt, IMG)
-    for h in range(HEADS):
-        for t in range(MAIN_PARTS):
-            send[MAIN_PARTS * h + t, IMG : IMG + TXT, :] = kv[h]
-        send[MAIN_PARTS * h + 2, CHUNK - TXT : CHUNK, :] = qg[h]
-    results.send(send, send_out.at[pl.ds(0, CTL_AT)])
-    results.finish()
+        out[...] = nz[lax.rem(lax.axis_index("z") + d, 4)]
 
 
 def attention_kernel(role, recv, after, dkv_out, odq, kv, kt, vt, qg, probs, dkv):
@@ -345,7 +334,7 @@
 
 def post_kernel(
     recv, proj, gains, ctl_rows, xhat_in, rstd_in, mod, wq_img, wq_txt, wq_ctl, wo_img, wo_txt, wo_ctl,
-    mine0, mine1, theirs0, theirs1,
+    mine0, mine1, theirs0, theirs1, token,
     wq, wo, main, xhat, rstd, slabs, sems, in_sems, out_sems,
 ):
     arrivals = [
@@ -355,15 +344,17 @@
     for copy in arrivals:
         copy.start()
     results = Results(out_sems)
+    token[...] = jnp.zeros_like(token)
     copies = weight_copies((wq_img, wq_txt, wq_ctl, wo_img, wo_txt, wo_ctl), wq, wo, sems)
-    for s in (2, 0, 1):
-        for copy in copies[s]:
+    for copy in (copies[2][0], copies[2][1], copies[0][0]):
+        copy.start()
+
+    def stream(s, parts, at, later):
+        count = parts[0].shape[0]
+        copies[s][0].wait()
+        copies[s][1].wait()
+        for copy in later:
             copy.start()
-
-    def stream(s, parts, at):
-        count = parts[0].shape[0]
-        for copy in copies[s]:
-            copy.wait()
         return back(s, *parts, wq.at[s], wo.at[s], mod, xhat[at : at + count, :], rstd[at : at + count, 0:1])
 
     def joint(at, count):
@@ -376,14 +367,14 @@
     head_back_main(recv, proj, gains, main)
     for copy in arrivals:
         copy.wait()
-    u, y_ctl = stream(2, [ctl_rows[:, j * WIDTH : (j + 1) * WIDTH] for j in range(4)], IMG + TXT)
+    u, y_ctl = stream(2, [ctl_rows[:, j * WIDTH : (j + 1) * WIDTH] for j in range(4)], IMG + TXT, (copies[0][1], copies[1][0]))
     slabs[:, 2 * SHARE : 3 * SHARE, :] = slab(u)
     leave(2 * SHARE, SHARE)
-    u, y = stream(0, joint(0, IMG), 0)
+    u, y = stream(0, joint(0, IMG), 0, (copies[1][1],))
     slabs[:, SHARE : 2 * SHARE, :] = slab(u)
     slabs[:, 0:SHARE, :] = slab(y + y_ctl)
     leave(0, 2 * SHARE)
-    u, y = stream(1, joint(IMG, TXT), IMG)
+    u, y = stream(1, joint(IMG, TXT), IMG, ())
     text = jnp.concatenate([y, u, jnp.zeros((IMG - 2 * TXT, D), F32)], 0).astype(BF16).T.astype(F32)
     for c in range(4):
         slabs[c, 3 * SHARE :, :] = pack_text(text[SHARE * c : SHARE * (c + 1)]).astype(BF16)
@@ -391,7 +382,7 @@
     results.finish()
 
 
-def weight_kernel(nz0, nz1, nz2, nz3, b0, b1, b2, b3, out):
+def weight_kernel(nz0, nz1, nz2, nz3, b0, b1, b2, b3, after, out):
     nz, blocks = (nz0, nz1, nz2, nz3), (b0, b1, b2, b3)
     total = jnp.concatenate(
         [
@@ -480,21 +471,14 @@
             shape((2 * IMG + TXT, D), F32),
             shape((2 * IMG + TXT, 128), F32),
         ] + [shape((2, SHARE, IMG), BF16)] * 4,
-        in_specs=[HBM] * 4 + [VMEM] * 2 + [HBM] * 6,
-        out_specs=[ANY] * 8,
+        in_specs=[VMEM] * 6 + [HBM] * 6,
+        out_specs=[VMEM] * 8,
         scratch_shapes=[
             pltpu.VMEM((3, 3, D, WIDTH), BF16),
             pltpu.VMEM((3, WIDTH, D), BF16),
             pltpu.VMEM((4, ROWS, IMG), BF16),
-            pltpu.VMEM((CTL_AT, CHUNK, 128), BF16),
-            pltpu.VMEM((BLOCKS - CTL_AT, CHUNK, 128), BF16),
-            pltpu.VMEM((2 * IMG + TXT, 2 * WIDTH), F32),
-            pltpu.VMEM((2 * IMG + TXT, D), F32),
-            pltpu.VMEM((2 * IMG + TXT, 128), F32),
             pltpu.VMEM((4, 2, SHARE, IMG), BF16),
-            pltpu.SemaphoreType.DMA((12,)),
-            pltpu.SemaphoreType.DMA((4,)),
-            pltpu.SemaphoreType.DMA((15,)),
+            pltpu.SemaphoreType.DMA((6,)),
         ],
         compiler_params=params(56),
         name="pre",
@@ -539,11 +523,11 @@
         name="head_back_ctl",
     )(back, proj, gains)
     blocks = shifted([ctl_rows] * 4, "z")
-    mine0, mine1, theirs0, theirs1 = pl.pallas_call(
+    mine0, mine1, theirs0, theirs1, token = pl.pallas_call(
         post_kernel,
-        out_shape=[rows] * 4,
+        out_shape=[rows] * 4 + [shape((8, 128), F32)],
         in_specs=[VMEM] * 4 + [HBM] * 2 + [VMEM] + [HBM] * 6,
-        out_specs=[ANY] * 4,
+        out_specs=[ANY] * 4 + [VMEM],
         scratch_shapes=[
             pltpu.VMEM((3, 3, D, WIDTH), BF16),
             pltpu.VMEM((3, WIDTH, D), BF16),
@@ -551,7 +535,7 @@
             pltpu.VMEM((2 * IMG + TXT, D), F32),
             pltpu.VMEM((2 * IMG + TXT, 128), F32),
             pltpu.VMEM((4, ROWS, IMG), BF16),
-            pltpu.SemaphoreType.DMA((12,)),
+            pltpu.SemaphoreType.DMA((6,)),
             pltpu.SemaphoreType.DMA((2,)),
             pltpu.SemaphoreType.DMA((12,)),
         ],
@@ -562,12 +546,12 @@
     terms = pl.pallas_call(
         weight_kernel,
         out_shape=shape((4, PIECE, 4 * WIDTH), BF16),
-        in_specs=[VMEM] * 8,
+        in_specs=[VMEM] * 8 + [SMEM],
         out_specs=VMEM,
         compiler_params=params(24),
         cost_estimate=pl.CostEstimate(flops=3_000_000_000, bytes_accessed=5_000_000, transcendentals=0),
         name="weight",
-    )(*nz, *blocks)
+    )(*nz, *blocks, token)
     got1 = lax.ppermute(theirs1, "tp", other_core)
     got0 = lax.ppermute(theirs0, "tp", other_core)
     passed = (mine1.astype(F32) + got1.astype(F32)).astype(BF16)

time: 208 us -> 192 us (0.923)
  Pallas kernels: 72.1 us -> 62.9 us
  waiting for transfers between devices: 66.9 us -> 59.7 us
    all_to_all x1, waiting for transfers between devices: 0.01 us -> 17.3 us  [per_device(): terms = lax.all_to_all(terms, 'y', 0, 0, tiled=True)]
    ppermute x6, waiting for transfers between devices: 37.6 us -> 23.2 us  [shifted(): lax.ppermute(parts[d], axis, [(i, (i + d) % 4) for i in range(4)])]
    ppermute x1, waiting for transfers between devices: 12.4 us -> 0.01 us  [per_device(): passed = lax.ppermute(passed, 'tp', other_chip)]
    pallas_call x1, Pallas kernels: 20.1 us -> 13.5 us  [per_device(): pl.pallas_call(pre_kernel, out_shape=[shape((BLOCKS, CHUNK, 128), BF16),...]
    pallas_call x1, Pallas kernels: 17.4 us -> 14.3 us  [per_device(): pl.pallas_call(post_kernel, out_shape=[rows] * 4 + [shape((8, 128), F32)]...]
    ppermute x1, waiting for transfers between devices: 1.7 us -> 3.88 us  [per_device(): theirs = lax.ppermute(theirs, 'w', [(0, 1), (1, 0)])]
  transfers between devices with their start and end apart: 15 -> 15, of which waited for: 9 -> 7; matrix products, arithmetic and copies ran while one was open for 1% -> 1% of each run, Pallas kernels for 22% -> 22%
where the time goes in v5:
time: 192 us
  Pallas kernels  62.9 us (33%)
  waiting for transfers between devices  59.7 us (31%)
  blocking collectives  33.1 us (17%)
  starting transfers between devices  28.4 us (15%)
  local copies, waits for them, and re-layouts  3.79 us (2%)
  other arithmetic  2.04 us (1%)
    all_to_all x1, blocking collectives, per_device(): back = lax.all_to_all(back, seq, 0, 0, tiled=True)  33.1 us
    pallas_call x1, Pallas kernels, per_device(): pl.pallas_call(attention_kernel, out_shape=[shape((keys, 128), BF16), sha...  24.7 us
    ppermute x6, waiting for transfers between devices, shifted(): lax.ppermute(parts[d], axis, [(i, (i + d) % 4) for i in range(4)])  23.2 us
    all_to_all x1, waiting for transfers between devices, per_device(): terms = lax.all_to_all(terms, 'y', 0, 0, tiled=True)  17.3 us
    pallas_call x1, Pallas kernels, per_device(): pl.pallas_call(post_kernel, out_shape=[rows] * 4 + [shape((8, 128), F32)]...  14.3 us
    pallas_call x1, Pallas kernels, per_device(): pl.pallas_call(pre_kernel, out_shape=[shape((BLOCKS, CHUNK, 128), BF16),...  13.5 us
    ppermute x1, waiting for transfers between devices, per_device(): from_chip = lax.ppermute(own, 'tp', other_chip)  11.7 us
    all_to_all x1, starting transfers between devices, per_device(): recv = lax.all_to_all(send, seq, 0, 0, tiled=True)  9.63 us
  transfers between devices with their start and end apart: 15, of which 7 were waited for; matrix products, arithmetic and copies ran while one was open for 1% of the time, Pallas kernels for 22%

profile of v5, /device:TPU:0, one launch (start us, length us, event | category | flops | bytes accessed | tf_op | source)
XLA Modules:
  0.0 191.6 jit_solution(17251764073897049793)
XLA Ops:
  0.6 1.9 %pack.1.in0 = bf16[1976,128]{1,0:T(8,128)(2,1)} custom-call(bf16[608,128]{1,0:T(8,128)(2,1)} %bitcast.12, bf16[608,128]{1,0:T(8,128)(2,1)} %bitcast.22, bf16[608,128]{1,0:T(8,128)(2,1)} %bitcast.14, bf16[16,608]{1,0:T(8,128)(2,1)} %txt.3, bf16[16,608]{1,0:T(8,128)(2,1)} %dy_txt.3), custom_call_target="tpu_custom_call" | custom-call | tf_op jit(solution)/shard_map/pack/pallas_call | solution.py:453
  2.6 3.2 %collective-permute-start.1 = (bf16[1976,128]{1,0:T(8,128)(2,1)}, bf16[1976,128]{1,0:T(8,128)(2,1)S(1)}, u32[]{:S(2)}, u32[]{:S(2)}) collective-permute-start(bf16[1976,128]{1,0:T(8,128)(2,1)} %pack.1.in0), channel_id=1, source_target_pairs={{0,2},{1,3},{2,0},{3,1},{4,6},{5,7},{6,4},{7,5},{8,10},{9,11},{10,... | collective-permute-start | bytes 1517576 | tf_op jit(solution)/shard_map/ppermute | solution.py:462
  5.8 11.7 %collective-permute-done.1.in2 = bf16[1976,128]{1,0:T(8,128)(2,1)S(1)} collective-permute-done((bf16[1976,128]{1,0:T(8,128)(2,1)}, bf16[1976,128]{1,0:T(8,128)(2,1)S(1)}, u32[]{:S(2)}, u32[]{:S(2)}) %collective-permute-start.1) | collective-permute-done | bytes 505888 | tf_op jit(solution)/shard_map/ppermute | solution.py:462
  17.5 1.9 collective-permute-done.2.in3
  19.4 0.8 copy-done.15
  20.2 13.5 %pre.1 = (bf16[32,192,128]{2,1,0:T(8,128)(2,1)}, f32[272,768]{1,0:T(8,128)}, f32[272,2432]{1,0:T(8,128)}, f32[272,128]{1,0:T(8,128)}, bf16[2,608,128]{2,1,0:T(8,...) custom-call(bf16[1976,128]{1,0:T(8,128)(2,1)} %pack.1.in0, ...), custom_call_target="tpu_custom_call" | custom-call | tf_op jit(solution)/shard_map/pre/pallas_call | solution.py:466
  33.7 9.6 %all-to-all-start = ((bf16[32,192,128]{2,1,0:T(8,128)(2,1)}), bf16[32,192,128]{2,1,0:T(8,128)(2,1)S(1)}, u32[]{:S(2)}, u32[]{:S(2)}) async-start(bf16[32,192,128]{2,1,0:T(8,128)(2,1)} %get-tuple-element.31), calls=%async_computation | async-start | bytes 3145728 | tf_op jit(solution)/shard_map/all_to_all | solution.py:487
  43.3 3.1 %collective-permute-start.3 = (bf16[2,608,128]{2,1,0:T(8,128)(2,1)S(1)}, bf16[2,608,128]{2,1,0:T(8,128)(2,1)S(1)}, u32[]{:S(2)}, u32[]{:S(2)}) collective-permute-start(bf16[2,608,128]{2,1,0:T(8,128)(2,1)S(1)} %copy-done.18), channel_id=1, source_target_pairs={{0,96},{32,0},{64,32},{96,64},{1,97},{33,1},{65,33},{97,65},{2,98}... | collective-permute-start | bytes 933896 | tf_op jit(solution)/shard_map/ppermute | solution.py:432
  47.2 2.3 %collective-permute-start.5 = (bf16[2,608,128]{2,1,0:T(8,128)(2,1)S(1)}, bf16[2,608,128]{2,1,0:T(8,128)(2,1)S(1)}, u32[]{:S(2)}, u32[]{:S(2)}) collective-permute-start(bf16[2,608,128]{2,1,0:T(8,128)(2,1)S(1)} %copy-done.16), channel_id=1, source_target_pairs={{0,64},{32,96},{64,0},{96,32},{1,65},{33,97},{65,1},{97,33},{2,66}... | collective-permute-start | bytes 933896 | tf_op jit(solution)/shard_map/ppermute | solution.py:432
  49.5 20.8 %collective-permute-done.3.after.nz3 = bf16[2,608,128]{2,1,0:T(8,128)(2,1)S(1)} collective-permute-done((bf16[2,608,128]{2,1,0:T(8,128)(2,1)S(1)}, bf16[2,608,128]{2,1,0:T(8,128)(2,1)S(1)}, u32[]{:S(2)}, u32[]{:S(2)}) %collective-permute-start.3) | collective-permute-done | bytes 311328 | tf_op jit(solution)/shard_map/ppermute | solution.py:432
  70.3 24.7 %attention.1 = (bf16[4608,128]{1,0:T(8,128)(2,1)S(1)}, bf16[2048,128]{1,0:T(8,128)(2,1)S(1)}) custom-call(s32[2]{0:T(128)S(1)} %pad_add_fusion.role, bf16[32,192,128]{2,1,0:T(8,128)(2,1)S(1)} %all-to-all-done.recv, bf16[2,608,128]{2,1,0:T(8,128)(2,1)S(1)} %collective-permute-done.3.after.nz3), custom_call_target="tpu_custom_call" | custom-call | flops 40000000000 | bytes 3200000 | tf_op jit(solution)/shard_map/attention/pallas_call | solution.py:490
  95.1 0.7 scatter.1
  95.8 33.1 %all_to_all.15.recv = bf16[32,192,128]{2,1,0:T(8,128)(2,1)S(1)} all-to-all(bf16[32,192,128]{2,1,0:T(8,128)(2,1)S(1)} %scatter.1), channel_id=1, replica_groups=mesh['z'=4,'y'=4,'w'=2,'tp'=4] {'z','y','w'}, dimensions={0} | all-to-all | bytes 3145728 | tf_op jit(solution)/shard_map/all_to_all | solution.py:515
  128.9 2.5 %head_back_ctl.1.ctl_rows.b0 = bf16[128,1536]{1,0:T(8,128)(2,1)S(1)} custom-call(bf16[32,192,128]{2,1,0:T(8,128)(2,1)S(1)} %all_to_all.15.recv, f32[272,768]{1,0:T(8,128)S(1)} %copy-done.2, f32[3,2,64]{2,1,0:T(2,128)S(1)} %copy-done.10), custom_call_target="tpu_custom_call" | custom-call | tf_op jit(solution)/shard_map/head_back_ctl/pallas_call | solution.py:517
  131.4 0.9 collective-permute-start.11
  132.3 0.5 collective-permute-start.10
  132.9 0.9 collective-permute-start.9
  133.7 14.3 %post.1 = (bf16[1976,128]{1,0:T(8,128)(2,1)}, bf16[1976,128]{1,0:T(8,128)(2,1)}, bf16[1976,128]{1,0:T(8,128)(2,1)}, bf16[1976,128]{1,0:T(8,128)(2,1)}, f32[8,128]{1,0:T(8,128)}) custom-call(bf16[32,192,128]{2,1,0:T(8,128)(2,1)} %copy-done, f32[272,768]{1,0:T(8,128)} %get-tuple-element.37.proj, f32[3,2,64]{2,1,0:T(2,128)} %gains.5, ...), custom_call_target="tpu_custom_call" | custom-call | flops 14000000000 | bytes 30000000 | tf_op jit(solution)/shard_map/post/pallas_call | solution.py:526
  148.1 2.4 %collective-permute-done.9.b1 = bf16[128,1536]{1,0:T(8,128)(2,1)S(1)} collective-permute-done((bf16[128,1536]{1,0:T(8,128)(2,1)S(1)}, bf16[128,1536]{1,0:T(8,128)(2,1)S(1)}, u32[]{:S(2)}, u32[]{:S(2)}) %collective-permute-start.9) | collective-permute-done | bytes 393248 | tf_op jit(solution)/shard_map/ppermute | solution.py:432
  150.5 1.0 copy-done.7
  151.5 0.7 copy-done.12
  152.2 1.9 weight.1
  154.1 1.3 copy-done.1
  155.4 3.6 %all-to-all-start.2 = ((bf16[4,152,1536]{2,1,0:T(8,128)(2,1)}), bf16[4,152,1536]{2,1,0:T(8,128)(2,1)S(1)}, u32[]{:S(2)}, u32[]{:S(2)}) async-start(bf16[4,152,1536]{2,1,0:T(8,128)(2,1)} %copy-done.1), calls=%async_computation.2 | async-start | bytes 3735552 | tf_op jit(solution)/shard_map/all_to_all | solution.py:559
  159.6 1.6 collective-permute-done.7
  161.2 2.0 %add_convert_fusion = bf16[1976,128]{1,0:T(8,128)(2,1)} fusion(bf16[1976,128]{1,0:T(8,128)(2,1)S(1)} %collective-permute-done.7, bf16[1976,128]{1,0:T(8,128)(2,1)} %get-tuple-element.42), kind=kLoop, calls=%fused_computation | loop fusion | flops 1011712 | bytes 1517568 | tf_op jit(solution)/shard_map/convert_element_type | solution.py:557
  163.2 2.8 %collective-permute-start.8 = (bf16[1976,128]{1,0:T(8,128)(2,1)}, bf16[1976,128]{1,0:T(8,128)(2,1)}, u32[]{:S(2)}, u32[]{:S(2)}) collective-permute-start(bf16[1976,128]{1,0:T(8,128)(2,1)} %add_convert_fusion), channel_id=1, source_target_pairs={{0,2},{1,3},{2,0},{3,1},{4,6},{5,7},{6,4},{7,5},{8,10},{9,11},{10,... | collective-permute-start | bytes 1517576 | tf_op jit(solution)/shard_map/ppermute | solution.py:558
  165.9 17.3 %all-to-all-done.2.terms = bf16[4,152,1536]{2,1,0:T(8,128)(2,1)S(1)} async-done(((bf16[4,152,1536]{2,1,0:T(8,128)(2,1)}), bf16[4,152,1536]{2,1,0:T(8,128)(2,1)S(1)}, u32[]{:S(2)}, u32[]{:S(2)}) %all-to-all-start.2) | async-done | bytes 1867808 | tf_op jit(solution)/shard_map/all_to_all | solution.py:559
  183.6 1.0 collective-permute-start.12
  184.7 2.2 %final.1 = (bf16[608,128]{1,0:T(8,128)(2,1)}, bf16[608,128]{1,0:T(8,128)(2,1)}, bf16[608,128]{1,0:T(8,128)(2,1)}, bf16[16,608]{1,0:T(8,128)(2,1)}, bf16[16,608]{1,0:T(8,128)(2,1)}) custom-call(bf16[608,128]{1,0:T(8,128)(2,1)S(1)} %bitcast.13, bf16[608,128]{1,0:T(8,128)(2,1)S(1)} %bitcast.15, bf16[16,608]{1,0:T(8,128)(2,1)S(1)} %copy-done.8, ...), custom_call_target="tpu_custom_call" | custom-call | tf_op jit(solution)/shard_map/final/pallas_call | solution.py:578
  186.9 3.9 %collective-permute-done.12.other = bf16[76,1536]{1,0:T(8,128)(2,1)S(1)} collective-permute-done((bf16[76,1536]{1,0:T(8,128)(2,1)S(1)}, bf16[76,1536]{1,0:T(8,128)(2,1)S(1)}, u32[]{:S(2)}, u32[]{:S(2)}) %collective-permute-start.12) | collective-permute-done | bytes 233504 | tf_op jit(solution)/shard_map/ppermute | solution.py:568
  190.8 0.8 weight_out.1
  (49 shorter events, 1.2 us)
Async XLA Ops:
  2.6 14.9 %collective-permute-start.1 = (bf16[1976,128]{1,0:T(8,128)(2,1)}, bf16[1976,128]{1,0:T(8,128)(2,1)S(1)}, u32[]{:S(2)}, u32[]{:S(2)}) collective-permute-start(bf16[1976,128]{1,0:T(8,128)(2,1)} %pack.1.in0), channel_id=1, source_target_pairs={{0,2},{1,3},{2,0},{3,1},{4,6},{5,7},{6,4},{7,5},{8,10},{9,11},{10,... | collective-permute-start | bytes 1517576 | tf_op jit(solution)/shard_map/ppermute | solution.py:462
  5.8 11.7 %collective-permute-start = (bf16[1976,128]{1,0:T(8,128)(2,1)}, bf16[1976,128]{1,0:T(8,128)(2,1)S(1)}, u32[]{:S(2)}, u32[]{:S(2)}) collective-permute-start(bf16[1976,128]{1,0:T(8,128)(2,1)} %pack.1.in0), channel_id=1, source_target_pairs={{0,1},{1,0},{2,3},{3,2},{4,5},{5,4},{6,7},{7,6},{8,9},{9,8},{10,11... | collective-permute-start | bytes 1517576 | tf_op jit(solution)/shard_map/ppermute | solution.py:463
  17.5 1.9 copy-start.13
  17.5 1.9 collective-permute-start.2
  17.5 1.9 copy-start.14
  33.7 9.7 %copy-start.18 = (bf16[2,608,128]{2,1,0:T(8,128)(2,1)S(1)}, bf16[2,608,128]{2,1,0:T(8,128)(2,1)}, u32[]{:S(2)}) copy-start(bf16[2,608,128]{2,1,0:T(8,128)(2,1)} %get-tuple-element.32) | copy-start | bytes 933892
  33.7 13.5 %copy-start.17 = (bf16[2,608,128]{2,1,0:T(8,128)(2,1)S(1)}, bf16[2,608,128]{2,1,0:T(8,128)(2,1)}, u32[]{:S(2)}) copy-start(bf16[2,608,128]{2,1,0:T(8,128)(2,1)} %get-tuple-element.35) | copy-start | bytes 933892
  33.7 13.5 %copy-start.16 = (bf16[2,608,128]{2,1,0:T(8,128)(2,1)S(1)}, bf16[2,608,128]{2,1,0:T(8,128)(2,1)}, u32[]{:S(2)}) copy-start(bf16[2,608,128]{2,1,0:T(8,128)(2,1)} %get-tuple-element.36) | copy-start | bytes 933892
  33.7 36.6 %all-to-all-start = ((bf16[32,192,128]{2,1,0:T(8,128)(2,1)}), bf16[32,192,128]{2,1,0:T(8,128)(2,1)S(1)}, u32[]{:S(2)}, u32[]{:S(2)}) async-start(bf16[32,192,128]{2,1,0:T(8,128)(2,1)} %get-tuple-element.31), calls=%async_computation | async-start | bytes 3145728 | tf_op jit(solution)/shard_map/all_to_all | solution.py:487
  43.3 27.0 %collective-permute-start.3 = (bf16[2,608,128]{2,1,0:T(8,128)(2,1)S(1)}, bf16[2,608,128]{2,1,0:T(8,128)(2,1)S(1)}, u32[]{:S(2)}, u32[]{:S(2)}) collective-permute-start(bf16[2,608,128]{2,1,0:T(8,128)(2,1)S(1)} %copy-done.18), channel_id=1, source_target_pairs={{0,96},{32,0},{64,32},{96,64},{1,97},{33,1},{65,33},{97,65},{2,98}... | collective-permute-start | bytes 933896 | tf_op jit(solution)/shard_map/ppermute | solution.py:432
  47.2 47.9 %collective-permute-start.4 = (bf16[2,608,128]{2,1,0:T(8,128)(2,1)S(1)}, bf16[2,608,128]{2,1,0:T(8,128)(2,1)S(1)}, u32[]{:S(2)}, u32[]{:S(2)}) collective-permute-start(bf16[2,608,128]{2,1,0:T(8,128)(2,1)S(1)} %copy-done.17), channel_id=1, source_target_pairs={{0,32},{32,64},{64,96},{96,0},{1,33},{33,65},{65,97},{97,1},{2,34}... | collective-permute-start | bytes 933896 | tf_op jit(solution)/shard_map/ppermute | solution.py:432
  47.2 47.8 %collective-permute-start.5 = (bf16[2,608,128]{2,1,0:T(8,128)(2,1)S(1)}, bf16[2,608,128]{2,1,0:T(8,128)(2,1)S(1)}, u32[]{:S(2)}, u32[]{:S(2)}) collective-permute-start(bf16[2,608,128]{2,1,0:T(8,128)(2,1)S(1)} %copy-done.16), channel_id=1, source_target_pairs={{0,64},{32,96},{64,0},{96,32},{1,65},{33,97},{65,1},{97,33},{2,66}... | collective-permute-start | bytes 933896 | tf_op jit(solution)/shard_map/ppermute | solution.py:432
  95.7 33.2 %copy-start.2 = (f32[272,768]{1,0:T(8,128)S(1)}, f32[272,768]{1,0:T(8,128)}, u32[]{:S(2)}) copy-start(f32[272,768]{1,0:T(8,128)} %get-tuple-element.37.proj) | copy-start | bytes 2506756
  95.7 33.2 %copy-start.10 = (f32[3,2,64]{2,1,0:T(2,128)S(1)}, f32[3,2,64]{2,1,0:T(2,128)}, u32[]{:S(2)}) copy-start(f32[3,2,64]{2,1,0:T(2,128)} %gains.5) | copy-start | bytes 4612
  128.9 4.8 %copy-start = (bf16[32,192,128]{2,1,0:T(8,128)(2,1)}, bf16[32,192,128]{2,1,0:T(8,128)(2,1)S(1)}, u32[]{:S(2)}) copy-start(bf16[32,192,128]{2,1,0:T(8,128)(2,1)S(1)} %all_to_all.15.recv) | copy-start | bytes 4718596
  131.4 2.3 %copy-start.6 = (bf16[128,1536]{1,0:T(8,128)(2,1)}, bf16[128,1536]{1,0:T(8,128)(2,1)S(1)}, u32[]{:S(2)}) copy-start(bf16[128,1536]{1,0:T(8,128)(2,1)S(1)} %head_back_ctl.1.ctl_rows.b0) | copy-start | bytes 1179652
  131.4 16.6 %collective-permute-start.11 = (bf16[128,1536]{1,0:T(8,128)(2,1)S(1)}, bf16[128,1536]{1,0:T(8,128)(2,1)S(1)}, u32[]{:S(2)}, u32[]{:S(2)}) collective-permute-start(bf16[128,1536]{1,0:T(8,128)(2,1)S(1)} %head_back_ctl.1.ctl_rows.b0), channel_id=1, source_target_pairs={{0,96},{32,0},{64,32},{96,64},{1,97},{33,1},{65,33},{97,65},{2,98}... | collective-permute-start | bytes 1179656 | tf_op jit(solution)/shard_map/ppermute | solution.py:432
  132.3 15.8 %collective-permute-start.10 = (bf16[128,1536]{1,0:T(8,128)(2,1)S(1)}, bf16[128,1536]{1,0:T(8,128)(2,1)S(1)}, u32[]{:S(2)}, u32[]{:S(2)}) collective-permute-start(bf16[128,1536]{1,0:T(8,128)(2,1)S(1)} %head_back_ctl.1.ctl_rows.b0), channel_id=1, source_target_pairs={{0,64},{32,96},{64,0},{96,32},{1,65},{33,97},{65,1},{97,33},{2,66}... | collective-permute-start | bytes 1179656 | tf_op jit(solution)/shard_map/ppermute | solution.py:432
  132.9 17.7 %collective-permute-start.9 = (bf16[128,1536]{1,0:T(8,128)(2,1)S(1)}, bf16[128,1536]{1,0:T(8,128)(2,1)S(1)}, u32[]{:S(2)}, u32[]{:S(2)}) collective-permute-start(bf16[128,1536]{1,0:T(8,128)(2,1)S(1)} %head_back_ctl.1.ctl_rows.b0), channel_id=1, source_target_pairs={{0,32},{32,64},{64,96},{96,0},{1,33},{33,65},{65,97},{97,1},{2,34}... | collective-permute-start | bytes 1179656 | tf_op jit(solution)/shard_map/ppermute | solution.py:432
  133.7 16.8 %copy-start.11 = (bf16[2,608,128]{2,1,0:T(8,128)(2,1)S(1)}, bf16[2,608,128]{2,1,0:T(8,128)(2,1)}, u32[]{:S(2)}) copy-start(bf16[2,608,128]{2,1,0:T(8,128)(2,1)} %get-tuple-element.49.nz0) | copy-start | bytes 933892
  150.5 1.0 copy-start.7
  154.1 1.3 copy-start.1
  155.4 27.9 %all-to-all-start.2 = ((bf16[4,152,1536]{2,1,0:T(8,128)(2,1)}), bf16[4,152,1536]{2,1,0:T(8,128)(2,1)S(1)}, u32[]{:S(2)}, u32[]{:S(2)}) async-start(bf16[4,152,1536]{2,1,0:T(8,128)(2,1)} %copy-done.1), calls=%async_computation.2 | async-start | bytes 3735552 | tf_op jit(solution)/shard_map/all_to_all | solution.py:559
  159.0 25.7 %copy-start.3 = (bf16[128,608]{0,1:T(8,128)(2,1)S(1)}, bf16[128,608]{0,1:T(8,128)(2,1)}, u32[]{:S(2)}) copy-start(bf16[128,608]{0,1:T(8,128)(2,1)} %param.14) | copy-start | bytes 466948
  159.0 25.7 %copy-start.4 = (bf16[128,608]{0,1:T(8,128)(2,1)S(1)}, bf16[128,608]{0,1:T(8,128)(2,1)}, u32[]{:S(2)}) copy-start(bf16[128,608]{0,1:T(8,128)(2,1)} %param.17) | copy-start | bytes 466948
  159.0 25.7 %copy-start.5 = (bf16[1976,128]{1,0:T(8,128)(2,1)S(1)}, bf16[1976,128]{1,0:T(8,128)(2,1)}, u32[]{:S(2)}) copy-start(bf16[1976,128]{1,0:T(8,128)(2,1)} %get-tuple-element.40.part0) | copy-start | bytes 1517572
  159.0 25.7 %copy-start.8 = (bf16[16,608]{1,0:T(8,128)(2,1)S(1)}, bf16[16,608]{1,0:T(8,128)(2,1)}, u32[]{:S(2)}) copy-start(bf16[16,608]{1,0:T(8,128)(2,1)} %txt.3) | copy-start | bytes 58372
  159.0 25.7 %copy-start.9 = (bf16[16,608]{1,0:T(8,128)(2,1)S(1)}, bf16[16,608]{1,0:T(8,128)(2,1)}, u32[]{:S(2)}) copy-start(bf16[16,608]{1,0:T(8,128)(2,1)} %dy_txt.3) | copy-start | bytes 58372
  159.0 2.2 %collective-permute-start.7 = (bf16[1976,128]{1,0:T(8,128)(2,1)}, bf16[1976,128]{1,0:T(8,128)(2,1)S(1)}, u32[]{:S(2)}, u32[]{:S(2)}) collective-permute-start(bf16[1976,128]{1,0:T(8,128)(2,1)} %get-tuple-element.43), channel_id=1, source_target_pairs={{0,1},{1,0},{2,3},{3,2},{4,5},{5,4},{6,7},{7,6},{8,9},{9,8},{10,11... | collective-permute-start | bytes 1517576 | tf_op jit(solution)/shard_map/ppermute | solution.py:555
  159.1 25.5 %collective-permute-start.6 = (bf16[1976,128]{1,0:T(8,128)(2,1)}, bf16[1976,128]{1,0:T(8,128)(2,1)S(1)}, u32[]{:S(2)}, u32[]{:S(2)}) collective-permute-start(bf16[1976,128]{1,0:T(8,128)(2,1)} %get-tuple-element.41), channel_id=1, source_target_pairs={{0,1},{1,0},{2,3},{3,2},{4,5},{5,4},{6,7},{7,6},{8,9},{9,8},{10,11... | collective-permute-start | bytes 1517576 | tf_op jit(solution)/shard_map/ppermute | solution.py:556
  163.2 21.5 %collective-permute-start.8 = (bf16[1976,128]{1,0:T(8,128)(2,1)}, bf16[1976,128]{1,0:T(8,128)(2,1)}, u32[]{:S(2)}, u32[]{:S(2)}) collective-permute-start(bf16[1976,128]{1,0:T(8,128)(2,1)} %add_convert_fusion), channel_id=1, source_target_pairs={{0,2},{1,3},{2,0},{3,1},{4,6},{5,7},{6,4},{7,5},{8,10},{9,11},{10,... | collective-permute-start | bytes 1517576 | tf_op jit(solution)/shard_map/ppermute | solution.py:558
  183.6 7.1 %collective-permute-start.12 = (bf16[76,1536]{1,0:T(8,128)(2,1)S(1)}, bf16[76,1536]{1,0:T(8,128)(2,1)S(1)}, u32[]{:S(2)}, u32[]{:S(2)}) collective-permute-start(bf16[76,1536]{1,0:T(8,128)(2,1)S(1)} %get-tuple-element.52), channel_id=1, source_target_pairs={{0,4},{4,0},{1,5},{5,1},{2,6},{6,2},{3,7},{7,3},{8,12},{12,8},{9,1... | collective-permute-start | bytes 700424 | tf_op jit(solution)/shard_map/ppermute | solution.py:568
  (2 other events, 1.5 us)

commit v6 on v5

--- a/solution.py
+++ b/solution.py
@@ -74,6 +74,22 @@
     ]
 
 
+def order_kernel(after, *refs):
+    pass
+
+
+def ordered(arrays, after):
+    return pl.pallas_call(
+        order_kernel,
+        out_shape=[jax.ShapeDtypeStruct(x.shape, x.dtype) for x in arrays],
+        in_specs=[ANY] * (1 + len(arrays)),
+        out_specs=[ANY] * len(arrays),
+        input_output_aliases={1 + i: i for i in range(len(arrays))},
+        compiler_params=params(1),
+        name="order",
+    )(after, *arrays)
+
+
 def pack_kernel(img, ctl, dy, txt, dy_txt, out, text_rows, sems):
     copies = [
         pltpu.make_async_copy(part, text_rows.at[i], sems.at[3 + i]) for i, part in enumerate((txt, dy_txt))
@@ -128,7 +144,7 @@
         centered = x - jnp.mean(x, axis=-1, keepdims=True)
         inverse = lax.rsqrt(jnp.mean(centered * centered, axis=-1, keepdims=True) + EPS)
         standard = centered * inverse
-        xhat[at : at + count, :] = standard
+        xhat[at : at + count, :] = standard.astype(BF16)
         rstd[at : at + count, :] = jnp.broadcast_to(inverse, (count, 128))
         n = (standard * (1.0 + mod[s, 1:2, :]) + mod[s, 0:1, :]).astype(BF16)
         copies[s][0].wait()
@@ -179,7 +195,7 @@
         out[...] = nz[lax.rem(lax.axis_index("z") + d, 4)]
 
 
-def attention_kernel(role, recv, after, dkv_out, odq, kv, kt, vt, qg, probs, dkv):
+def attention_kernel(role, recv, dkv_out, odq, kv, kt, vt, qg, probs, dkv):
     is_main = role[0]
     live = role[1]
 
@@ -258,7 +274,7 @@
     dkv_out[...] = dkv[...].astype(BF16)
 
 
-def scatter_kernel(role, dkv, odq, after0, after1, out):
+def scatter_kernel(role, dkv, odq, after0, after1, after2, out):
     for b in range(BLOCKS):
         out[b, 0:IMG, :] = dkv[IMG * b : IMG * (b + 1), :]
 
@@ -355,7 +371,7 @@
         copies[s][1].wait()
         for copy in later:
             copy.start()
-        return back(s, *parts, wq.at[s], wo.at[s], mod, xhat[at : at + count, :], rstd[at : at + count, 0:1])
+        return back(s, *parts, wq.at[s], wo.at[s], mod, xhat[at : at + count, :].astype(F32), rstd[at : at + count, 0:1])
 
     def joint(at, count):
         return [main[at : at + count, j * WIDTH : (j + 1) * WIDTH] for j in range(4)]
@@ -468,7 +484,7 @@
         out_shape=[
             shape((BLOCKS, CHUNK, 128), BF16),
             shape((2 * IMG + TXT, 2 * WIDTH), F32),
-            shape((2 * IMG + TXT, D), F32),
+            shape((2 * IMG + TXT, D), BF16),
             shape((2 * IMG + TXT, 128), F32),
         ] + [shape((2, SHARE, IMG), BF16)] * 4,
         in_specs=[VMEM] * 6 + [HBM] * 6,
@@ -485,12 +501,12 @@
     )(own, from_core, from_chip, from_both, mod, gains, *weights)
 
     recv = lax.all_to_all(send, seq, 0, 0, tiled=True)
-    nz = shifted(slabs, "z")
+    nz = shifted([slabs[0], *ordered(slabs[1:], recv)], "z")
     keys = IMAGE_KEYS + TEXT_KEYS
     dkv, odq = pl.pallas_call(
         attention_kernel,
         out_shape=[shape((keys, 128), BF16), shape((BLOCKS * CTL_Q, 128), BF16)],
-        in_specs=[SMEM, VMEM, ANY],
+        in_specs=[SMEM, VMEM],
         out_specs=[VMEM] * 2,
         scratch_shapes=[
             pltpu.VMEM((keys, 128), BF16),
@@ -503,15 +519,15 @@
         compiler_params=params(32),
         cost_estimate=pl.CostEstimate(flops=40_000_000_000, bytes_accessed=3_200_000, transcendentals=8_400_000),
         name="attention",
-    )(role, recv, nz[3])
+    )(role, recv)
     back = pl.pallas_call(
         scatter_kernel,
         out_shape=shape((BLOCKS, CHUNK, 128), BF16),
-        in_specs=[SMEM] + [VMEM] * 2 + [ANY] * 2,
+        in_specs=[SMEM] + [VMEM] * 2 + [ANY] * 3,
         out_specs=VMEM,
         compiler_params=params(16),
         name="scatter",
-    )(role, dkv, odq, *nz[1:3])
+    )(role, dkv, odq, *nz[1:])
     back = lax.all_to_all(back, seq, 0, 0, tiled=True)
 
     ctl_rows = pl.pallas_call(
@@ -532,7 +548,7 @@
             pltpu.VMEM((3, 3, D, WIDTH), BF16),
             pltpu.VMEM((3, WIDTH, D), BF16),
             pltpu.VMEM((IMG + TXT, 4 * WIDTH), BF16),
-            pltpu.VMEM((2 * IMG + TXT, D), F32),
+            pltpu.VMEM((2 * IMG + TXT, D), BF16),
             pltpu.VMEM((2 * IMG + TXT, 128), F32),
             pltpu.VMEM((4, ROWS, IMG), BF16),
             pltpu.SemaphoreType.DMA((6,)),

time: 192 us -> 188 us (0.979)
  local copies, waits for them, and re-layouts: 3.79 us -> 8.49 us
  blocking collectives: 33.1 us -> 29.7 us
  starting transfers between devices: 28.4 us -> 25.6 us
    all_to_all x1, waiting for transfers between devices: 0.01 us -> 23.1 us  [per_device(): recv = lax.all_to_all(send, seq, 0, 0, tiled=True)]
    ppermute x6, waiting for transfers between devices: 23.2 us -> 1.57 us  [shifted(): lax.ppermute(parts[d], axis, [(i, (i + d) % 4) for i in range(4)])]
    unnamed x38 -> x44, local copies, waits for them, and re-layouts: 3.79 us -> 8.49 us
    ppermute x1, waiting for transfers between devices: 3.88 us -> 0.01 us  [per_device(): theirs = lax.ppermute(theirs, 'w', [(0, 1), (1, 0)])]
    all_to_all x1, blocking collectives: 33.1 us -> 29.7 us  [per_device(): back = lax.all_to_all(back, seq, 0, 0, tiled=True)]
  transfers between devices with their start and end apart: 15 -> 15, of which waited for: 7 -> 6; matrix products, arithmetic and copies ran while one was open for 1% -> 1% of each run, Pallas kernels for 22% -> 22%
where the time goes in v6:
time: 188 us; the launch traced here: 187 us
  Pallas kernels  63.1 us (34%)
  waiting for transfers between devices  57.9 us (31%)
  blocking collectives  29.7 us (16%)
  starting transfers between devices  25.6 us (14%)
  local copies, waits for them, and re-layouts  8.49 us (5%)
    all_to_all x1, blocking collectives, per_device(): back = lax.all_to_all(back, seq, 0, 0, tiled=True)  29.7 us
    pallas_call x1, Pallas kernels, per_device(): pl.pallas_call(attention_kernel, out_shape=[shape((keys, 128), BF16), sha...  24.8 us
    all_to_all x1, waiting for transfers between devices, per_device(): recv = lax.all_to_all(send, seq, 0, 0, tiled=True)  23.1 us
    all_to_all x1, waiting for transfers between devices, per_device(): terms = lax.all_to_all(terms, 'y', 0, 0, tiled=True)  18 us
    pallas_call x1, Pallas kernels, per_device(): pl.pallas_call(post_kernel, out_shape=[rows] * 4 + [shape((8, 128), F32)]...  14.4 us
    pallas_call x1, Pallas kernels, per_device(): pl.pallas_call(pre_kernel, out_shape=[shape((BLOCKS, CHUNK, 128), BF16),...  13.5 us
    ppermute x1, waiting for transfers between devices, per_device(): from_chip = lax.ppermute(own, 'tp', other_chip)  11.7 us
    all_to_all x1, starting transfers between devices, per_device(): recv = lax.all_to_all(send, seq, 0, 0, tiled=True)  9.63 us
  transfers between devices with their start and end apart: 15, of which 6 were waited for; matrix products, arithmetic and copies ran while one was open for 1% of the time, Pallas kernels for 22%

profile of v6, /device:TPU:0, one launch (start us, length us, event | category | flops | bytes accessed | tf_op | source)
XLA Modules:
  0.0 187.4 jit_solution(9947555878776001560)
XLA Ops:
  0.6 1.9 %pack.1.in0 = bf16[1976,128]{1,0:T(8,128)(2,1)} custom-call(bf16[608,128]{1,0:T(8,128)(2,1)} %bitcast.12, bf16[608,128]{1,0:T(8,128)(2,1)} %bitcast.22, bf16[608,128]{1,0:T(8,128)(2,1)} %bitcast.14, bf16[16,608]{1,0:T(8,128)(2,1)} %txt.3, bf16[16,608]{1,0:T(8,128)(2,1)} %dy_txt.3), custom_call_target="tpu_custom_call" | custom-call | tf_op jit(solution)/shard_map/pack/pallas_call | solution.py:469
  2.6 3.2 %collective-permute-start.1 = (bf16[1976,128]{1,0:T(8,128)(2,1)}, bf16[1976,128]{1,0:T(8,128)(2,1)S(1)}, u32[]{:S(2)}, u32[]{:S(2)}) collective-permute-start(bf16[1976,128]{1,0:T(8,128)(2,1)} %pack.1.in0), channel_id=1, source_target_pairs={{0,2},{1,3},{2,0},{3,1},{4,6},{5,7},{6,4},{7,5},{8,10},{9,11},{10,... | collective-permute-start | bytes 1517576 | tf_op jit(solution)/shard_map/ppermute | solution.py:478
  5.8 11.7 %collective-permute-done.1.in2 = bf16[1976,128]{1,0:T(8,128)(2,1)S(1)} collective-permute-done((bf16[1976,128]{1,0:T(8,128)(2,1)}, bf16[1976,128]{1,0:T(8,128)(2,1)S(1)}, u32[]{:S(2)}, u32[]{:S(2)}) %collective-permute-start.1) | collective-permute-done | bytes 505888 | tf_op jit(solution)/shard_map/ppermute | solution.py:478
  17.5 1.9 collective-permute-done.2.in3
  19.4 0.8 copy-done.21
  20.2 13.5 %pre.1 = (bf16[32,192,128]{2,1,0:T(8,128)(2,1)}, f32[272,768]{1,0:T(8,128)}, bf16[272,2432]{1,0:T(8,128)(2,1)}, f32[272,128]{1,0:T(8,128)}, bf16[2,608,128]{2,1,...) custom-call(bf16[1976,128]{1,0:T(8,128)(2,1)} %pack.1.in0, ...), custom_call_target="tpu_custom_call" | custom-call | tf_op jit(solution)/shard_map/pre/pallas_call | solution.py:482
  33.7 9.6 %all-to-all-start = ((bf16[32,192,128]{2,1,0:T(8,128)(2,1)}), bf16[32,192,128]{2,1,0:T(8,128)(2,1)S(1)}, u32[]{:S(2)}, u32[]{:S(2)}) async-start(bf16[32,192,128]{2,1,0:T(8,128)(2,1)} %get-tuple-element.34), calls=%async_computation | async-start | bytes 3145728 | tf_op jit(solution)/shard_map/all_to_all | solution.py:503
  44.1 23.1 %all-to-all-done.recv.after = bf16[32,192,128]{2,1,0:T(8,128)(2,1)S(1)} async-done(((bf16[32,192,128]{2,1,0:T(8,128)(2,1)}), bf16[32,192,128]{2,1,0:T(8,128)(2,1)S(1)}, u32[]{:S(2)}, u32[]{:S(2)}) %all-to-all-start) | async-done | bytes 1572896 | tf_op jit(solution)/shard_map/all_to_all | solution.py:503
  67.3 2.3 %collective-permute-start.4 = (bf16[2,608,128]{2,1,0:T(8,128)(2,1)S(1)}, bf16[2,608,128]{2,1,0:T(8,128)(2,1)S(1)}, u32[]{:S(2)}, u32[]{:S(2)}) collective-permute-start(bf16[2,608,128]{2,1,0:T(8,128)(2,1)S(1)} %get-tuple-element.41), channel_id=1, source_target_pairs={{0,64},{32,96},{64,0},{96,32},{1,65},{33,97},{65,1},{97,33},{2,66}... | collective-permute-start | bytes 933896 | tf_op jit(solution)/shard_map/ppermute | solution.py:448
  69.6 1.2 collective-permute-start.5
  70.7 24.8 %attention.1 = (bf16[4608,128]{1,0:T(8,128)(2,1)S(1)}, bf16[2048,128]{1,0:T(8,128)(2,1)S(1)}) custom-call(s32[2]{0:T(128)S(1)} %pad_add_fusion.role, bf16[32,192,128]{2,1,0:T(8,128)(2,1)S(1)} %all-to-all-done.recv.after), custom_call_target="tpu_custom_call" | custom-call | flops 40000000000 | bytes 3200000 | tf_op jit(solution)/shard_map/attention/pallas_call | solution.py:506
  96.2 29.7 %all_to_all.15.recv = bf16[32,192,128]{2,1,0:T(8,128)(2,1)S(1)} all-to-all(bf16[32,192,128]{2,1,0:T(8,128)(2,1)S(1)} %scatter.1), channel_id=1, replica_groups=mesh['z'=4,'y'=4,'w'=2,'tp'=4] {'z','y','w'}, dimensions={0} | all-to-all | bytes 3145728 | tf_op jit(solution)/shard_map/all_to_all | solution.py:531
  125.9 2.5 %head_back_ctl.1.ctl_rows.b0 = bf16[128,1536]{1,0:T(8,128)(2,1)S(1)} custom-call(bf16[32,192,128]{2,1,0:T(8,128)(2,1)S(1)} %all_to_all.15.recv, f32[272,768]{1,0:T(8,128)S(1)} %copy-done.2, f32[3,2,64]{2,1,0:T(2,128)S(1)} %copy-done.15), custom_call_target="tpu_custom_call" | custom-call | tf_op jit(solution)/shard_map/head_back_ctl/pallas_call | solution.py:533
  128.5 0.9 collective-permute-start.11
  129.9 0.9 collective-permute-start.9
  130.7 14.4 %post.1 = (bf16[1976,128]{1,0:T(8,128)(2,1)}, bf16[1976,128]{1,0:T(8,128)(2,1)}, bf16[1976,128]{1,0:T(8,128)(2,1)}, bf16[1976,128]{1,0:T(8,128)(2,1)}, f32[8,128]{1,0:T(8,128)}) custom-call(bf16[32,192,128]{2,1,0:T(8,128)(2,1)} %copy-done, f32[272,768]{1,0:T(8,128)} %get-tuple-element.43.proj, f32[3,2,64]{2,1,0:T(2,128)} %gains.5, ...), custom_call_target="tpu_custom_call" | custom-call | flops 14000000000 | bytes 30000000 | tf_op jit(solution)/shard_map/post/pallas_call | solution.py:542
  145.2 1.6 collective-permute-done.9.b1
  146.8 1.0 copy-done.9
  148.5 1.9 %weight.1 = bf16[4,152,1536]{2,1,0:T(8,128)(2,1)S(1)} custom-call(bf16[2,608,128]{2,1,0:T(8,128)(2,1)S(1)} %copy-done.16, bf16[2,608,128]{2,1,0:T(8,128)(2,1)S(1)} %collective-permute-done.3.after0.nz1, bf16[2,608,128]{2,1,0:T(8,128)(2,1)S(1)} %collective-permute-done.4.after1.nz2, bf16[2,608,128]{2,1,0:T(8,128)(2,1)S(1)} %collective-permute-done.5.after2.nz3, ...), custom_call_target="tpu_custom_call" | custom-call | flops 3000000000 | bytes 5000000 | tf_op jit(solution)/shard_map/weight/pallas_call | solution.py:562
  150.4 1.3 copy-done.1
  151.6 3.7 %all-to-all-start.2 = ((bf16[4,152,1536]{2,1,0:T(8,128)(2,1)}), bf16[4,152,1536]{2,1,0:T(8,128)(2,1)S(1)}, u32[]{:S(2)}, u32[]{:S(2)}) async-start(bf16[4,152,1536]{2,1,0:T(8,128)(2,1)} %copy-done.1), calls=%async_computation.2 | async-start | bytes 3735552 | tf_op jit(solution)/shard_map/all_to_all | solution.py:575
  156.0 1.6 collective-permute-done.7
  157.6 0.9 add_convert_fusion
  158.5 2.7 %collective-permute-start.8 = (bf16[1976,128]{1,0:T(8,128)(2,1)}, bf16[1976,128]{1,0:T(8,128)(2,1)}, u32[]{:S(2)}, u32[]{:S(2)}) collective-permute-start(bf16[1976,128]{1,0:T(8,128)(2,1)} %add_convert_fusion), channel_id=1, source_target_pairs={{0,2},{1,3},{2,0},{3,1},{4,6},{5,7},{6,4},{7,5},{8,10},{9,11},{10,... | collective-permute-start | bytes 1517576 | tf_op jit(solution)/shard_map/ppermute | solution.py:574
  161.2 18.0 %all-to-all-done.2.terms = bf16[4,152,1536]{2,1,0:T(8,128)(2,1)S(1)} async-done(((bf16[4,152,1536]{2,1,0:T(8,128)(2,1)}), bf16[4,152,1536]{2,1,0:T(8,128)(2,1)S(1)}, u32[]{:S(2)}, u32[]{:S(2)}) %all-to-all-start.2) | async-done | bytes 1867808 | tf_op jit(solution)/shard_map/all_to_all | solution.py:575
  179.7 0.8 copy-done.6
  180.5 0.9 copy-done.3
  181.4 0.9 copy-done.4
  182.3 1.0 copy-done.5
  183.4 1.0 copy-done.7
  184.4 2.2 %final.1 = (bf16[608,128]{1,0:T(8,128)(2,1)}, bf16[608,128]{1,0:T(8,128)(2,1)}, bf16[608,128]{1,0:T(8,128)(2,1)}, bf16[16,608]{1,0:T(8,128)(2,1)}, bf16[16,608]{1,0:T(8,128)(2,1)}) custom-call(bf16[608,128]{1,0:T(8,128)(2,1)S(1)} %bitcast.13, bf16[608,128]{1,0:T(8,128)(2,1)S(1)} %bitcast.15, bf16[16,608]{1,0:T(8,128)(2,1)S(1)} %copy-done.13, ...), custom_call_target="tpu_custom_call" | custom-call | tf_op jit(solution)/shard_map/final/pallas_call | solution.py:594
  186.6 0.8 weight_out.1
  (56 shorter events, 3.2 us)
Async XLA Ops:
  2.6 14.9 %collective-permute-start.1 = (bf16[1976,128]{1,0:T(8,128)(2,1)}, bf16[1976,128]{1,0:T(8,128)(2,1)S(1)}, u32[]{:S(2)}, u32[]{:S(2)}) collective-permute-start(bf16[1976,128]{1,0:T(8,128)(2,1)} %pack.1.in0), channel_id=1, source_target_pairs={{0,2},{1,3},{2,0},{3,1},{4,6},{5,7},{6,4},{7,5},{8,10},{9,11},{10,... | collective-permute-start | bytes 1517576 | tf_op jit(solution)/shard_map/ppermute | solution.py:478
  5.8 11.7 %collective-permute-start = (bf16[1976,128]{1,0:T(8,128)(2,1)}, bf16[1976,128]{1,0:T(8,128)(2,1)S(1)}, u32[]{:S(2)}, u32[]{:S(2)}) collective-permute-start(bf16[1976,128]{1,0:T(8,128)(2,1)} %pack.1.in0), channel_id=1, source_target_pairs={{0,1},{1,0},{2,3},{3,2},{4,5},{5,4},{6,7},{7,6},{8,9},{9,8},{10,11... | collective-permute-start | bytes 1517576 | tf_op jit(solution)/shard_map/ppermute | solution.py:479
  17.5 1.9 %copy-start.19 = (bf16[1976,128]{1,0:T(8,128)(2,1)}, bf16[1976,128]{1,0:T(8,128)(2,1)S(1)}, u32[]{:S(2)}) copy-start(bf16[1976,128]{1,0:T(8,128)(2,1)S(1)} %collective-permute-done.1.in2) | copy-start | bytes 1517572
  17.5 1.9 %collective-permute-start.2 = (bf16[1976,128]{1,0:T(8,128)(2,1)S(1)}, bf16[1976,128]{1,0:T(8,128)(2,1)S(1)}, u32[]{:S(2)}, u32[]{:S(2)}) collective-permute-start(bf16[1976,128]{1,0:T(8,128)(2,1)S(1)} %collective-permute-done.1.in2), channel_id=1, source_target_pairs={{0,1},{1,0},{2,3},{3,2},{4,5},{5,4},{6,7},{7,6},{8,9},{9,8},{10,11... | collective-permute-start | bytes 1517576 | tf_op jit(solution)/shard_map/ppermute | solution.py:480
  17.5 1.9 %copy-start.20 = (bf16[1976,128]{1,0:T(8,128)(2,1)}, bf16[1976,128]{1,0:T(8,128)(2,1)S(1)}, u32[]{:S(2)}) copy-start(bf16[1976,128]{1,0:T(8,128)(2,1)S(1)} %collective-permute-done.in1) | copy-start | bytes 1517572
  33.7 33.5 %copy-start.10 = (bf16[2,608,128]{2,1,0:T(8,128)(2,1)S(1)}, bf16[2,608,128]{2,1,0:T(8,128)(2,1)}, u32[]{:S(2)}) copy-start(bf16[2,608,128]{2,1,0:T(8,128)(2,1)} %get-tuple-element.37.refs_0_) | copy-start | bytes 933892
  33.7 33.5 %copy-start.11 = (bf16[2,608,128]{2,1,0:T(8,128)(2,1)S(1)}, bf16[2,608,128]{2,1,0:T(8,128)(2,1)}, u32[]{:S(2)}) copy-start(bf16[2,608,128]{2,1,0:T(8,128)(2,1)} %get-tuple-element.38.refs_1_) | copy-start | bytes 933892
  33.7 33.5 %copy-start.12 = (bf16[2,608,128]{2,1,0:T(8,128)(2,1)S(1)}, bf16[2,608,128]{2,1,0:T(8,128)(2,1)}, u32[]{:S(2)}) copy-start(bf16[2,608,128]{2,1,0:T(8,128)(2,1)} %get-tuple-element.39.refs_2_) | copy-start | bytes 933892
  33.7 33.5 %all-to-all-start = ((bf16[32,192,128]{2,1,0:T(8,128)(2,1)}), bf16[32,192,128]{2,1,0:T(8,128)(2,1)S(1)}, u32[]{:S(2)}, u32[]{:S(2)}) async-start(bf16[32,192,128]{2,1,0:T(8,128)(2,1)} %get-tuple-element.34), calls=%async_computation | async-start | bytes 3145728 | tf_op jit(solution)/shard_map/all_to_all | solution.py:503
  67.2 28.3 %collective-permute-start.3 = (bf16[2,608,128]{2,1,0:T(8,128)(2,1)S(1)}, bf16[2,608,128]{2,1,0:T(8,128)(2,1)S(1)}, u32[]{:S(2)}, u32[]{:S(2)}) collective-permute-start(bf16[2,608,128]{2,1,0:T(8,128)(2,1)S(1)} %get-tuple-element.40), channel_id=1, source_target_pairs={{0,32},{32,64},{64,96},{96,0},{1,33},{33,65},{65,97},{97,1},{2,34}... | collective-permute-start | bytes 933896 | tf_op jit(solution)/shard_map/ppermute | solution.py:448
  67.3 28.2 %collective-permute-start.4 = (bf16[2,608,128]{2,1,0:T(8,128)(2,1)S(1)}, bf16[2,608,128]{2,1,0:T(8,128)(2,1)S(1)}, u32[]{:S(2)}, u32[]{:S(2)}) collective-permute-start(bf16[2,608,128]{2,1,0:T(8,128)(2,1)S(1)} %get-tuple-element.41), channel_id=1, source_target_pairs={{0,64},{32,96},{64,0},{96,32},{1,65},{33,97},{65,1},{97,33},{2,66}... | collective-permute-start | bytes 933896 | tf_op jit(solution)/shard_map/ppermute | solution.py:448
  69.6 26.0 %collective-permute-start.5 = (bf16[2,608,128]{2,1,0:T(8,128)(2,1)S(1)}, bf16[2,608,128]{2,1,0:T(8,128)(2,1)S(1)}, u32[]{:S(2)}, u32[]{:S(2)}) collective-permute-start(bf16[2,608,128]{2,1,0:T(8,128)(2,1)S(1)} %get-tuple-element.42), channel_id=1, source_target_pairs={{0,96},{32,0},{64,32},{96,64},{1,97},{33,1},{65,33},{97,65},{2,98}... | collective-permute-start | bytes 933896 | tf_op jit(solution)/shard_map/ppermute | solution.py:448
  96.2 29.7 %copy-start.2 = (f32[272,768]{1,0:T(8,128)S(1)}, f32[272,768]{1,0:T(8,128)}, u32[]{:S(2)}) copy-start(f32[272,768]{1,0:T(8,128)} %get-tuple-element.43.proj) | copy-start | bytes 2506756
  96.2 29.7 %copy-start.15 = (f32[3,2,64]{2,1,0:T(2,128)S(1)}, f32[3,2,64]{2,1,0:T(2,128)}, u32[]{:S(2)}) copy-start(f32[3,2,64]{2,1,0:T(2,128)} %gains.5) | copy-start | bytes 4612
  125.9 4.8 %copy-start = (bf16[32,192,128]{2,1,0:T(8,128)(2,1)}, bf16[32,192,128]{2,1,0:T(8,128)(2,1)S(1)}, u32[]{:S(2)}) copy-start(bf16[32,192,128]{2,1,0:T(8,128)(2,1)S(1)} %all_to_all.15.recv) | copy-start | bytes 4718596
  128.4 2.3 %copy-start.8 = (bf16[128,1536]{1,0:T(8,128)(2,1)}, bf16[128,1536]{1,0:T(8,128)(2,1)S(1)}, u32[]{:S(2)}) copy-start(bf16[128,1536]{1,0:T(8,128)(2,1)S(1)} %head_back_ctl.1.ctl_rows.b0) | copy-start | bytes 1179652
  128.5 16.7 %collective-permute-start.11 = (bf16[128,1536]{1,0:T(8,128)(2,1)S(1)}, bf16[128,1536]{1,0:T(8,128)(2,1)S(1)}, u32[]{:S(2)}, u32[]{:S(2)}) collective-permute-start(bf16[128,1536]{1,0:T(8,128)(2,1)S(1)} %head_back_ctl.1.ctl_rows.b0), channel_id=1, source_target_pairs={{0,96},{32,0},{64,32},{96,64},{1,97},{33,1},{65,33},{97,65},{2,98}... | collective-permute-start | bytes 1179656 | tf_op jit(solution)/shard_map/ppermute | solution.py:448
  129.3 15.9 %collective-permute-start.10 = (bf16[128,1536]{1,0:T(8,128)(2,1)S(1)}, bf16[128,1536]{1,0:T(8,128)(2,1)S(1)}, u32[]{:S(2)}, u32[]{:S(2)}) collective-permute-start(bf16[128,1536]{1,0:T(8,128)(2,1)S(1)} %head_back_ctl.1.ctl_rows.b0), channel_id=1, source_target_pairs={{0,64},{32,96},{64,0},{96,32},{1,65},{33,97},{65,1},{97,33},{2,66}... | collective-permute-start | bytes 1179656 | tf_op jit(solution)/shard_map/ppermute | solution.py:448
  129.9 16.9 %collective-permute-start.9 = (bf16[128,1536]{1,0:T(8,128)(2,1)S(1)}, bf16[128,1536]{1,0:T(8,128)(2,1)S(1)}, u32[]{:S(2)}, u32[]{:S(2)}) collective-permute-start(bf16[128,1536]{1,0:T(8,128)(2,1)S(1)} %head_back_ctl.1.ctl_rows.b0), channel_id=1, source_target_pairs={{0,32},{32,64},{64,96},{96,0},{1,33},{33,65},{65,97},{97,1},{2,34}... | collective-permute-start | bytes 1179656 | tf_op jit(solution)/shard_map/ppermute | solution.py:448
  130.7 16.0 %copy-start.16 = (bf16[2,608,128]{2,1,0:T(8,128)(2,1)S(1)}, bf16[2,608,128]{2,1,0:T(8,128)(2,1)}, u32[]{:S(2)}) copy-start(bf16[2,608,128]{2,1,0:T(8,128)(2,1)} %get-tuple-element.55.nz0) | copy-start | bytes 933892
  146.8 1.0 copy-start.9
  150.4 1.3 copy-start.1
  151.6 5.9 %copy-start.18 = (bf16[1976,128]{1,0:T(8,128)(2,1)S(1)}, bf16[1976,128]{1,0:T(8,128)(2,1)}, u32[]{:S(2)}) copy-start(bf16[1976,128]{1,0:T(8,128)(2,1)} %get-tuple-element.48) | copy-start | bytes 1517572
  151.6 27.6 %all-to-all-start.2 = ((bf16[4,152,1536]{2,1,0:T(8,128)(2,1)}), bf16[4,152,1536]{2,1,0:T(8,128)(2,1)S(1)}, u32[]{:S(2)}, u32[]{:S(2)}) async-start(bf16[4,152,1536]{2,1,0:T(8,128)(2,1)} %copy-done.1), calls=%async_computation.2 | async-start | bytes 3735552 | tf_op jit(solution)/shard_map/all_to_all | solution.py:575
  155.4 25.1 %copy-start.13 = (bf16[16,608]{1,0:T(8,128)(2,1)S(1)}, bf16[16,608]{1,0:T(8,128)(2,1)}, u32[]{:S(2)}) copy-start(bf16[16,608]{1,0:T(8,128)(2,1)} %txt.3) | copy-start | bytes 58372
  155.4 25.1 %copy-start.14 = (bf16[16,608]{1,0:T(8,128)(2,1)S(1)}, bf16[16,608]{1,0:T(8,128)(2,1)}, u32[]{:S(2)}) copy-start(bf16[16,608]{1,0:T(8,128)(2,1)} %dy_txt.3) | copy-start | bytes 58372
  155.4 2.2 %collective-permute-start.7 = (bf16[1976,128]{1,0:T(8,128)(2,1)}, bf16[1976,128]{1,0:T(8,128)(2,1)S(1)}, u32[]{:S(2)}, u32[]{:S(2)}) collective-permute-start(bf16[1976,128]{1,0:T(8,128)(2,1)} %get-tuple-element.49), channel_id=1, source_target_pairs={{0,1},{1,0},{2,3},{3,2},{4,5},{5,4},{6,7},{7,6},{8,9},{9,8},{10,11... | collective-permute-start | bytes 1517576 | tf_op jit(solution)/shard_map/ppermute | solution.py:571
  155.5 24.2 %collective-permute-start.6 = (bf16[1976,128]{1,0:T(8,128)(2,1)}, bf16[1976,128]{1,0:T(8,128)(2,1)S(1)}, u32[]{:S(2)}, u32[]{:S(2)}) collective-permute-start(bf16[1976,128]{1,0:T(8,128)(2,1)} %get-tuple-element.47), channel_id=1, source_target_pairs={{0,1},{1,0},{2,3},{3,2},{4,5},{5,4},{6,7},{7,6},{8,9},{9,8},{10,11... | collective-permute-start | bytes 1517576 | tf_op jit(solution)/shard_map/ppermute | solution.py:572
  158.5 22.0 %collective-permute-start.8 = (bf16[1976,128]{1,0:T(8,128)(2,1)}, bf16[1976,128]{1,0:T(8,128)(2,1)}, u32[]{:S(2)}, u32[]{:S(2)}) collective-permute-start(bf16[1976,128]{1,0:T(8,128)(2,1)} %add_convert_fusion), channel_id=1, source_target_pairs={{0,2},{1,3},{2,0},{3,1},{4,6},{5,7},{6,4},{7,5},{8,10},{9,11},{10,... | collective-permute-start | bytes 1517576 | tf_op jit(solution)/shard_map/ppermute | solution.py:574
  179.6 7.0 %collective-permute-start.12 = (bf16[76,1536]{1,0:T(8,128)(2,1)S(1)}, bf16[76,1536]{1,0:T(8,128)(2,1)S(1)}, u32[]{:S(2)}, u32[]{:S(2)}) collective-permute-start(bf16[76,1536]{1,0:T(8,128)(2,1)S(1)} %get-tuple-element.58), channel_id=1, source_target_pairs={{0,4},{4,0},{1,5},{5,1},{2,6},{6,2},{3,7},{7,3},{8,12},{12,8},{9,1... | collective-permute-start | bytes 700424 | tf_op jit(solution)/shard_map/ppermute | solution.py:584
  182.3 1.0 copy-start.5
  183.4 1.0 copy-start.7
  (5 other events, 4.1 us)

commit v7 on v6

--- a/solution.py
+++ b/solution.py
@@ -12,7 +12,8 @@
 D = 2432
 SHARE = 608
 PIECE = 152
-ROWS = 3 * SHARE + PIECE
+TEXT_ROWS = 160
+ROWS = 3 * SHARE + TEXT_ROWS
 IMG = 128
 TXT = 16
 BLOCKS = 32
@@ -56,12 +57,14 @@
 
 
 def spread_text(packed):
+    packed = packed[0:PIECE]
     return jnp.concatenate([packed] + [pltpu.roll(packed, 128 - 32 * a, 1) for a in (1, 2, 3)], 0)
 
 
 def pack_text(columns):
     pieces = [columns[PIECE * a : PIECE * (a + 1)] for a in range(4)]
-    return pieces[0] + sum(pltpu.roll(pieces[a], 32 * a, 1) for a in (1, 2, 3))
+    packed = pieces[0] + sum(pltpu.roll(pieces[a], 32 * a, 1) for a in (1, 2, 3))
+    return jnp.concatenate([packed, jnp.zeros((TEXT_ROWS - PIECE, IMG), F32)], 0)
 
 
 def weight_copies(sources, wq, wo, sems):
@@ -394,7 +397,7 @@
     text = jnp.concatenate([y, u, jnp.zeros((IMG - 2 * TXT, D), F32)], 0).astype(BF16).T.astype(F32)
     for c in range(4):
         slabs[c, 3 * SHARE :, :] = pack_text(text[SHARE * c : SHARE * (c + 1)]).astype(BF16)
-    leave(3 * SHARE, PIECE)
+    leave(3 * SHARE, TEXT_ROWS)
     results.finish()
 
 

time: 188 us -> 189 us (level)
  no operation moved by 1% of the time
where the time goes in v7:
time: 189 us; the launch traced here: 187 us
  Pallas kernels  63.1 us (33%)
  waiting for transfers between devices  58 us (31%)
  blocking collectives  29.7 us (16%)
  starting transfers between devices  25.7 us (14%)
  local copies, waits for them, and re-layouts  8.49 us (4%)
    all_to_all x1, blocking collectives, per_device(): back = lax.all_to_all(back, seq, 0, 0, tiled=True)  29.7 us
    pallas_call x1, Pallas kernels, per_device(): pl.pallas_call(attention_kernel, out_shape=[shape((keys, 128), BF16), sha...  24.8 us
    all_to_all x1, waiting for transfers between devices, per_device(): recv = lax.all_to_all(send, seq, 0, 0, tiled=True)  23.1 us
    all_to_all x1, waiting for transfers between devices, per_device(): terms = lax.all_to_all(terms, 'y', 0, 0, tiled=True)  18 us
    pallas_call x1, Pallas kernels, per_device(): pl.pallas_call(post_kernel, out_shape=[rows] * 4 + [shape((8, 128), F32)]...  14.4 us
    pallas_call x1, Pallas kernels, per_device(): pl.pallas_call(pre_kernel, out_shape=[shape((BLOCKS, CHUNK, 128), BF16),...  13.5 us
    ppermute x1, waiting for transfers between devices, per_device(): from_chip = lax.ppermute(own, 'tp', other_chip)  11.8 us
    all_to_all x1, starting transfers between devices, per_device(): recv = lax.all_to_all(send, seq, 0, 0, tiled=True)  9.63 us
  transfers between devices with their start and end apart: 15, of which 6 were waited for; matrix products, arithmetic and copies ran while one was open for 1% of the time, Pallas kernels for 22%

profile of v7, /device:TPU:0, one launch (start us, length us, event | category | flops | bytes accessed | tf_op | source)
XLA Modules:
  0.0 187.4 jit_solution(16715771037598218616)
XLA Ops:
  0.6 1.9 %pack.1.in0 = bf16[1984,128]{1,0:T(8,128)(2,1)} custom-call(bf16[608,128]{1,0:T(8,128)(2,1)} %bitcast.12, bf16[608,128]{1,0:T(8,128)(2,1)} %bitcast.22, bf16[608,128]{1,0:T(8,128)(2,1)} %bitcast.14, bf16[16,608]{1,0:T(8,128)(2,1)} %txt.3, bf16[16,608]{1,0:T(8,128)(2,1)} %dy_txt.3), custom_call_target="tpu_custom_call" | custom-call | tf_op jit(solution)/shard_map/pack/pallas_call | solution.py:472
  2.6 3.2 %collective-permute-start.1 = (bf16[1984,128]{1,0:T(8,128)(2,1)}, bf16[1984,128]{1,0:T(8,128)(2,1)S(1)}, u32[]{:S(2)}, u32[]{:S(2)}) collective-permute-start(bf16[1984,128]{1,0:T(8,128)(2,1)} %pack.1.in0), channel_id=1, source_target_pairs={{0,2},{1,3},{2,0},{3,1},{4,6},{5,7},{6,4},{7,5},{8,10},{9,11},{10,... | collective-permute-start | bytes 1523720 | tf_op jit(solution)/shard_map/ppermute | solution.py:481
  5.8 11.8 %collective-permute-done.1.in2 = bf16[1984,128]{1,0:T(8,128)(2,1)S(1)} collective-permute-done((bf16[1984,128]{1,0:T(8,128)(2,1)}, bf16[1984,128]{1,0:T(8,128)(2,1)S(1)}, u32[]{:S(2)}, u32[]{:S(2)}) %collective-permute-start.1) | collective-permute-done | bytes 507936 | tf_op jit(solution)/shard_map/ppermute | solution.py:481
  17.6 1.9 collective-permute-done.2.in3
  19.4 0.8 copy-done.21
  20.2 13.5 %pre.1 = (bf16[32,192,128]{2,1,0:T(8,128)(2,1)}, f32[272,768]{1,0:T(8,128)}, bf16[272,2432]{1,0:T(8,128)(2,1)}, f32[272,128]{1,0:T(8,128)}, bf16[2,608,128]{2,1,...) custom-call(bf16[1984,128]{1,0:T(8,128)(2,1)} %pack.1.in0, ...), custom_call_target="tpu_custom_call" | custom-call | tf_op jit(solution)/shard_map/pre/pallas_call | solution.py:485
  33.8 9.6 %all-to-all-start = ((bf16[32,192,128]{2,1,0:T(8,128)(2,1)}), bf16[32,192,128]{2,1,0:T(8,128)(2,1)S(1)}, u32[]{:S(2)}, u32[]{:S(2)}) async-start(bf16[32,192,128]{2,1,0:T(8,128)(2,1)} %get-tuple-element.34), calls=%async_computation | async-start | bytes 3145728 | tf_op jit(solution)/shard_map/all_to_all | solution.py:506
  44.1 23.1 %all-to-all-done.recv.after = bf16[32,192,128]{2,1,0:T(8,128)(2,1)S(1)} async-done(((bf16[32,192,128]{2,1,0:T(8,128)(2,1)}), bf16[32,192,128]{2,1,0:T(8,128)(2,1)S(1)}, u32[]{:S(2)}, u32[]{:S(2)}) %all-to-all-start) | async-done | bytes 1572896 | tf_op jit(solution)/shard_map/all_to_all | solution.py:506
  67.4 2.3 %collective-permute-start.4 = (bf16[2,608,128]{2,1,0:T(8,128)(2,1)S(1)}, bf16[2,608,128]{2,1,0:T(8,128)(2,1)S(1)}, u32[]{:S(2)}, u32[]{:S(2)}) collective-permute-start(bf16[2,608,128]{2,1,0:T(8,128)(2,1)S(1)} %get-tuple-element.41), channel_id=1, source_target_pairs={{0,64},{32,96},{64,0},{96,32},{1,65},{33,97},{65,1},{97,33},{2,66}... | collective-permute-start | bytes 933896 | tf_op jit(solution)/shard_map/ppermute | solution.py:451
  69.6 1.2 collective-permute-start.5
  70.8 24.8 %attention.1 = (bf16[4608,128]{1,0:T(8,128)(2,1)S(1)}, bf16[2048,128]{1,0:T(8,128)(2,1)S(1)}) custom-call(s32[2]{0:T(128)S(1)} %pad_add_fusion.role, bf16[32,192,128]{2,1,0:T(8,128)(2,1)S(1)} %all-to-all-done.recv.after), custom_call_target="tpu_custom_call" | custom-call | flops 40000000000 | bytes 3200000 | tf_op jit(solution)/shard_map/attention/pallas_call | solution.py:509
  96.3 29.7 %all_to_all.15.recv = bf16[32,192,128]{2,1,0:T(8,128)(2,1)S(1)} all-to-all(bf16[32,192,128]{2,1,0:T(8,128)(2,1)S(1)} %scatter.1), channel_id=1, replica_groups=mesh['z'=4,'y'=4,'w'=2,'tp'=4] {'z','y','w'}, dimensions={0} | all-to-all | bytes 3145728 | tf_op jit(solution)/shard_map/all_to_all | solution.py:534
  126.0 2.5 %head_back_ctl.1.ctl_rows.b0 = bf16[128,1536]{1,0:T(8,128)(2,1)S(1)} custom-call(bf16[32,192,128]{2,1,0:T(8,128)(2,1)S(1)} %all_to_all.15.recv, f32[272,768]{1,0:T(8,128)S(1)} %copy-done.2, f32[3,2,64]{2,1,0:T(2,128)S(1)} %copy-done.15), custom_call_target="tpu_custom_call" | custom-call | tf_op jit(solution)/shard_map/head_back_ctl/pallas_call | solution.py:536
  128.5 0.9 collective-permute-start.11
  129.9 0.9 collective-permute-start.9
  130.8 14.4 %post.1 = (bf16[1984,128]{1,0:T(8,128)(2,1)}, bf16[1984,128]{1,0:T(8,128)(2,1)}, bf16[1984,128]{1,0:T(8,128)(2,1)}, bf16[1984,128]{1,0:T(8,128)(2,1)}, f32[8,128]{1,0:T(8,128)}) custom-call(bf16[32,192,128]{2,1,0:T(8,128)(2,1)} %copy-done, f32[272,768]{1,0:T(8,128)} %get-tuple-element.43.proj, f32[3,2,64]{2,1,0:T(2,128)} %gains.5, ...), custom_call_target="tpu_custom_call" | custom-call | flops 14000000000 | bytes 30000000 | tf_op jit(solution)/shard_map/post/pallas_call | solution.py:545
  145.3 1.6 collective-permute-done.9.b1
  146.8 1.0 copy-done.9
  148.5 1.9 %weight.1 = bf16[4,152,1536]{2,1,0:T(8,128)(2,1)S(1)} custom-call(bf16[2,608,128]{2,1,0:T(8,128)(2,1)S(1)} %copy-done.16, bf16[2,608,128]{2,1,0:T(8,128)(2,1)S(1)} %collective-permute-done.3.after0.nz1, bf16[2,608,128]{2,1,0:T(8,128)(2,1)S(1)} %collective-permute-done.4.after1.nz2, bf16[2,608,128]{2,1,0:T(8,128)(2,1)S(1)} %collective-permute-done.5.after2.nz3, ...), custom_call_target="tpu_custom_call" | custom-call | flops 3000000000 | bytes 5000000 | tf_op jit(solution)/shard_map/weight/pallas_call | solution.py:565
  150.4 1.3 copy-done.1
  151.7 3.7 %all-to-all-start.2 = ((bf16[4,152,1536]{2,1,0:T(8,128)(2,1)}), bf16[4,152,1536]{2,1,0:T(8,128)(2,1)S(1)}, u32[]{:S(2)}, u32[]{:S(2)}) async-start(bf16[4,152,1536]{2,1,0:T(8,128)(2,1)} %copy-done.1), calls=%async_computation.2 | async-start | bytes 3735552 | tf_op jit(solution)/shard_map/all_to_all | solution.py:578
  156.0 1.6 collective-permute-done.7
  157.6 0.9 add_convert_fusion
  158.5 2.7 %collective-permute-start.8 = (bf16[1984,128]{1,0:T(8,128)(2,1)}, bf16[1984,128]{1,0:T(8,128)(2,1)}, u32[]{:S(2)}, u32[]{:S(2)}) collective-permute-start(bf16[1984,128]{1,0:T(8,128)(2,1)} %add_convert_fusion), channel_id=1, source_target_pairs={{0,2},{1,3},{2,0},{3,1},{4,6},{5,7},{6,4},{7,5},{8,10},{9,11},{10,... | collective-permute-start | bytes 1523720 | tf_op jit(solution)/shard_map/ppermute | solution.py:577
  161.2 18.0 %all-to-all-done.2.terms = bf16[4,152,1536]{2,1,0:T(8,128)(2,1)S(1)} async-done(((bf16[4,152,1536]{2,1,0:T(8,128)(2,1)}), bf16[4,152,1536]{2,1,0:T(8,128)(2,1)S(1)}, u32[]{:S(2)}, u32[]{:S(2)}) %all-to-all-start.2) | async-done | bytes 1867808 | tf_op jit(solution)/shard_map/all_to_all | solution.py:578
  179.7 0.8 copy-done.6
  180.6 0.9 copy-done.3
  181.5 0.9 copy-done.4
  182.4 1.0 copy-done.5
  183.4 1.0 copy-done.7
  184.5 2.2 %final.1 = (bf16[608,128]{1,0:T(8,128)(2,1)}, bf16[608,128]{1,0:T(8,128)(2,1)}, bf16[608,128]{1,0:T(8,128)(2,1)}, bf16[16,608]{1,0:T(8,128)(2,1)}, bf16[16,608]{1,0:T(8,128)(2,1)}) custom-call(bf16[608,128]{1,0:T(8,128)(2,1)S(1)} %bitcast.13, bf16[608,128]{1,0:T(8,128)(2,1)S(1)} %bitcast.15, bf16[16,608]{1,0:T(8,128)(2,1)S(1)} %copy-done.13, ...), custom_call_target="tpu_custom_call" | custom-call | tf_op jit(solution)/shard_map/final/pallas_call | solution.py:597
  186.6 0.8 weight_out.1
  (56 shorter events, 3.2 us)
Async XLA Ops:
  2.6 15.0 %collective-permute-start.1 = (bf16[1984,128]{1,0:T(8,128)(2,1)}, bf16[1984,128]{1,0:T(8,128)(2,1)S(1)}, u32[]{:S(2)}, u32[]{:S(2)}) collective-permute-start(bf16[1984,128]{1,0:T(8,128)(2,1)} %pack.1.in0), channel_id=1, source_target_pairs={{0,2},{1,3},{2,0},{3,1},{4,6},{5,7},{6,4},{7,5},{8,10},{9,11},{10,... | collective-permute-start | bytes 1523720 | tf_op jit(solution)/shard_map/ppermute | solution.py:481
  5.8 11.8 %collective-permute-start = (bf16[1984,128]{1,0:T(8,128)(2,1)}, bf16[1984,128]{1,0:T(8,128)(2,1)S(1)}, u32[]{:S(2)}, u32[]{:S(2)}) collective-permute-start(bf16[1984,128]{1,0:T(8,128)(2,1)} %pack.1.in0), channel_id=1, source_target_pairs={{0,1},{1,0},{2,3},{3,2},{4,5},{5,4},{6,7},{7,6},{8,9},{9,8},{10,11... | collective-permute-start | bytes 1523720 | tf_op jit(solution)/shard_map/ppermute | solution.py:482
  17.5 1.9 %copy-start.19 = (bf16[1984,128]{1,0:T(8,128)(2,1)}, bf16[1984,128]{1,0:T(8,128)(2,1)S(1)}, u32[]{:S(2)}) copy-start(bf16[1984,128]{1,0:T(8,128)(2,1)S(1)} %collective-permute-done.1.in2) | copy-start | bytes 1523716
  17.5 1.9 %collective-permute-start.2 = (bf16[1984,128]{1,0:T(8,128)(2,1)S(1)}, bf16[1984,128]{1,0:T(8,128)(2,1)S(1)}, u32[]{:S(2)}, u32[]{:S(2)}) collective-permute-start(bf16[1984,128]{1,0:T(8,128)(2,1)S(1)} %collective-permute-done.1.in2), channel_id=1, source_target_pairs={{0,1},{1,0},{2,3},{3,2},{4,5},{5,4},{6,7},{7,6},{8,9},{9,8},{10,11... | collective-permute-start | bytes 1523720 | tf_op jit(solution)/shard_map/ppermute | solution.py:483
  17.6 1.9 %copy-start.20 = (bf16[1984,128]{1,0:T(8,128)(2,1)}, bf16[1984,128]{1,0:T(8,128)(2,1)S(1)}, u32[]{:S(2)}) copy-start(bf16[1984,128]{1,0:T(8,128)(2,1)S(1)} %collective-permute-done.in1) | copy-start | bytes 1523716
  33.7 33.5 %copy-start.10 = (bf16[2,608,128]{2,1,0:T(8,128)(2,1)S(1)}, bf16[2,608,128]{2,1,0:T(8,128)(2,1)}, u32[]{:S(2)}) copy-start(bf16[2,608,128]{2,1,0:T(8,128)(2,1)} %get-tuple-element.37.refs_0_) | copy-start | bytes 933892
  33.7 33.5 %copy-start.11 = (bf16[2,608,128]{2,1,0:T(8,128)(2,1)S(1)}, bf16[2,608,128]{2,1,0:T(8,128)(2,1)}, u32[]{:S(2)}) copy-start(bf16[2,608,128]{2,1,0:T(8,128)(2,1)} %get-tuple-element.38.refs_1_) | copy-start | bytes 933892
  33.7 33.5 %copy-start.12 = (bf16[2,608,128]{2,1,0:T(8,128)(2,1)S(1)}, bf16[2,608,128]{2,1,0:T(8,128)(2,1)}, u32[]{:S(2)}) copy-start(bf16[2,608,128]{2,1,0:T(8,128)(2,1)} %get-tuple-element.39.refs_2_) | copy-start | bytes 933892
  33.8 33.5 %all-to-all-start = ((bf16[32,192,128]{2,1,0:T(8,128)(2,1)}), bf16[32,192,128]{2,1,0:T(8,128)(2,1)S(1)}, u32[]{:S(2)}, u32[]{:S(2)}) async-start(bf16[32,192,128]{2,1,0:T(8,128)(2,1)} %get-tuple-element.34), calls=%async_computation | async-start | bytes 3145728 | tf_op jit(solution)/shard_map/all_to_all | solution.py:506
  67.3 28.3 %collective-permute-start.3 = (bf16[2,608,128]{2,1,0:T(8,128)(2,1)S(1)}, bf16[2,608,128]{2,1,0:T(8,128)(2,1)S(1)}, u32[]{:S(2)}, u32[]{:S(2)}) collective-permute-start(bf16[2,608,128]{2,1,0:T(8,128)(2,1)S(1)} %get-tuple-element.40), channel_id=1, source_target_pairs={{0,32},{32,64},{64,96},{96,0},{1,33},{33,65},{65,97},{97,1},{2,34}... | collective-permute-start | bytes 933896 | tf_op jit(solution)/shard_map/ppermute | solution.py:451
  67.4 28.2 %collective-permute-start.4 = (bf16[2,608,128]{2,1,0:T(8,128)(2,1)S(1)}, bf16[2,608,128]{2,1,0:T(8,128)(2,1)S(1)}, u32[]{:S(2)}, u32[]{:S(2)}) collective-permute-start(bf16[2,608,128]{2,1,0:T(8,128)(2,1)S(1)} %get-tuple-element.41), channel_id=1, source_target_pairs={{0,64},{32,96},{64,0},{96,32},{1,65},{33,97},{65,1},{97,33},{2,66}... | collective-permute-start | bytes 933896 | tf_op jit(solution)/shard_map/ppermute | solution.py:451
  69.6 26.0 %collective-permute-start.5 = (bf16[2,608,128]{2,1,0:T(8,128)(2,1)S(1)}, bf16[2,608,128]{2,1,0:T(8,128)(2,1)S(1)}, u32[]{:S(2)}, u32[]{:S(2)}) collective-permute-start(bf16[2,608,128]{2,1,0:T(8,128)(2,1)S(1)} %get-tuple-element.42), channel_id=1, source_target_pairs={{0,96},{32,0},{64,32},{96,64},{1,97},{33,1},{65,33},{97,65},{2,98}... | collective-permute-start | bytes 933896 | tf_op jit(solution)/shard_map/ppermute | solution.py:451
  96.2 29.7 %copy-start.2 = (f32[272,768]{1,0:T(8,128)S(1)}, f32[272,768]{1,0:T(8,128)}, u32[]{:S(2)}) copy-start(f32[272,768]{1,0:T(8,128)} %get-tuple-element.43.proj) | copy-start | bytes 2506756
  96.3 29.7 %copy-start.15 = (f32[3,2,64]{2,1,0:T(2,128)S(1)}, f32[3,2,64]{2,1,0:T(2,128)}, u32[]{:S(2)}) copy-start(f32[3,2,64]{2,1,0:T(2,128)} %gains.5) | copy-start | bytes 4612
  126.0 4.8 %copy-start = (bf16[32,192,128]{2,1,0:T(8,128)(2,1)}, bf16[32,192,128]{2,1,0:T(8,128)(2,1)S(1)}, u32[]{:S(2)}) copy-start(bf16[32,192,128]{2,1,0:T(8,128)(2,1)S(1)} %all_to_all.15.recv) | copy-start | bytes 4718596
  128.5 2.3 %copy-start.8 = (bf16[128,1536]{1,0:T(8,128)(2,1)}, bf16[128,1536]{1,0:T(8,128)(2,1)S(1)}, u32[]{:S(2)}) copy-start(bf16[128,1536]{1,0:T(8,128)(2,1)S(1)} %head_back_ctl.1.ctl_rows.b0) | copy-start | bytes 1179652
  128.5 16.7 %collective-permute-start.11 = (bf16[128,1536]{1,0:T(8,128)(2,1)S(1)}, bf16[128,1536]{1,0:T(8,128)(2,1)S(1)}, u32[]{:S(2)}, u32[]{:S(2)}) collective-permute-start(bf16[128,1536]{1,0:T(8,128)(2,1)S(1)} %head_back_ctl.1.ctl_rows.b0), channel_id=1, source_target_pairs={{0,96},{32,0},{64,32},{96,64},{1,97},{33,1},{65,33},{97,65},{2,98}... | collective-permute-start | bytes 1179656 | tf_op jit(solution)/shard_map/ppermute | solution.py:451
  129.4 15.9 %collective-permute-start.10 = (bf16[128,1536]{1,0:T(8,128)(2,1)S(1)}, bf16[128,1536]{1,0:T(8,128)(2,1)S(1)}, u32[]{:S(2)}, u32[]{:S(2)}) collective-permute-start(bf16[128,1536]{1,0:T(8,128)(2,1)S(1)} %head_back_ctl.1.ctl_rows.b0), channel_id=1, source_target_pairs={{0,64},{32,96},{64,0},{96,32},{1,65},{33,97},{65,1},{97,33},{2,66}... | collective-permute-start | bytes 1179656 | tf_op jit(solution)/shard_map/ppermute | solution.py:451
  129.9 16.9 %collective-permute-start.9 = (bf16[128,1536]{1,0:T(8,128)(2,1)S(1)}, bf16[128,1536]{1,0:T(8,128)(2,1)S(1)}, u32[]{:S(2)}, u32[]{:S(2)}) collective-permute-start(bf16[128,1536]{1,0:T(8,128)(2,1)S(1)} %head_back_ctl.1.ctl_rows.b0), channel_id=1, source_target_pairs={{0,32},{32,64},{64,96},{96,0},{1,33},{33,65},{65,97},{97,1},{2,34}... | collective-permute-start | bytes 1179656 | tf_op jit(solution)/shard_map/ppermute | solution.py:451
  130.8 16.0 %copy-start.16 = (bf16[2,608,128]{2,1,0:T(8,128)(2,1)S(1)}, bf16[2,608,128]{2,1,0:T(8,128)(2,1)}, u32[]{:S(2)}) copy-start(bf16[2,608,128]{2,1,0:T(8,128)(2,1)} %get-tuple-element.55.nz0) | copy-start | bytes 933892
  146.8 1.0 copy-start.9
  150.4 1.3 copy-start.1
  151.7 5.9 %copy-start.18 = (bf16[1984,128]{1,0:T(8,128)(2,1)S(1)}, bf16[1984,128]{1,0:T(8,128)(2,1)}, u32[]{:S(2)}) copy-start(bf16[1984,128]{1,0:T(8,128)(2,1)} %get-tuple-element.48) | copy-start | bytes 1523716
  151.7 27.6 %all-to-all-start.2 = ((bf16[4,152,1536]{2,1,0:T(8,128)(2,1)}), bf16[4,152,1536]{2,1,0:T(8,128)(2,1)S(1)}, u32[]{:S(2)}, u32[]{:S(2)}) async-start(bf16[4,152,1536]{2,1,0:T(8,128)(2,1)} %copy-done.1), calls=%async_computation.2 | async-start | bytes 3735552 | tf_op jit(solution)/shard_map/all_to_all | solution.py:578
  155.4 25.1 %copy-start.13 = (bf16[16,608]{1,0:T(8,128)(2,1)S(1)}, bf16[16,608]{1,0:T(8,128)(2,1)}, u32[]{:S(2)}) copy-start(bf16[16,608]{1,0:T(8,128)(2,1)} %txt.3) | copy-start | bytes 58372
  155.4 25.1 %copy-start.14 = (bf16[16,608]{1,0:T(8,128)(2,1)S(1)}, bf16[16,608]{1,0:T(8,128)(2,1)}, u32[]{:S(2)}) copy-start(bf16[16,608]{1,0:T(8,128)(2,1)} %dy_txt.3) | copy-start | bytes 58372
  155.4 2.2 %collective-permute-start.7 = (bf16[1984,128]{1,0:T(8,128)(2,1)}, bf16[1984,128]{1,0:T(8,128)(2,1)S(1)}, u32[]{:S(2)}, u32[]{:S(2)}) collective-permute-start(bf16[1984,128]{1,0:T(8,128)(2,1)} %get-tuple-element.49), channel_id=1, source_target_pairs={{0,1},{1,0},{2,3},{3,2},{4,5},{5,4},{6,7},{7,6},{8,9},{9,8},{10,11... | collective-permute-start | bytes 1523720 | tf_op jit(solution)/shard_map/ppermute | solution.py:574
  155.5 24.2 %collective-permute-start.6 = (bf16[1984,128]{1,0:T(8,128)(2,1)}, bf16[1984,128]{1,0:T(8,128)(2,1)S(1)}, u32[]{:S(2)}, u32[]{:S(2)}) collective-permute-start(bf16[1984,128]{1,0:T(8,128)(2,1)} %get-tuple-element.47), channel_id=1, source_target_pairs={{0,1},{1,0},{2,3},{3,2},{4,5},{5,4},{6,7},{7,6},{8,9},{9,8},{10,11... | collective-permute-start | bytes 1523720 | tf_op jit(solution)/shard_map/ppermute | solution.py:575
  158.5 22.0 %collective-permute-start.8 = (bf16[1984,128]{1,0:T(8,128)(2,1)}, bf16[1984,128]{1,0:T(8,128)(2,1)}, u32[]{:S(2)}, u32[]{:S(2)}) collective-permute-start(bf16[1984,128]{1,0:T(8,128)(2,1)} %add_convert_fusion), channel_id=1, source_target_pairs={{0,2},{1,3},{2,0},{3,1},{4,6},{5,7},{6,4},{7,5},{8,10},{9,11},{10,... | collective-permute-start | bytes 1523720 | tf_op jit(solution)/shard_map/ppermute | solution.py:577
  179.6 7.0 %collective-permute-start.12 = (bf16[76,1536]{1,0:T(8,128)(2,1)S(1)}, bf16[76,1536]{1,0:T(8,128)(2,1)S(1)}, u32[]{:S(2)}, u32[]{:S(2)}) collective-permute-start(bf16[76,1536]{1,0:T(8,128)(2,1)S(1)} %get-tuple-element.58), channel_id=1, source_target_pairs={{0,4},{4,0},{1,5},{5,1},{2,6},{6,2},{3,7},{7,3},{8,12},{12,8},{9,1... | collective-permute-start | bytes 700424 | tf_op jit(solution)/shard_map/ppermute | solution.py:587
  182.4 1.0 copy-start.5
  183.4 1.0 copy-start.7
  (5 other events, 4.1 us)

commit v8 on v7

--- a/solution.py
+++ b/solution.py
@@ -599,7 +599,7 @@
         out_shape=[shape((SHARE, IMG), BF16)] * 3 + [shape((TXT, SHARE), BF16)] * 2,
         in_specs=[VMEM] * 7,
         out_specs=[VMEM] * 5,
-        compiler_params=params(16),
+        compiler_params=pltpu.CompilerParams(vmem_limit_bytes=63_400_000),
         name="final",
     )(img.T, dy_img.T, txt, dy_txt, mine0, got0, passed)
     return y_img.T, y_txt, d_img.T, d_txt, d_ctl.T, grad_qkv.transpose(1, 0, 2), grad_out.T

time: 189 us -> 187 us (0.989)
  local copies, waits for them, and re-layouts: 8.49 us -> 4.53 us
  waiting for transfers between devices: 58 us -> 60.9 us
    unnamed x44 -> x32, local copies, waits for them, and re-layouts: 8.49 us -> 4.53 us
    ppermute x1, waiting for transfers between devices: 0.01 us -> 3 us  [per_device(): theirs = lax.ppermute(theirs, 'w', [(0, 1), (1, 0)])]
  transfers between devices with their start and end apart: 15 -> 15, of which waited for: 6 -> 7; matrix products, arithmetic and copies ran while one was open for 1% -> 1% of each run, Pallas kernels for 22% -> 23%
where the time goes in v8:
time: 187 us
  Pallas kernels  63.5 us (34%)
  waiting for transfers between devices  60.9 us (33%)
  blocking collectives  29.7 us (16%)
  starting transfers between devices  25.7 us (14%)
  local copies, waits for them, and re-layouts  4.53 us (2%)
    all_to_all x1, blocking collectives, per_device(): back = lax.all_to_all(back, seq, 0, 0, tiled=True)  29.7 us
    pallas_call x1, Pallas kernels, per_device(): pl.pallas_call(attention_kernel, out_shape=[shape((keys, 128), BF16), sha...  24.8 us
    all_to_all x1, waiting for transfers between devices, per_device(): recv = lax.all_to_all(send, seq, 0, 0, tiled=True)  23.1 us
    all_to_all x1, waiting for transfers between devices, per_device(): terms = lax.all_to_all(terms, 'y', 0, 0, tiled=True)  18 us
    pallas_call x1, Pallas kernels, per_device(): pl.pallas_call(post_kernel, out_shape=[rows] * 4 + [shape((8, 128), F32)]...  14.4 us
    pallas_call x1, Pallas kernels, per_device(): pl.pallas_call(pre_kernel, out_shape=[shape((BLOCKS, CHUNK, 128), BF16),...  13.5 us
    ppermute x1, waiting for transfers between devices, per_device(): from_chip = lax.ppermute(own, 'tp', other_chip)  11.8 us
    all_to_all x1, starting transfers between devices, per_device(): recv = lax.all_to_all(send, seq, 0, 0, tiled=True)  9.63 us
  transfers between devices with their start and end apart: 15, of which 7 were waited for; matrix products, arithmetic and copies ran while one was open for 1% of the time, Pallas kernels for 23%

profile of v8, /device:TPU:0, one launch (start us, length us, event | category | flops | bytes accessed | tf_op | source)
XLA Modules:
  0.0 186.8 jit_solution(14313667577426578207)
XLA Ops:
  0.6 1.9 %pack.1.in0 = bf16[1984,128]{1,0:T(8,128)(2,1)} custom-call(bf16[608,128]{1,0:T(8,128)(2,1)} %bitcast.18, bf16[608,128]{1,0:T(8,128)(2,1)} %bitcast.22, bf16[608,128]{1,0:T(8,128)(2,1)} %bitcast.20, bf16[16,608]{1,0:T(8,128)(2,1)} %txt.3, bf16[16,608]{1,0:T(8,128)(2,1)} %dy_txt.3), custom_call_target="tpu_custom_call" | custom-call | tf_op jit(solution)/shard_map/pack/pallas_call | solution.py:472
  2.6 3.2 %collective-permute-start.1 = (bf16[1984,128]{1,0:T(8,128)(2,1)}, bf16[1984,128]{1,0:T(8,128)(2,1)S(1)}, u32[]{:S(2)}, u32[]{:S(2)}) collective-permute-start(bf16[1984,128]{1,0:T(8,128)(2,1)} %pack.1.in0), channel_id=1, source_target_pairs={{0,2},{1,3},{2,0},{3,1},{4,6},{5,7},{6,4},{7,5},{8,10},{9,11},{10,... | collective-permute-start | bytes 1523720 | tf_op jit(solution)/shard_map/ppermute | solution.py:481
  5.8 11.8 %collective-permute-done.1.in2 = bf16[1984,128]{1,0:T(8,128)(2,1)S(1)} collective-permute-done((bf16[1984,128]{1,0:T(8,128)(2,1)}, bf16[1984,128]{1,0:T(8,128)(2,1)S(1)}, u32[]{:S(2)}, u32[]{:S(2)}) %collective-permute-start.1) | collective-permute-done | bytes 507936 | tf_op jit(solution)/shard_map/ppermute | solution.py:481
  17.6 1.9 %collective-permute-done.2.in3 = bf16[1984,128]{1,0:T(8,128)(2,1)S(1)} collective-permute-done((bf16[1984,128]{1,0:T(8,128)(2,1)S(1)}, bf16[1984,128]{1,0:T(8,128)(2,1)S(1)}, u32[]{:S(2)}, u32[]{:S(2)}) %collective-permute-start.2) | collective-permute-done | bytes 507936 | tf_op jit(solution)/shard_map/ppermute | solution.py:483
  19.4 0.8 copy-done.15
  20.2 13.5 %pre.1 = (bf16[32,192,128]{2,1,0:T(8,128)(2,1)}, f32[272,768]{1,0:T(8,128)}, bf16[272,2432]{1,0:T(8,128)(2,1)}, f32[272,128]{1,0:T(8,128)}, bf16[2,608,128]{2,1,...) custom-call(bf16[1984,128]{1,0:T(8,128)(2,1)} %pack.1.in0, ...), custom_call_target="tpu_custom_call" | custom-call | tf_op jit(solution)/shard_map/pre/pallas_call | solution.py:485
  33.7 9.6 %all-to-all-start = ((bf16[32,192,128]{2,1,0:T(8,128)(2,1)}), bf16[32,192,128]{2,1,0:T(8,128)(2,1)S(1)}, u32[]{:S(2)}, u32[]{:S(2)}) async-start(bf16[32,192,128]{2,1,0:T(8,128)(2,1)} %get-tuple-element.34), calls=%async_computation | async-start | bytes 3145728 | tf_op jit(solution)/shard_map/all_to_all | solution.py:506
  44.1 23.1 %all-to-all-done.recv.after = bf16[32,192,128]{2,1,0:T(8,128)(2,1)S(1)} async-done(((bf16[32,192,128]{2,1,0:T(8,128)(2,1)}), bf16[32,192,128]{2,1,0:T(8,128)(2,1)S(1)}, u32[]{:S(2)}, u32[]{:S(2)}) %all-to-all-start) | async-done | bytes 1572896 | tf_op jit(solution)/shard_map/all_to_all | solution.py:506
  67.4 2.3 %collective-permute-start.4 = (bf16[2,608,128]{2,1,0:T(8,128)(2,1)S(1)}, bf16[2,608,128]{2,1,0:T(8,128)(2,1)S(1)}, u32[]{:S(2)}, u32[]{:S(2)}) collective-permute-start(bf16[2,608,128]{2,1,0:T(8,128)(2,1)S(1)} %get-tuple-element.41), channel_id=1, source_target_pairs={{0,64},{32,96},{64,0},{96,32},{1,65},{33,97},{65,1},{97,33},{2,66}... | collective-permute-start | bytes 933896 | tf_op jit(solution)/shard_map/ppermute | solution.py:451
  69.6 1.2 collective-permute-start.5
  70.8 24.8 %attention.1 = (bf16[4608,128]{1,0:T(8,128)(2,1)S(1)}, bf16[2048,128]{1,0:T(8,128)(2,1)S(1)}) custom-call(s32[2]{0:T(128)S(1)} %pad_add_fusion.role, bf16[32,192,128]{2,1,0:T(8,128)(2,1)S(1)} %all-to-all-done.recv.after), custom_call_target="tpu_custom_call" | custom-call | flops 40000000000 | bytes 3200000 | tf_op jit(solution)/shard_map/attention/pallas_call | solution.py:509
  95.6 0.7 scatter.1
  96.3 29.7 %all_to_all.15.recv = bf16[32,192,128]{2,1,0:T(8,128)(2,1)S(1)} all-to-all(bf16[32,192,128]{2,1,0:T(8,128)(2,1)S(1)} %scatter.1), channel_id=1, replica_groups=mesh['z'=4,'y'=4,'w'=2,'tp'=4] {'z','y','w'}, dimensions={0} | all-to-all | bytes 3145728 | tf_op jit(solution)/shard_map/all_to_all | solution.py:534
  125.9 2.5 %head_back_ctl.1.ctl_rows.b0 = bf16[128,1536]{1,0:T(8,128)(2,1)S(1)} custom-call(bf16[32,192,128]{2,1,0:T(8,128)(2,1)S(1)} %all_to_all.15.recv, f32[272,768]{1,0:T(8,128)S(1)} %copy-done.2, f32[3,2,64]{2,1,0:T(2,128)S(1)} %copy-done.8), custom_call_target="tpu_custom_call" | custom-call | tf_op jit(solution)/shard_map/head_back_ctl/pallas_call | solution.py:536
  128.5 0.9 collective-permute-start.11
  129.4 0.6 collective-permute-start.10
  129.9 0.8 collective-permute-start.9
  130.8 14.4 %post.1 = (bf16[1984,128]{1,0:T(8,128)(2,1)}, bf16[1984,128]{1,0:T(8,128)(2,1)}, bf16[1984,128]{1,0:T(8,128)(2,1)}, bf16[1984,128]{1,0:T(8,128)(2,1)}, f32[8,128]{1,0:T(8,128)}) custom-call(bf16[32,192,128]{2,1,0:T(8,128)(2,1)} %copy-done, f32[272,768]{1,0:T(8,128)} %get-tuple-element.43.proj, f32[3,2,64]{2,1,0:T(2,128)} %gains.5, ...), custom_call_target="tpu_custom_call" | custom-call | flops 14000000000 | bytes 30000000 | tf_op jit(solution)/shard_map/post/pallas_call | solution.py:545
  145.2 1.5 collective-permute-done.9.b1
  146.7 1.0 copy-done.4
  147.7 0.7 copy-done.10
  148.4 1.9 %weight.1 = bf16[4,152,1536]{2,1,0:T(8,128)(2,1)S(1)} custom-call(bf16[2,608,128]{2,1,0:T(8,128)(2,1)S(1)} %copy-done.9, bf16[2,608,128]{2,1,0:T(8,128)(2,1)S(1)} %collective-permute-done.3.after0.nz1, bf16[2,608,128]{2,1,0:T(8,128)(2,1)S(1)} %collective-permute-done.4.after1.nz2, bf16[2,608,128]{2,1,0:T(8,128)(2,1)S(1)} %collective-permute-done.5.after2.nz3, ...), custom_call_target="tpu_custom_call" | custom-call | flops 3000000000 | bytes 5000000 | tf_op jit(solution)/shard_map/weight/pallas_call | solution.py:565
  150.3 1.3 copy-done.1
  151.6 3.7 %all-to-all-start.2 = ((bf16[4,152,1536]{2,1,0:T(8,128)(2,1)}), bf16[4,152,1536]{2,1,0:T(8,128)(2,1)S(1)}, u32[]{:S(2)}, u32[]{:S(2)}) async-start(bf16[4,152,1536]{2,1,0:T(8,128)(2,1)} %copy-done.1), calls=%async_computation.2 | async-start | bytes 3735552 | tf_op jit(solution)/shard_map/all_to_all | solution.py:578
  155.9 1.6 collective-permute-done.7
  157.5 0.9 add_convert_fusion
  158.4 2.7 %collective-permute-start.8 = (bf16[1984,128]{1,0:T(8,128)(2,1)}, bf16[1984,128]{1,0:T(8,128)(2,1)}, u32[]{:S(2)}, u32[]{:S(2)}) collective-permute-start(bf16[1984,128]{1,0:T(8,128)(2,1)} %add_convert_fusion), channel_id=1, source_target_pairs={{0,2},{1,3},{2,0},{3,1},{4,6},{5,7},{6,4},{7,5},{8,10},{9,11},{10,... | collective-permute-start | bytes 1523720 | tf_op jit(solution)/shard_map/ppermute | solution.py:577
  161.2 18.0 %all-to-all-done.2.terms = bf16[4,152,1536]{2,1,0:T(8,128)(2,1)S(1)} async-done(((bf16[4,152,1536]{2,1,0:T(8,128)(2,1)}), bf16[4,152,1536]{2,1,0:T(8,128)(2,1)S(1)}, u32[]{:S(2)}, u32[]{:S(2)}) %all-to-all-start.2) | async-done | bytes 1867808 | tf_op jit(solution)/shard_map/all_to_all | solution.py:578
  179.6 0.8 copy-done.11
  180.4 2.6 %final.1 = (bf16[608,128]{1,0:T(8,128)(2,1)}, bf16[608,128]{1,0:T(8,128)(2,1)}, bf16[608,128]{1,0:T(8,128)(2,1)}, bf16[16,608]{1,0:T(8,128)(2,1)}, bf16[16,608]{1,0:T(8,128)(2,1)}) custom-call(bf16[608,128]{1,0:T(8,128)(2,1)} %bitcast.19, bf16[608,128]{1,0:T(8,128)(2,1)} %bitcast.21, bf16[16,608]{1,0:T(8,128)(2,1)} %txt.3, bf16[16,608]{1,0:T(8,128)(2,1)} %dy_txt.3, ...), custom_call_target="tpu_custom_call" | custom-call | tf_op jit(solution)/shard_map/final/pallas_call | solution.py:597
  183.0 3.0 %collective-permute-done.12.other = bf16[76,1536]{1,0:T(8,128)(2,1)S(1)} collective-permute-done((bf16[76,1536]{1,0:T(8,128)(2,1)S(1)}, bf16[76,1536]{1,0:T(8,128)(2,1)S(1)}, u32[]{:S(2)}, u32[]{:S(2)}) %collective-permute-start.12) | collective-permute-done | bytes 233504 | tf_op jit(solution)/shard_map/ppermute | solution.py:587
  186.0 0.8 weight_out.1
  (44 shorter events, 1.3 us)
Async XLA Ops:
  2.6 15.0 %collective-permute-start.1 = (bf16[1984,128]{1,0:T(8,128)(2,1)}, bf16[1984,128]{1,0:T(8,128)(2,1)S(1)}, u32[]{:S(2)}, u32[]{:S(2)}) collective-permute-start(bf16[1984,128]{1,0:T(8,128)(2,1)} %pack.1.in0), channel_id=1, source_target_pairs={{0,2},{1,3},{2,0},{3,1},{4,6},{5,7},{6,4},{7,5},{8,10},{9,11},{10,... | collective-permute-start | bytes 1523720 | tf_op jit(solution)/shard_map/ppermute | solution.py:481
  5.8 11.8 %collective-permute-start = (bf16[1984,128]{1,0:T(8,128)(2,1)}, bf16[1984,128]{1,0:T(8,128)(2,1)S(1)}, u32[]{:S(2)}, u32[]{:S(2)}) collective-permute-start(bf16[1984,128]{1,0:T(8,128)(2,1)} %pack.1.in0), channel_id=1, source_target_pairs={{0,1},{1,0},{2,3},{3,2},{4,5},{5,4},{6,7},{7,6},{8,9},{9,8},{10,11... | collective-permute-start | bytes 1523720 | tf_op jit(solution)/shard_map/ppermute | solution.py:482
  17.5 1.9 %copy-start.13 = (bf16[1984,128]{1,0:T(8,128)(2,1)}, bf16[1984,128]{1,0:T(8,128)(2,1)S(1)}, u32[]{:S(2)}) copy-start(bf16[1984,128]{1,0:T(8,128)(2,1)S(1)} %collective-permute-done.1.in2) | copy-start | bytes 1523716
  17.6 1.9 %collective-permute-start.2 = (bf16[1984,128]{1,0:T(8,128)(2,1)S(1)}, bf16[1984,128]{1,0:T(8,128)(2,1)S(1)}, u32[]{:S(2)}, u32[]{:S(2)}) collective-permute-start(bf16[1984,128]{1,0:T(8,128)(2,1)S(1)} %collective-permute-done.1.in2), channel_id=1, source_target_pairs={{0,1},{1,0},{2,3},{3,2},{4,5},{5,4},{6,7},{7,6},{8,9},{9,8},{10,11... | collective-permute-start | bytes 1523720 | tf_op jit(solution)/shard_map/ppermute | solution.py:483
  17.6 1.9 %copy-start.14 = (bf16[1984,128]{1,0:T(8,128)(2,1)}, bf16[1984,128]{1,0:T(8,128)(2,1)S(1)}, u32[]{:S(2)}) copy-start(bf16[1984,128]{1,0:T(8,128)(2,1)S(1)} %collective-permute-done.in1) | copy-start | bytes 1523716
  19.4 0.8 copy-start.15
  33.7 33.5 %copy-start.5 = (bf16[2,608,128]{2,1,0:T(8,128)(2,1)S(1)}, bf16[2,608,128]{2,1,0:T(8,128)(2,1)}, u32[]{:S(2)}) copy-start(bf16[2,608,128]{2,1,0:T(8,128)(2,1)} %get-tuple-element.37.refs_0_) | copy-start | bytes 933892
  33.7 33.5 %copy-start.6 = (bf16[2,608,128]{2,1,0:T(8,128)(2,1)S(1)}, bf16[2,608,128]{2,1,0:T(8,128)(2,1)}, u32[]{:S(2)}) copy-start(bf16[2,608,128]{2,1,0:T(8,128)(2,1)} %get-tuple-element.38.refs_1_) | copy-start | bytes 933892
  33.7 33.5 %copy-start.7 = (bf16[2,608,128]{2,1,0:T(8,128)(2,1)S(1)}, bf16[2,608,128]{2,1,0:T(8,128)(2,1)}, u32[]{:S(2)}) copy-start(bf16[2,608,128]{2,1,0:T(8,128)(2,1)} %get-tuple-element.39.refs_2_) | copy-start | bytes 933892
  33.7 33.5 %all-to-all-start = ((bf16[32,192,128]{2,1,0:T(8,128)(2,1)}), bf16[32,192,128]{2,1,0:T(8,128)(2,1)S(1)}, u32[]{:S(2)}, u32[]{:S(2)}) async-start(bf16[32,192,128]{2,1,0:T(8,128)(2,1)} %get-tuple-element.34), calls=%async_computation | async-start | bytes 3145728 | tf_op jit(solution)/shard_map/all_to_all | solution.py:506
  67.3 28.3 %collective-permute-start.3 = (bf16[2,608,128]{2,1,0:T(8,128)(2,1)S(1)}, bf16[2,608,128]{2,1,0:T(8,128)(2,1)S(1)}, u32[]{:S(2)}, u32[]{:S(2)}) collective-permute-start(bf16[2,608,128]{2,1,0:T(8,128)(2,1)S(1)} %get-tuple-element.40), channel_id=1, source_target_pairs={{0,32},{32,64},{64,96},{96,0},{1,33},{33,65},{65,97},{97,1},{2,34}... | collective-permute-start | bytes 933896 | tf_op jit(solution)/shard_map/ppermute | solution.py:451
  67.4 28.2 %collective-permute-start.4 = (bf16[2,608,128]{2,1,0:T(8,128)(2,1)S(1)}, bf16[2,608,128]{2,1,0:T(8,128)(2,1)S(1)}, u32[]{:S(2)}, u32[]{:S(2)}) collective-permute-start(bf16[2,608,128]{2,1,0:T(8,128)(2,1)S(1)} %get-tuple-element.41), channel_id=1, source_target_pairs={{0,64},{32,96},{64,0},{96,32},{1,65},{33,97},{65,1},{97,33},{2,66}... | collective-permute-start | bytes 933896 | tf_op jit(solution)/shard_map/ppermute | solution.py:451
  69.6 26.0 %collective-permute-start.5 = (bf16[2,608,128]{2,1,0:T(8,128)(2,1)S(1)}, bf16[2,608,128]{2,1,0:T(8,128)(2,1)S(1)}, u32[]{:S(2)}, u32[]{:S(2)}) collective-permute-start(bf16[2,608,128]{2,1,0:T(8,128)(2,1)S(1)} %get-tuple-element.42), channel_id=1, source_target_pairs={{0,96},{32,0},{64,32},{96,64},{1,97},{33,1},{65,33},{97,65},{2,98}... | collective-permute-start | bytes 933896 | tf_op jit(solution)/shard_map/ppermute | solution.py:451
  96.2 29.7 %copy-start.2 = (f32[272,768]{1,0:T(8,128)S(1)}, f32[272,768]{1,0:T(8,128)}, u32[]{:S(2)}) copy-start(f32[272,768]{1,0:T(8,128)} %get-tuple-element.43.proj) | copy-start | bytes 2506756
  96.2 29.7 %copy-start.8 = (f32[3,2,64]{2,1,0:T(2,128)S(1)}, f32[3,2,64]{2,1,0:T(2,128)}, u32[]{:S(2)}) copy-start(f32[3,2,64]{2,1,0:T(2,128)} %gains.5) | copy-start | bytes 4612
  125.9 4.8 %copy-start = (bf16[32,192,128]{2,1,0:T(8,128)(2,1)}, bf16[32,192,128]{2,1,0:T(8,128)(2,1)S(1)}, u32[]{:S(2)}) copy-start(bf16[32,192,128]{2,1,0:T(8,128)(2,1)S(1)} %all_to_all.15.recv) | copy-start | bytes 4718596
  128.5 2.3 %copy-start.3 = (bf16[128,1536]{1,0:T(8,128)(2,1)}, bf16[128,1536]{1,0:T(8,128)(2,1)S(1)}, u32[]{:S(2)}) copy-start(bf16[128,1536]{1,0:T(8,128)(2,1)S(1)} %head_back_ctl.1.ctl_rows.b0) | copy-start | bytes 1179652
  128.5 16.7 %collective-permute-start.11 = (bf16[128,1536]{1,0:T(8,128)(2,1)S(1)}, bf16[128,1536]{1,0:T(8,128)(2,1)S(1)}, u32[]{:S(2)}, u32[]{:S(2)}) collective-permute-start(bf16[128,1536]{1,0:T(8,128)(2,1)S(1)} %head_back_ctl.1.ctl_rows.b0), channel_id=1, source_target_pairs={{0,96},{32,0},{64,32},{96,64},{1,97},{33,1},{65,33},{97,65},{2,98}... | collective-permute-start | bytes 1179656 | tf_op jit(solution)/shard_map/ppermute | solution.py:451
  129.4 15.9 %collective-permute-start.10 = (bf16[128,1536]{1,0:T(8,128)(2,1)S(1)}, bf16[128,1536]{1,0:T(8,128)(2,1)S(1)}, u32[]{:S(2)}, u32[]{:S(2)}) collective-permute-start(bf16[128,1536]{1,0:T(8,128)(2,1)S(1)} %head_back_ctl.1.ctl_rows.b0), channel_id=1, source_target_pairs={{0,64},{32,96},{64,0},{96,32},{1,65},{33,97},{65,1},{97,33},{2,66}... | collective-permute-start | bytes 1179656 | tf_op jit(solution)/shard_map/ppermute | solution.py:451
  129.9 16.8 %collective-permute-start.9 = (bf16[128,1536]{1,0:T(8,128)(2,1)S(1)}, bf16[128,1536]{1,0:T(8,128)(2,1)S(1)}, u32[]{:S(2)}, u32[]{:S(2)}) collective-permute-start(bf16[128,1536]{1,0:T(8,128)(2,1)S(1)} %head_back_ctl.1.ctl_rows.b0), channel_id=1, source_target_pairs={{0,32},{32,64},{64,96},{96,0},{1,33},{33,65},{65,97},{97,1},{2,34}... | collective-permute-start | bytes 1179656 | tf_op jit(solution)/shard_map/ppermute | solution.py:451
  130.8 16.0 %copy-start.9 = (bf16[2,608,128]{2,1,0:T(8,128)(2,1)S(1)}, bf16[2,608,128]{2,1,0:T(8,128)(2,1)}, u32[]{:S(2)}) copy-start(bf16[2,608,128]{2,1,0:T(8,128)(2,1)} %get-tuple-element.55.nz0) | copy-start | bytes 933892
  146.7 1.0 copy-start.4
  147.7 0.7 copy-start.10
  150.3 1.3 copy-start.1
  151.6 5.9 %copy-start.12 = (bf16[1984,128]{1,0:T(8,128)(2,1)S(1)}, bf16[1984,128]{1,0:T(8,128)(2,1)}, u32[]{:S(2)}) copy-start(bf16[1984,128]{1,0:T(8,128)(2,1)} %get-tuple-element.48) | copy-start | bytes 1523716
  151.6 27.5 %all-to-all-start.2 = ((bf16[4,152,1536]{2,1,0:T(8,128)(2,1)}), bf16[4,152,1536]{2,1,0:T(8,128)(2,1)S(1)}, u32[]{:S(2)}, u32[]{:S(2)}) async-start(bf16[4,152,1536]{2,1,0:T(8,128)(2,1)} %copy-done.1), calls=%async_computation.2 | async-start | bytes 3735552 | tf_op jit(solution)/shard_map/all_to_all | solution.py:578
  155.3 2.2 %collective-permute-start.7 = (bf16[1984,128]{1,0:T(8,128)(2,1)}, bf16[1984,128]{1,0:T(8,128)(2,1)S(1)}, u32[]{:S(2)}, u32[]{:S(2)}) collective-permute-start(bf16[1984,128]{1,0:T(8,128)(2,1)} %get-tuple-element.49), channel_id=1, source_target_pairs={{0,1},{1,0},{2,3},{3,2},{4,5},{5,4},{6,7},{7,6},{8,9},{9,8},{10,11... | collective-permute-start | bytes 1523720 | tf_op jit(solution)/shard_map/ppermute | solution.py:574
  155.4 24.2 %collective-permute-start.6 = (bf16[1984,128]{1,0:T(8,128)(2,1)}, bf16[1984,128]{1,0:T(8,128)(2,1)S(1)}, u32[]{:S(2)}, u32[]{:S(2)}) collective-permute-start(bf16[1984,128]{1,0:T(8,128)(2,1)} %get-tuple-element.47), channel_id=1, source_target_pairs={{0,1},{1,0},{2,3},{3,2},{4,5},{5,4},{6,7},{7,6},{8,9},{9,8},{10,11... | collective-permute-start | bytes 1523720 | tf_op jit(solution)/shard_map/ppermute | solution.py:575
  158.4 21.2 %collective-permute-start.8 = (bf16[1984,128]{1,0:T(8,128)(2,1)}, bf16[1984,128]{1,0:T(8,128)(2,1)}, u32[]{:S(2)}, u32[]{:S(2)}) collective-permute-start(bf16[1984,128]{1,0:T(8,128)(2,1)} %add_convert_fusion), channel_id=1, source_target_pairs={{0,2},{1,3},{2,0},{3,1},{4,6},{5,7},{6,4},{7,5},{8,10},{9,11},{10,... | collective-permute-start | bytes 1523720 | tf_op jit(solution)/shard_map/ppermute | solution.py:577
  179.5 6.5 %collective-permute-start.12 = (bf16[76,1536]{1,0:T(8,128)(2,1)S(1)}, bf16[76,1536]{1,0:T(8,128)(2,1)S(1)}, u32[]{:S(2)}, u32[]{:S(2)}) collective-permute-start(bf16[76,1536]{1,0:T(8,128)(2,1)S(1)} %get-tuple-element.58), channel_id=1, source_target_pairs={{0,4},{4,0},{1,5},{5,1},{2,6},{6,2},{3,7},{7,3},{8,12},{12,8},{9,1... | collective-permute-start | bytes 700424 | tf_op jit(solution)/shard_map/ppermute | solution.py:587
  179.6 0.8 copy-start.11
